TPU v7x, 512 devices: a whole 4x8x8 slice. The times are simulated.
512 devices in a mesh: dp: 8 (over y), pipe: 16 (over x, z_hi, core), tensor: 4 (over z_lo).
Axes of the slice: x: 4, y: 8, z: 8 (z_hi: 2, z_lo: 4; z = z_hi * 4 + z_lo), core: 2. Of those that a mesh axis runs over, the one named last changes fastest.
Arguments:
- final_normed: bfloat16 [16384, 7168], P(('dp', 'pipe'), 'tensor'), may hold values from -4 to 4
- embed_cot: bfloat16 [16384, 7168], P(('dp', 'pipe'), 'tensor'), may hold values from -1.796875 to 1.796875
- head: bfloat16 [512, 7168], P('tensor'), may hold values from -1 to 1
- rest_lse: float32 [16384], P(('dp', 'pipe')), may hold values from 6 to 12
- loss_grad: float32 [16384], P(('dp', 'pipe')), may hold values from 1 to 4
- target_ids: int32 [16384], P(('dp', 'pipe')), may hold values from 0 to 511
- embed_ids: int32 [16384], P(('dp', 'pipe')), may hold values from 0 to 63
Outputs:
- token_loss: float32 [16384], P(('dp', 'pipe'))
- grad_hidden: bfloat16 [16384, 7168], P(('dp', 'pipe'), 'tensor')
- head_grad: float32 [512, 7168], P('tensor', 'dp')
- embed_grad: float32 [64, 7168], P('dp', 'tensor')
All inputs are finite; a program needn't handle non-finite values.
Results may differ from a plain program's by a relative error of at most 0.0047.
Values may be sent and summed in bfloat16 or wider, within the bound.
No kernel may reach another device: no remote copies, remote signals or barrier semaphores. Data moves between devices by JAX's collectives and lax.ppermute only.
A program may use at most 64 MiB of HBM per device.

v0:
```python
import jax
import jax.numpy as jnp
from jax import lax
from jax.sharding import PartitionSpec as P

EMB_DEV = 8


def joined(value, axis, join):
    pieces = jax.tree.map(lambda part: lax.all_gather(part, axis), value)
    head = jax.tree.map(lambda part: part[0], pieces)
    tail = jax.tree.map(lambda part: part[1:], pieces)
    total, _ = lax.scan(lambda total, share: (join(total, share), None), head, tail)
    return total


def merge_softmax(first, second):
    largest = jnp.maximum(first[0], second[0])
    summed = first[1] * jnp.exp(first[0] - largest) + second[1] * jnp.exp(second[0] - largest)
    return (largest, summed, first[2] + second[2])


def shards(final_normed, embed_cot, head, rest_lse, loss_grad, target_ids, embed_ids):
    vocab_rows = head.shape[0]
    tensor_rank = lax.axis_index("tensor")
    normed = lax.all_gather(final_normed, "tensor", axis=1, tiled=True)
    logits = lax.dot_general(
        normed, head, (((1,), (1,)), ((), ())), preferred_element_type=jnp.float32
    )
    columns = lax.broadcasted_iota(jnp.int32, (1, vocab_rows), 1) + tensor_rank * vocab_rows
    target_hits = target_ids[:, None] == columns
    row_peak = jnp.max(logits, axis=1)
    row_total = jnp.sum(jnp.exp(logits - row_peak[:, None]), axis=1)
    row_picked = jnp.sum(jnp.where(target_hits, logits, 0.0), axis=1)
    window_peak, window_total, picked = joined(
        (row_peak, row_total, row_picked), "tensor", merge_softmax
    )
    top_all = jnp.maximum(window_peak, rest_lse)
    full_total = window_total * jnp.exp(window_peak - top_all) + jnp.exp(rest_lse - top_all)
    log_total = top_all + jnp.log(full_total)
    token_loss = log_total - picked
    dlogits = (
        loss_grad[:, None]
        * (jnp.exp(logits - log_total[:, None]) - target_hits.astype(jnp.float32))
    ).astype(jnp.bfloat16)
    head_term = lax.dot_general(
        dlogits, normed, (((0,), (0,)), ((), ())), preferred_element_type=jnp.float32
    )
    data_count = lax.axis_size("dp")
    embed_rows = EMB_DEV * data_count
    onehot = (embed_ids[:, None] == lax.broadcasted_iota(jnp.int32, (1, embed_rows), 1)).astype(
        jnp.bfloat16
    )
    embed_term = lax.dot_general(
        onehot, embed_cot, (((0,), (0,)), ((), ())), preferred_element_type=jnp.float32
    )
    all_dlogits = lax.all_gather(dlogits, "tensor", axis=1, tiled=True)
    quarters = lax.all_to_all(head, "tensor", split_axis=1, concat_axis=0, tiled=True)
    grad_hidden = jnp.dot(all_dlogits, quarters, preferred_element_type=jnp.float32).astype(
        jnp.bfloat16
    )
    head_summed, embed_summed = lax.psum((head_term, embed_term), "pipe")
    head_grad, embed_grad = (
        lax.psum_scatter(head_summed, "dp", scatter_dimension=1, tiled=True),
        lax.psum_scatter(embed_summed, "dp", scatter_dimension=0, tiled=True),
    )
    return (token_loss, grad_hidden, head_grad, embed_grad)


def solution(mesh):
    return jax.shard_map(
        shards,
        mesh=mesh,
        in_specs=(
            P(("dp", "pipe"), "tensor"),
            P(("dp", "pipe"), "tensor"),
            P("tensor", None),
            P(("dp", "pipe")),
            P(("dp", "pipe")),
            P(("dp", "pipe")),
            P(("dp", "pipe")),
        ),
        out_specs=(
            P(("dp", "pipe")),
            P(("dp", "pipe"), "tensor"),
            P("tensor", "dp"),
            P("dp", "tensor"),
        ),
        check_vma=False,
    )
```

profile of v0, /device:TPU:1, one launch (start us, length us, event | category | flops | bytes accessed | tf_op | source)
XLA Modules:
  0.0 382.8 jit_solution(12527996369910605201)
XLA Ops:
  7.2 0.0 copy-start
  7.2 0.0 all-gather.8.cloned.1.call-start
  7.2 0.7 all-gather.8.cloned.1.call-update
  7.9 0.0 reduce-scatter.3.cloned.1.call-start
  8.0 0.0 copy-start.3
  8.0 56.3 %all-gather.8.cloned.1.call-done = bf16[128,7168]{1,0:T(8,128)(2,1)} async-done(((bf16[128,1792]{1,0:T(8,128)(2,1)}), bf16[128,7168]{1,0:T(8,128)(2,1)}) %all-gather.8.cloned.1.call-update) | async-done | bytes 1835024 | tf_op jit(solution)/shard_map/all_gather | solution.py:26
  64.3 2.8 fusion.17
  67.1 0.1 fusion.7
  67.2 7.3 %all-gather.4 = f32[4,1,128]{2,1,0:T(1,128)S(1)} all-gather(f32[1,1,128]{2,1,0:T(1,128)S(1)} %bitcast.55), channel_id=3, replica_groups=mesh['dp'=8,'pipe'=16,'tensor'=4] {'tensor'}, dimensions={0}, use_global_device_ids=true | all-gather | bytes 2560 | tf_op jit(solution)/shard_map/all_gather | solution.py:10
  74.5 5.8 %all-gather.5 = f32[4,1,128]{2,1,0:T(1,128)S(1)} all-gather(f32[1,1,128]{2,1,0:T(1,128)S(1)} %bitcast.54), channel_id=4, replica_groups=mesh['dp'=8,'pipe'=16,'tensor'=4] {'tensor'}, dimensions={0}, use_global_device_ids=true | all-gather | bytes 2560 | tf_op jit(solution)/shard_map/all_gather | solution.py:10
  80.3 7.2 %all-gather.3 = f32[4,1,128]{2,1,0:T(1,128)S(1)} all-gather(f32[1,1,128]{2,1,0:T(1,128)S(1)} %bitcast.53), channel_id=2, replica_groups=mesh['dp'=8,'pipe'=16,'tensor'=4] {'tensor'}, dimensions={0}, use_global_device_ids=true | all-gather | bytes 2560 | tf_op jit(solution)/shard_map/all_gather | solution.py:10
  87.5 0.1 while.14
  87.7 0.5 fusion.16
  88.2 0.1 fusion.10
  88.3 2.4 fusion.18
  90.7 0.0 reduce-scatter.3.cloned.1.call-update
  90.8 1.5 copy-done.1
  92.2 2.3 copy.13
  94.5 3.7 all-to-all-start
  98.2 0.0 reduce-scatter.5.cloned.1.call-start
  98.3 1.1 fusion.11
  99.4 0.0 reduce-scatter.5.cloned.1.call-update
  99.4 0.0 all-reduce.2.cloned.1.call-start
  99.5 50.9 %reduce-scatter.3.cloned.1.call-done = f32[128,896]{1,0:T(8,128)} async-done(((f32[128,7168]{1,0:T(8,128)}), f32[128,896]{1,0:T(8,128)}) %reduce-scatter.3.cloned.1.call-update) | async-done | bytes 458768 | tf_op jit(solution)/shard_map/reduce_scatter | solution.py:64
  150.4 0.0 all-reduce.2.cloned.1.call-update
  150.4 37.4 %reduce-scatter.5.cloned.1.call-done = f32[8,1792]{1,0:T(8,128)} async-done(((f32[64,1792]{1,0:T(8,128)}), f32[8,1792]{1,0:T(8,128)}) %reduce-scatter.5.cloned.1.call-update) | async-done | bytes 57360 | tf_op jit(solution)/shard_map/reduce_scatter | solution.py:65
  187.8 85.3 %psum.17 = f32[8,1792]{1,0:T(8,128)} all-reduce(f32[8,1792]{1,0:T(8,128)} %reduce-scatter.5.cloned.1.call-done), channel_id=1, replica_groups=mesh['dp'=8,'pipe'=16,'tensor'=4] {'pipe'}, use_global_device_ids=true, to_apply=%region_7.8 | all-reduce | flops 14336 | bytes 114688 | tf_op jit(solution)/shard_map/psum | solution.py:62
  273.1 2.5 copy.14
  275.7 11.4 %all_gather.31 = bf16[128,512]{0,1:T(8,128)(2,1)S(1)} all-gather(bf16[128,128]{0,1:T(8,128)(2,1)S(1)} %fusion.10), channel_id=1, replica_groups=mesh['dp'=8,'pipe'=16,'tensor'=4] {'tensor'}, dimensions={1}, use_global_device_ids=true | all-gather | bytes 163840 | tf_op jit(solution)/shard_map/all_gather | solution.py:57
  287.0 2.7 convolution_convert_fusion
  289.7 84.7 %all-reduce.2.cloned.1.call-done = f32[128,896]{1,0:T(8,128)} async-done(((f32[128,896]{1,0:T(8,128)}), f32[128,896]{1,0:T(8,128)}) %all-reduce.2.cloned.1.call-update) | async-done | bytes 458768 | tf_op jit(solution)/shard_map/psum | solution.py:62
  374.4 1.8 copy.39
  (25 shorter events, 0.1 us)
Async XLA Ops:
  7.2 91.1 %copy-start = (bf16[128,1792]{1,0:T(8,128)(2,1)S(1)}, bf16[128,1792]{1,0:T(8,128)(2,1)}, u32[]{:S(2)}) copy-start(bf16[128,1792]{1,0:T(8,128)(2,1)} %param.10) | copy-start | bytes 1376260
  7.2 57.1 %all-gather.8.cloned.1.call-start = ((), (), s32[]{:S(2)}) async-start(), calls=%async_computation.3 | async-start | bytes 2293760 | tf_op jit(solution)/shard_map/all_gather | solution.py:26
  7.9 142.5 %reduce-scatter.3.cloned.1.call-start = ((), (), s32[]{:S(2)}) async-start(), calls=%async_computation.4 | async-start | bytes 4128768 | tf_op jit(solution)/shard_map/reduce_scatter | solution.py:64
  8.0 59.1 %copy-start.3 = (s32[128]{0:T(128)S(1)}, s32[128]{0:T(128)}, u32[]{:S(2)}) copy-start(s32[128]{0:T(128)} %param.14) | copy-start | bytes 1540
  8.0 79.7 %copy-start.6 = (f32[128]{0:T(128)S(1)}, f32[128]{0:T(128)}, u32[]{:S(2)}) copy-start(f32[128]{0:T(128)} %param.12) | copy-start | bytes 1540
  8.0 80.2 %copy-start.4 = (f32[128]{0:T(128)S(1)}, f32[128]{0:T(128)}, u32[]{:S(2)}) copy-start(f32[128]{0:T(128)} %param.13) | copy-start | bytes 1540
  64.3 24.0 %copy-start.2 = (bf16[128,7168]{1,0:T(8,128)(2,1)S(1)}, bf16[128,7168]{1,0:T(8,128)(2,1)}, u32[]{:S(2)}) copy-start(bf16[128,7168]{1,0:T(8,128)(2,1)} %all-gather.8.cloned.1.call-done) | copy-start | bytes 5505028
  90.7 1.5 copy-start.1
  94.5 3.8 copy-start.5
  94.5 178.6 %all-to-all-start = ((bf16[128,4,1792]{0,2,1:T(8,128)(2,1)}), bf16[128,4,1792]{0,2,1:T(8,128)(2,1)S(1)}, u32[]{:S(2)}, u32[]{:S(2)}) async-start(bf16[128,4,1792]{0,2,1:T(8,128)(2,1)} %bitcast.48), calls=%async_computation | async-start | bytes 3670016 | tf_op jit(solution)/shard_map/all_to_all | solution.py:58
  98.2 89.6 %reduce-scatter.5.cloned.1.call-start = ((), (), s32[]{:S(2)}) async-start(), calls=%async_computation.6 | async-start | bytes 516096 | tf_op jit(solution)/shard_map/reduce_scatter | solution.py:65
  99.4 275.0 %all-reduce.2.cloned.1.call-start = ((), (), s32[]{:S(2)}) async-start(), calls=%async_computation.5 | async-start | bytes 917504 | tf_op jit(solution)/shard_map/psum | solution.py:62
Sparse Core Ops, SparseCore 0:
  10.1 54.1 all-gather.7
  90.9 59.4 reduce-scatter.2
  153.8 33.9 reduce-scatter.4
  190.9 183.5 all-reduce.1
where the time goes:
time: 383 us
  waiting for transfers between devices  230 us (60%)
  blocking collectives  117 us (31%)
  between operations  13.9 us (4%)
  matrix products  9.06 us (2%)
  local copies, waits for them, and re-layouts  8.14 us (2%)
  starting transfers between devices  3.88 us (1%)
    psum x1, blocking collectives, shards(): head_summed, embed_summed = lax.psum((head_term, embed_term), 'pipe')  85.3 us
    psum x1, waiting for transfers between devices, shards(): head_summed, embed_summed = lax.psum((head_term, embed_term), 'pipe')  84.7 us
    all_gather x1, waiting for transfers between devices, shards(): normed = lax.all_gather(final_normed, 'tensor', axis=1, tiled=True)  56.3 us
    reduce_scatter x1, waiting for transfers between devices, shards(): lax.psum_scatter(head_summed, 'dp', scatter_dimension=1, tiled=True)  50.9 us
    reduce_scatter x1, waiting for transfers between devices, shards(): lax.psum_scatter(embed_summed, 'dp', scatter_dimension=0, tiled=True)  37.4 us
    all_gather x3, blocking collectives, joined(): pieces = jax.tree.map(lambda part: lax.all_gather(part, axis), value)  20.3 us
    all_gather x1, blocking collectives, shards(): all_dlogits = lax.all_gather(dlogits, 'tensor', axis=1, tiled=True)  11.4 us
  transfers between devices with their start and end apart: 5, of which 4 were waited for; matrix products, arithmetic and copies ran while one was open for 2% of the time, Pallas kernels for 0%

commit v1 on v0

v1 whole, which is shorter than its diff:
```python
import jax
import jax.numpy as jnp
from jax import lax
from jax.sharding import Mesh
from jax.sharding import PartitionSpec as P

F32, BF16 = jnp.float32, jnp.bfloat16
RING = ("zhi", "tensor")
OWNERS = ("core", "tensor")
REPLICAS = ("x", "zhi", "core")


def dot(a, b, dims):
    return lax.dot_general(a, b, (dims, ((), ())), preferred_element_type=F32)


def shift(value, by):
    count = lax.axis_size(RING)
    return lax.ppermute(value, RING, [(i, (i + by) % count) for i in range(count)])


def swap_cores(value):
    return lax.ppermute(value, "core", [(0, 1), (1, 0)])


def exchange(value, axes):
    return lax.all_to_all(value, axes, 0, 0)


def spread(value, axes):
    count = lax.axis_size(axes)
    return exchange(jnp.broadcast_to(value[None], (count,) + value.shape), axes)


def window_quarter(head, core, rank, half):
    rows = head.shape[0]

    def block(ahead):
        at = (rank + ahead) % 4 * (2 * half) + core * half
        return lax.dynamic_slice_in_dim(head, at, half, 1)

    def row(ahead):
        return (rank + ahead) % 4 * rows

    after, before, across = block(1), block(3), block(2)
    middle = rows // 2
    pieces = (
        (shift(after, 1), row(3)),
        (shift(before, -1), row(1)),
        (shift(across[:middle], 2), row(2)),
        (shift(across[middle:], -2), row(2) + middle),
        (block(0), row(0)),
    )
    whole = jnp.zeros((4 * rows, half), head.dtype)
    for piece, at in pieces:
        whole = lax.dynamic_update_slice_in_dim(whole, piece, at, 0)
    return whole


def by_core(own, other, core):
    return jnp.where(core == 0, own, other), jnp.where(core == 0, other, own)


def three_parts(value):
    first = lax.reduce_precision(value, 8, 7)
    second = lax.reduce_precision(value - first, 8, 7)
    return first, second, value - first - second


def shards(final_normed, embed_cot, head, rest_lse, loss_grad, target_ids, embed_ids):
    core, rank = lax.axis_index("core"), lax.axis_index("tensor")
    tokens, width = final_normed.shape
    half = width // 2
    part = tokens // 4
    vocab = 4 * head.shape[0]
    replicas = lax.axis_size("dp")

    def own_half(value):
        return lax.dynamic_slice_in_dim(value, core * half, half, 1)

    def other_half(value):
        return lax.dynamic_slice_in_dim(value, (1 - core) * half, half, 1)

    window = window_quarter(head, core, rank, half)
    normed = jnp.concatenate(
        by_core(own_half(final_normed), swap_cores(other_half(final_normed)), core), 0
    )

    embed_rows = 8 * replicas
    onehot = (embed_ids[:, None] == lax.broadcasted_iota(jnp.int32, (1, embed_rows), 1)).astype(BF16)
    embed_term = dot(onehot, embed_cot, ((0,), (0,)))
    embed_term = own_half(embed_term) + swap_cores(other_half(embed_term).astype(BF16)).astype(F32)

    logits = dot(normed, window, ((1,), (1,)))
    logits = exchange(logits.reshape(8, part, vocab), OWNERS).sum(0)

    def own_part(value):
        return lax.dynamic_slice_in_dim(value, rank * part, part, 0)[:, None]

    lse_rest = own_part(rest_lse)
    hits = own_part(target_ids) == lax.broadcasted_iota(jnp.int32, (1, vocab), 1)
    top = jnp.maximum(jnp.max(logits, axis=1, keepdims=True), lse_rest)
    total = jnp.exp(lse_rest - top) + jnp.sum(jnp.exp(logits - top), axis=1, keepdims=True)
    lse = top + jnp.log(total)
    loss = lse - jnp.sum(jnp.where(hits, logits, 0.0), axis=1, keepdims=True)
    dlogits = own_part(loss_grad) * (jnp.exp(logits - lse) - hits.astype(F32))

    lane = lax.broadcasted_iota(jnp.int32, (part, 128), 1)
    first, second, third = three_parts(loss)
    extra = jnp.where(lane == 0, first, jnp.where(lane == 1, second, jnp.where(lane == 2, third, 0.0)))
    sent = jnp.concatenate((dlogits, extra), 1).astype(BF16)
    gathered = spread(sent, OWNERS).reshape(2 * tokens, vocab + 128)
    dlogits = gathered[:, :vocab]
    loss = lax.dynamic_slice_in_dim(gathered[:, vocab : vocab + 3], core * tokens, tokens, 0)
    token_loss = jnp.sum(loss.astype(F32), axis=1)

    head_term = dot(dlogits, normed, ((0,), (0,))).astype(BF16).reshape(4, vocab // 4, half)
    embed_term = (
        embed_term.astype(BF16).reshape(replicas, 4, 2, half).swapaxes(0, 1).reshape(4, 2 * replicas, half)
    )
    term = exchange(jnp.concatenate((head_term, embed_term), 1), "x").astype(F32).sum(0).astype(BF16)
    rows = vocab // 4 // replicas
    term = jnp.concatenate(
        (
            term[: vocab // 4].reshape(replicas, rows, half),
            term[vocab // 4 :].reshape(replicas, 2, half),
        ),
        1,
    )
    term = exchange(term, "dp").astype(F32).sum(0).astype(BF16)

    def owner(source):
        source, quarter = divmod(source, 4)
        source, at_core = divmod(source, 2)
        source, at_zhi = divmod(source, 2)
        at_dp, at_x = divmod(source, 4)
        return ((((2 * quarter + at_core) * 4 + at_dp // 2) * 2 + at_zhi) * 2 + at_dp % 2) * 4 + at_x

    every = ("dp",) + REPLICAS + ("tensor",)
    moved = lax.ppermute(term[:rows], every, [(i, owner(i)) for i in range(lax.axis_size(every))])
    pieces = spread(jnp.concatenate((moved, term[rows:]), 0), REPLICAS)
    pieces = pieces.astype(F32).reshape(4, 2, 2, rows + 2, half).sum(1)
    head_grad = pieces[:, :, :rows].reshape(vocab // 4, half)
    embed_grad = pieces[:, :, rows:].transpose(0, 2, 1, 3).reshape(8, width)

    grad_hidden = dot(dlogits, window, ((1,), (0,))).astype(BF16)
    mine = lax.dynamic_slice_in_dim(grad_hidden, core * tokens, tokens, 0)
    theirs = swap_cores(lax.dynamic_slice_in_dim(grad_hidden, (1 - core) * tokens, tokens, 0))
    grad_hidden = jnp.concatenate(by_core(mine, theirs, core), 1)
    return (token_loss, grad_hidden, head_grad, embed_grad)


def solution(mesh):
    sizes = (mesh.shape["dp"], 4, 2, 2, mesh.shape["tensor"])
    split = Mesh(mesh.devices.reshape(sizes), ("dp",) + REPLICAS + ("tensor",))
    token = ("dp",) + REPLICAS
    return jax.shard_map(
        shards,
        mesh=split,
        in_specs=(
            P(token, "tensor"),
            P(token, "tensor"),
            P("tensor", None),
            P(token),
            P(token),
            P(token),
            P(token),
        ),
        out_specs=(P(token), P(token, "tensor"), P("tensor", "dp"), P("dp", "tensor")),
        check_vma=False,
    )
```

time: 383 us -> 149 us (0.39)
  waiting for transfers between devices: 230 us -> 40.7 us
  blocking collectives: 117 us -> 35.4 us
  starting transfers between devices: 3.88 us -> 55.9 us
  between operations: 13.9 us -> 1.19 us
  matrix products: 9.06 us -> 2.48 us
    reduce_scatter x2 -> x0, waiting for transfers between devices: 88.3 us -> none  [the longest x1 50.9 us: shards(): lax.psum_scatter(head_summed, 'dp', scatter_dimension=1, tiled=True)]
    psum x1 -> x0, blocking collectives: 85.3 us -> none  [shards(): head_summed, embed_summed = lax.psum((head_term, embed_term), 'pipe')]
    psum x1 -> x0, waiting for transfers between devices: 84.7 us -> none  [shards(): head_summed, embed_summed = lax.psum((head_term, embed_term), 'pipe')]
    all_gather x1 -> x0, waiting for transfers between devices: 56.3 us -> none  [shards(): normed = lax.all_gather(final_normed, 'tensor', axis=1, tiled=True)]
    all_to_all x1 -> x3, waiting for transfers between devices: 0.01 us -> 37 us  [exchange(): return lax.all_to_all(value, axes, 0, 0)]
    all_to_all x0 -> x2, blocking collectives: none -> 35.4 us  [exchange(): return lax.all_to_all(value, axes, 0, 0)]
    ppermute x0 -> x8, starting transfers between devices: none -> 34.1 us  [the longest x4 20.8 us: shift(): lax.ppermute(value, RING, [(i, (i + by) % count) for i in range(count)])]
    all_gather x4 -> x0, blocking collectives: 31.6 us -> none  [the longest x3 20.3 us: joined(): pieces = jax.tree.map(lambda part: lax.all_gather(part, axis), value)]
  transfers between devices with their start and end apart: 5 -> 11, of which waited for: 4 -> 6; matrix products, arithmetic and copies ran while one was open for 2% -> 4% of each run, Pallas kernels for 0% -> 0%
where the time goes in v1:
time: 149 us; the launch traced here: 148 us
  starting transfers between devices  55.9 us (38%)
  waiting for transfers between devices  40.7 us (27%)
  blocking collectives  35.4 us (24%)
  local copies, waits for them, and re-layouts  8.71 us (6%)
  other arithmetic  3.63 us (2%)
  matrix products  2.48 us (2%)
    all_to_all x3, waiting for transfers between devices, exchange(): return lax.all_to_all(value, axes, 0, 0)  37 us
    all_to_all x2, blocking collectives, exchange(): return lax.all_to_all(value, axes, 0, 0)  35.4 us
    all_to_all x3, starting transfers between devices, exchange(): return lax.all_to_all(value, axes, 0, 0)  21.8 us
    ppermute x4, starting transfers between devices, shift(): lax.ppermute(value, RING, [(i, (i + by) % count) for i in range(count)])  20.8 us
    ppermute x3, starting transfers between devices, swap_cores(): return lax.ppermute(value, 'core', [(0, 1), (1, 0)])  7.44 us
    ppermute x1, starting transfers between devices, shards(): lax.ppermute(term[:rows], every, [(i, owner(i)) for i in range(lax.axis_s...  5.86 us
  transfers between devices with their start and end apart: 11, of which 6 were waited for; matrix products, arithmetic and copies ran while one was open for 4% of the time, Pallas kernels for 0%

profile of v1, /device:TPU:1, one launch (start us, length us, event | category | flops | bytes accessed | tf_op | source)
XLA Modules:
  0.0 148.0 jit_solution(6422709672610933546)
XLA Ops:
  0.7 1.1 constant_dynamic-slice_fusion.3
  1.8 4.8 %collective-permute-start.1 = (bf16[128,896]{1,0:T(8,128)(2,1)S(1)}, bf16[128,896]{1,0:T(8,128)(2,1)S(1)}, u32[]{:S(2)}, u32[]{:S(2)}) collective-permute-start(bf16[128,896]{1,0:T(8,128)(2,1)S(1)} %get-tuple-element.11), channel_id=1, source_target_pairs={{0,1},{1,2},{2,3},{3,8},{8,9},{9,10},{10,11},{11,0},{4,5},{5,6},{6... | collective-permute-start | bytes 688136 | tf_op jit(solution)/shard_map/ppermute | solution.py:19
  6.7 8.6 %collective-permute-start.2 = (bf16[128,896]{1,0:T(8,128)(2,1)S(1)}, bf16[128,896]{1,0:T(8,128)(2,1)S(1)}, u32[]{:S(2)}, u32[]{:S(2)}) collective-permute-start(bf16[128,896]{1,0:T(8,128)(2,1)S(1)} %get-tuple-element.10), channel_id=1, source_target_pairs={{0,11},{1,0},{2,1},{3,2},{8,3},{9,8},{10,9},{11,10},{4,15},{5,4},{... | collective-permute-start | bytes 688136 | tf_op jit(solution)/shard_map/ppermute | solution.py:19
  15.3 1.0 fusion.7
  16.3 1.9 %collective-permute-start.3 = (bf16[64,896]{1,0:T(8,128)(2,1)S(1)}, bf16[64,896]{1,0:T(8,128)(2,1)S(1)}, u32[]{:S(2)}, u32[]{:S(2)}) collective-permute-start(bf16[64,896]{1,0:T(8,128)(2,1)S(1)} %get-tuple-element.9), channel_id=1, source_target_pairs={{0,2},{1,3},{2,8},{3,9},{8,10},{9,11},{10,0},{11,1},{4,6},{5,7},{6... | collective-permute-start | bytes 344072 | tf_op jit(solution)/shard_map/ppermute | solution.py:19
  18.3 5.5 %collective-permute-start.4 = (bf16[64,896]{1,0:T(8,128)(2,1)S(1)}, bf16[64,896]{1,0:T(8,128)(2,1)S(1)}, u32[]{:S(2)}, u32[]{:S(2)}) collective-permute-start(bf16[64,896]{1,0:T(8,128)(2,1)S(1)} %get-tuple-element.8), channel_id=1, source_target_pairs={{0,10},{1,11},{2,0},{3,1},{8,2},{9,3},{10,8},{11,9},{4,14},{5,15},... | collective-permute-start | bytes 344072 | tf_op jit(solution)/shard_map/ppermute | solution.py:19
  23.7 1.0 constant_dynamic-slice_fusion.5
  24.7 3.4 %collective-permute-start = (bf16[128,896]{1,0:T(8,128)(2,1)S(1)}, bf16[128,896]{1,0:T(8,128)(2,1)S(1)}, u32[]{:S(2)}, u32[]{:S(2)}) collective-permute-start(bf16[128,896]{1,0:T(8,128)(2,1)S(1)} %constant_dynamic-slice_fusion.5), channel_id=1, source_target_pairs={{0,4},{4,0},{1,5},{5,1},{2,6},{6,2},{3,7},{7,3},{8,12},{12,8},{9,1... | collective-permute-start | bytes 688136 | tf_op jit(solution)/shard_map/ppermute | solution.py:23
  28.5 1.0 dynamic-slice_dynamic-update-slice_fusion
  29.6 1.3 fusion
  30.9 6.4 %all-to-all-start = ((f32[8,32,512]{2,1,0:T(8,128)}), f32[8,32,512]{2,1,0:T(8,128)S(1)}, u32[]{:S(2)}, u32[]{:S(2)}) async-start(f32[8,32,512]{2,1,0:T(8,128)} %bitcast), calls=%async_computation | async-start | bytes 1048576 | tf_op jit(solution)/shard_map/all_to_all | solution.py:27
  37.4 14.5 %all-to-all-done = f32[8,32,512]{2,1,0:T(8,128)S(1)} async-done(((f32[8,32,512]{2,1,0:T(8,128)}), f32[8,32,512]{2,1,0:T(8,128)S(1)}, u32[]{:S(2)}, u32[]{:S(2)}) %all-to-all-start) | async-done | bytes 524320 | tf_op jit(solution)/shard_map/all_to_all | solution.py:27
  52.7 0.8 broadcast_in_dim.57
  53.4 3.6 %all-to-all-start.1 = ((bf16[8,32,640]{2,1,0:T(8,128)(2,1)}), bf16[8,32,640]{2,1,0:T(8,128)(2,1)S(1)}, u32[]{:S(2)}, u32[]{:S(2)}) async-start(bf16[8,32,640]{2,1,0:T(8,128)(2,1)} %broadcast_in_dim.57), calls=%async_computation.1 | async-start | bytes 655360 | tf_op jit(solution)/shard_map/all_to_all | solution.py:27
  57.4 2.0 %collective-permute-start.6 = (bf16[64,896]{1,0:T(8,128)(2,1)S(1)}, bf16[64,896]{1,0:T(8,128)(2,1)S(1)}, u32[]{:S(2)}, u32[]{:S(2)}) collective-permute-start(bf16[64,896]{1,0:T(8,128)(2,1)S(1)} %dynamic-slice_convert_fusion), channel_id=1, source_target_pairs={{0,4},{4,0},{1,5},{5,1},{2,6},{6,2},{3,7},{7,3},{8,12},{12,8},{9,1... | collective-permute-start | bytes 344072 | tf_op jit(solution)/shard_map/ppermute | solution.py:23
  59.4 1.2 collective-permute-done.6
  60.8 6.6 %all-to-all-done.1 = bf16[8,32,640]{2,1,0:T(8,128)(2,1)S(1)} async-done(((bf16[8,32,640]{2,1,0:T(8,128)(2,1)}), bf16[8,32,640]{2,1,0:T(8,128)(2,1)S(1)}, u32[]{:S(2)}, u32[]{:S(2)}) %all-to-all-start.1) | async-done | bytes 327712 | tf_op jit(solution)/shard_map/all_to_all | solution.py:27
  68.0 18.0 %all_to_all.25 = bf16[4,144,896]{2,1,0:T(8,128)(2,1)S(1)} all-to-all(bf16[4,144,896]{2,1,0:T(8,128)(2,1)S(1)} %pad_maximum_fusion), channel_id=1, replica_groups=mesh['dp'=8,'x'=4,'zhi'=2,'core'=2,'tensor'=4] {'x'}, dimensions={0} | all-to-all | bytes 2064384 | tf_op jit(solution)/shard_map/all_to_all | solution.py:27
  86.3 17.4 %all_to_all.26 = bf16[8,18,896]{2,1,0:T(8,128)(2,1)S(1)} all-to-all(bf16[8,18,896]{2,1,0:T(8,128)(2,1)S(1)} %pad_maximum_fusion.3), channel_id=1, replica_groups=mesh['dp'=8,'x'=4,'zhi'=2,'core'=2,'tensor'=4] {'dp'}, dimensions={0} | all-to-all | bytes 516096 | tf_op jit(solution)/shard_map/all_to_all | solution.py:27
  103.8 5.9 %collective-permute-start.7 = (bf16[16,896]{1,0:T(8,128)(2,1)S(1)}, bf16[16,896]{1,0:T(8,128)(2,1)S(1)}, u32[]{:S(2)}, u32[]{:S(2)}) collective-permute-start(bf16[16,896]{1,0:T(8,128)(2,1)S(1)} %slice.44), channel_id=1, source_target_pairs={{0,0},{1,128},{2,256},{3,384},{4,64},{5,192},{6,320},{7,448},{8,8}... | collective-permute-start | bytes 86024 | tf_op jit(solution)/shard_map/ppermute | solution.py:140
  109.7 1.7 %collective-permute-done.7 = bf16[16,896]{1,0:T(8,128)(2,1)S(1)} collective-permute-done((bf16[16,896]{1,0:T(8,128)(2,1)S(1)}, bf16[16,896]{1,0:T(8,128)(2,1)S(1)}, u32[]{:S(2)}, u32[]{:S(2)}) %collective-permute-start.7) | collective-permute-done | bytes 28704 | tf_op jit(solution)/shard_map/ppermute | solution.py:140
  111.4 0.9 broadcast_in_dim.58
  112.3 11.8 %all-to-all-start.4 = ((bf16[16,18,896]{2,1,0:T(8,128)(2,1)}), bf16[16,18,896]{2,1,0:T(8,128)(2,1)S(1)}, u32[]{:S(2)}, u32[]{:S(2)}) async-start(bf16[16,18,896]{2,1,0:T(8,128)(2,1)} %broadcast_in_dim.58), calls=%async_computation.4 | async-start | bytes 1376256 | tf_op jit(solution)/shard_map/all_to_all | solution.py:27
  124.6 2.0 %collective-permute-start.5 = (bf16[128,896]{1,0:T(8,128)(2,1)S(1)}, bf16[128,896]{1,0:T(8,128)(2,1)S(1)}, u32[]{:S(2)}, u32[]{:S(2)}) collective-permute-start(bf16[128,896]{1,0:T(8,128)(2,1)S(1)} %constant_dynamic-slice_fusion), channel_id=1, source_target_pairs={{0,4},{4,0},{1,5},{5,1},{2,6},{6,2},{3,7},{7,3},{8,12},{12,8},{9,1... | collective-permute-start | bytes 688136 | tf_op jit(solution)/shard_map/ppermute | solution.py:23
  126.7 0.6 convert_reduce_fusion
  127.3 0.7 collective-permute-done.5
  128.1 0.8 pad_maximum_fusion.2
  128.9 15.9 %all-to-all-done.4 = bf16[16,18,896]{2,1,0:T(8,128)(2,1)S(1)} async-done(((bf16[16,18,896]{2,1,0:T(8,128)(2,1)}), bf16[16,18,896]{2,1,0:T(8,128)(2,1)S(1)}, u32[]{:S(2)}, u32[]{:S(2)}) %all-to-all-start.4) | async-done | bytes 516128 | tf_op jit(solution)/shard_map/all_to_all | solution.py:27
  144.8 0.6 reshape.140
  145.4 0.9 reduce_sum.75
  146.5 0.9 copy.33
  147.4 0.6 copy.44
  (64 shorter events, 3.4 us)
Async XLA Ops:
  0.6 56.4 %copy-start = (bf16[128,1792]{1,0:T(8,128)(2,1)S(1)}, bf16[128,1792]{1,0:T(8,128)(2,1)}, u32[]{:S(2)}) copy-start(bf16[128,1792]{1,0:T(8,128)(2,1)} %param.8) | copy-start | bytes 1376260
  1.8 26.4 %collective-permute-start.1 = (bf16[128,896]{1,0:T(8,128)(2,1)S(1)}, bf16[128,896]{1,0:T(8,128)(2,1)S(1)}, u32[]{:S(2)}, u32[]{:S(2)}) collective-permute-start(bf16[128,896]{1,0:T(8,128)(2,1)S(1)} %get-tuple-element.11), channel_id=1, source_target_pairs={{0,1},{1,2},{2,3},{3,8},{8,9},{9,10},{10,11},{11,0},{4,5},{5,6},{6... | collective-permute-start | bytes 688136 | tf_op jit(solution)/shard_map/ppermute | solution.py:19
  6.7 21.7 %collective-permute-start.2 = (bf16[128,896]{1,0:T(8,128)(2,1)S(1)}, bf16[128,896]{1,0:T(8,128)(2,1)S(1)}, u32[]{:S(2)}, u32[]{:S(2)}) collective-permute-start(bf16[128,896]{1,0:T(8,128)(2,1)S(1)} %get-tuple-element.10), channel_id=1, source_target_pairs={{0,11},{1,0},{2,1},{3,2},{8,3},{9,8},{10,9},{11,10},{4,15},{5,4},{... | collective-permute-start | bytes 688136 | tf_op jit(solution)/shard_map/ppermute | solution.py:19
  15.3 14.2 %copy-start.1 = (bf16[128,1792]{1,0:T(8,128)(2,1)S(1)}, bf16[128,1792]{1,0:T(8,128)(2,1)}, u32[]{:S(2)}) copy-start(bf16[128,1792]{1,0:T(8,128)(2,1)} %param.7) | copy-start | bytes 1376260
  16.3 12.1 %collective-permute-start.3 = (bf16[64,896]{1,0:T(8,128)(2,1)S(1)}, bf16[64,896]{1,0:T(8,128)(2,1)S(1)}, u32[]{:S(2)}, u32[]{:S(2)}) collective-permute-start(bf16[64,896]{1,0:T(8,128)(2,1)S(1)} %get-tuple-element.9), channel_id=1, source_target_pairs={{0,2},{1,3},{2,8},{3,9},{8,10},{9,11},{10,0},{11,1},{4,6},{5,7},{6... | collective-permute-start | bytes 344072 | tf_op jit(solution)/shard_map/ppermute | solution.py:19
  18.3 10.2 %collective-permute-start.4 = (bf16[64,896]{1,0:T(8,128)(2,1)S(1)}, bf16[64,896]{1,0:T(8,128)(2,1)S(1)}, u32[]{:S(2)}, u32[]{:S(2)}) collective-permute-start(bf16[64,896]{1,0:T(8,128)(2,1)S(1)} %get-tuple-element.8), channel_id=1, source_target_pairs={{0,10},{1,11},{2,0},{3,1},{8,2},{9,3},{10,8},{11,9},{4,14},{5,15},... | collective-permute-start | bytes 344072 | tf_op jit(solution)/shard_map/ppermute | solution.py:19
  24.7 4.7 %collective-permute-start = (bf16[128,896]{1,0:T(8,128)(2,1)S(1)}, bf16[128,896]{1,0:T(8,128)(2,1)S(1)}, u32[]{:S(2)}, u32[]{:S(2)}) collective-permute-start(bf16[128,896]{1,0:T(8,128)(2,1)S(1)} %constant_dynamic-slice_fusion.5), channel_id=1, source_target_pairs={{0,4},{4,0},{1,5},{5,1},{2,6},{6,2},{3,7},{7,3},{8,12},{12,8},{9,1... | collective-permute-start | bytes 688136 | tf_op jit(solution)/shard_map/ppermute | solution.py:23
  29.4 7.8 %copy-start.4 = (s32[128]{0:T(128)S(1)}, s32[128]{0:T(128)}, u32[]{:S(2)}) copy-start(s32[128]{0:T(128)} %param.12) | copy-start | bytes 1540
  29.4 7.9 %copy-start.5 = (f32[128]{0:T(128)S(1)}, f32[128]{0:T(128)}, u32[]{:S(2)}) copy-start(f32[128]{0:T(128)} %param.11) | copy-start | bytes 1540
  29.6 22.5 %copy-start.2 = (f32[128]{0:T(128)S(1)}, f32[128]{0:T(128)}, u32[]{:S(2)}) copy-start(f32[128]{0:T(128)} %param.10) | copy-start | bytes 1540
  30.9 26.1 %copy-start.3 = (s32[128]{0:T(128)S(1)}, s32[128]{0:T(128)}, u32[]{:S(2)}) copy-start(s32[128]{0:T(128)} %param.13) | copy-start | bytes 1540
  30.9 21.1 %all-to-all-start = ((f32[8,32,512]{2,1,0:T(8,128)}), f32[8,32,512]{2,1,0:T(8,128)S(1)}, u32[]{:S(2)}, u32[]{:S(2)}) async-start(f32[8,32,512]{2,1,0:T(8,128)} %bitcast), calls=%async_computation | async-start | bytes 1048576 | tf_op jit(solution)/shard_map/all_to_all | solution.py:27
  53.4 14.0 %all-to-all-start.1 = ((bf16[8,32,640]{2,1,0:T(8,128)(2,1)}), bf16[8,32,640]{2,1,0:T(8,128)(2,1)S(1)}, u32[]{:S(2)}, u32[]{:S(2)}) async-start(bf16[8,32,640]{2,1,0:T(8,128)(2,1)} %broadcast_in_dim.57), calls=%async_computation.1 | async-start | bytes 655360 | tf_op jit(solution)/shard_map/all_to_all | solution.py:27
  57.4 3.2 %collective-permute-start.6 = (bf16[64,896]{1,0:T(8,128)(2,1)S(1)}, bf16[64,896]{1,0:T(8,128)(2,1)S(1)}, u32[]{:S(2)}, u32[]{:S(2)}) collective-permute-start(bf16[64,896]{1,0:T(8,128)(2,1)S(1)} %dynamic-slice_convert_fusion), channel_id=1, source_target_pairs={{0,4},{4,0},{1,5},{5,1},{2,6},{6,2},{3,7},{7,3},{8,12},{12,8},{9,1... | collective-permute-start | bytes 344072 | tf_op jit(solution)/shard_map/ppermute | solution.py:23
  103.8 7.6 %collective-permute-start.7 = (bf16[16,896]{1,0:T(8,128)(2,1)S(1)}, bf16[16,896]{1,0:T(8,128)(2,1)S(1)}, u32[]{:S(2)}, u32[]{:S(2)}) collective-permute-start(bf16[16,896]{1,0:T(8,128)(2,1)S(1)} %slice.44), channel_id=1, source_target_pairs={{0,0},{1,128},{2,256},{3,384},{4,64},{5,192},{6,320},{7,448},{8,8}... | collective-permute-start | bytes 86024 | tf_op jit(solution)/shard_map/ppermute | solution.py:140
  112.3 32.4 %all-to-all-start.4 = ((bf16[16,18,896]{2,1,0:T(8,128)(2,1)}), bf16[16,18,896]{2,1,0:T(8,128)(2,1)S(1)}, u32[]{:S(2)}, u32[]{:S(2)}) async-start(bf16[16,18,896]{2,1,0:T(8,128)(2,1)} %broadcast_in_dim.58), calls=%async_computation.4 | async-start | bytes 1376256 | tf_op jit(solution)/shard_map/all_to_all | solution.py:27
  124.6 3.4 %collective-permute-start.5 = (bf16[128,896]{1,0:T(8,128)(2,1)S(1)}, bf16[128,896]{1,0:T(8,128)(2,1)S(1)}, u32[]{:S(2)}, u32[]{:S(2)}) collective-permute-start(bf16[128,896]{1,0:T(8,128)(2,1)S(1)} %constant_dynamic-slice_fusion), channel_id=1, source_target_pairs={{0,4},{4,0},{1,5},{5,1},{2,6},{6,2},{3,7},{7,3},{8,12},{12,8},{9,1... | collective-permute-start | bytes 688136 | tf_op jit(solution)/shard_map/ppermute | solution.py:23

commit v2 on v1

v2 whole, which is shorter than its diff:
```python
import jax
import jax.numpy as jnp
from jax import lax
from jax.sharding import Mesh
from jax.sharding import PartitionSpec as P

F32, BF16 = jnp.float32, jnp.bfloat16
RING = ("zhi", "tensor")
GROUP = ("x", "core")
EVERY = ("dp", "x", "zhi", "core", "tensor")
LANES = 128


def dot(a, b, dims):
    return lax.dot_general(a, b, (dims, ((), ())), preferred_element_type=F32)


def shift(value, by):
    count = lax.axis_size(RING)
    return lax.ppermute(value, RING, [(i, (i + by) % count) for i in range(count)])


def swap(value, axis):
    return lax.ppermute(value, axis, [(0, 1), (1, 0)])


def exchange(value, axes):
    return lax.all_to_all(value, axes, 0, 0)


def spread(value, axes):
    count = lax.axis_size(axes)
    return exchange(jnp.broadcast_to(value[None], (count,) + value.shape), axes)


def half_of(value, which):
    half = value.shape[1] // 2
    return lax.dynamic_slice_in_dim(value, which * half, half, 1)


def window_half(head, core, rank):
    rows, width = head.shape
    half = width // 8
    chunk = rows // 4

    def block(ahead):
        at = (rank + ahead) % 4 * (2 * half) + core * half
        return lax.dynamic_slice_in_dim(head, at, half, 1)

    across, middle = block(2), rows // 2
    pieces = (
        (shift(block(1), 1), 3, 0),
        (shift(block(3), -1), 1, 0),
        (shift(across[:middle], 2), 2, 0),
        (shift(across[middle:], -2), 2, 2),
        (block(0), 0, 0),
    )
    whole = jnp.zeros((4, 4, chunk, half), head.dtype)
    for piece, ahead, first in pieces:
        piece = piece.reshape(-1, 1, chunk, half)
        whole = lax.dynamic_update_slice(whole, piece, (first, (rank + ahead) % 4, 0, 0))
    return whole.reshape(4 * rows, half)


def three_parts(value):
    first = lax.reduce_precision(value, 8, 7)
    second = lax.reduce_precision(value - first, 8, 7)
    return first, second, value - first - second


def owner(flip):
    def place(source):
        source, quarter = divmod(source, 4)
        source, at_core = divmod(source, 2)
        source, at_zhi = divmod(source, 2)
        at_dp, at_x = divmod(source, 4)
        at_zhi = at_zhi ^ flip
        return ((((2 * quarter + at_core) * 4 + at_x) * 2 + at_zhi) * 2 + at_dp % 2) * 4 + at_dp // 2

    return [(i, place(i)) for i in range(lax.axis_size(EVERY))]


def shards(final_normed, embed_cot, head, rest_lse, loss_grad, target_ids, embed_ids):
    core, rank = lax.axis_index("core"), lax.axis_index("tensor")
    tokens, width = final_normed.shape
    half = width // 2
    part = tokens // 4
    vocab = 4 * head.shape[0]
    replicas = lax.axis_size("dp")

    mine = window_half(head, core, rank)
    other = swap(mine, "core")
    logits = dot(half_of(final_normed, core), mine, ((1,), (1,))) + dot(
        half_of(final_normed, 1 - core), other, ((1,), (1,))
    )
    logits = exchange(logits.reshape(4, part, vocab), "tensor").sum(0)

    halves = final_normed.reshape(tokens, 2, half).swapaxes(0, 1)
    normed = exchange(
        jnp.broadcast_to(halves[None], (4, 2, tokens, half)).reshape(8, tokens, half), GROUP
    ).reshape(8 * tokens, half)

    embed_rows = 8 * replicas
    onehot = (embed_ids[:, None] == lax.broadcasted_iota(jnp.int32, (1, embed_rows), 1)).astype(BF16)
    embed = dot(onehot, embed_cot, ((0,), (0,))).astype(BF16)
    embed = jnp.pad(embed, ((0, 0), (0, 16 * LANES - width)))
    embed = exchange(embed.reshape(embed_rows, 8, 2 * LANES).swapaxes(0, 1), GROUP).astype(F32).sum(0)
    embed = (embed + swap(embed.astype(BF16), "zhi").astype(F32)).astype(BF16)
    embed = jnp.concatenate(
        (
            embed[:, :LANES].reshape(replicas, 8, LANES),
            embed[:, LANES:].reshape(replicas, 8, LANES),
        ),
        1,
    )

    def own_part(value):
        return lax.dynamic_slice_in_dim(value, rank * part, part, 0)[:, None]

    lse_rest = own_part(rest_lse)
    column = lax.broadcasted_iota(jnp.int32, (1, vocab), 1)
    column = (column // 32 % 4) * 128 + column // 128 * 32 + column % 32
    hits = own_part(target_ids) == column
    top = jnp.maximum(jnp.max(logits, axis=1, keepdims=True), lse_rest)
    total = jnp.exp(lse_rest - top) + jnp.sum(jnp.exp(logits - top), axis=1, keepdims=True)
    lse = top + jnp.log(total)
    loss = lse - jnp.sum(jnp.where(hits, logits, 0.0), axis=1, keepdims=True)
    dlogits = own_part(loss_grad) * (jnp.exp(logits - lse) - hits.astype(F32))

    lane = lax.broadcasted_iota(jnp.int32, (part, LANES), 1)
    first, second, third = three_parts(loss)
    extra = jnp.where(lane == 0, first, jnp.where(lane == 1, second, jnp.where(lane == 2, third, 0.0)))
    sent = jnp.concatenate((dlogits, extra), 1).astype(BF16)
    gathered = spread(sent, "tensor").reshape(tokens, vocab + LANES)
    dlogits = gathered[:, :vocab]
    token_loss = jnp.sum(gathered[:, vocab : vocab + 3].astype(F32), axis=1)

    quarters = dlogits.reshape(tokens, 4, vocab // 4).swapaxes(0, 1)
    quarters = jnp.broadcast_to(quarters[:, None], (4, 2, tokens, vocab // 4))
    quarter = exchange(quarters.reshape(8, tokens, vocab // 4), GROUP).reshape(8 * tokens, vocab // 4)
    term = dot(quarter, normed, ((0,), (0,))).astype(BF16)
    term = jnp.concatenate((term.reshape(replicas, 16, half), embed), 2)
    term = exchange(term, "dp").astype(F32).sum(0).astype(BF16)

    block = term[:, :half]
    moved = lax.ppermute(block, EVERY, owner(0)).astype(F32) + lax.ppermute(
        block, EVERY, owner(1)
    ).astype(F32)
    pieces = spread(jnp.concatenate((moved.astype(BF16), term[:, half:]), 1), GROUP).astype(F32)
    head_grad = pieces[:, :, :half].reshape(vocab // 4, half)
    embed_grad = pieces[: width // (2 * LANES), :, half:].reshape(width // (2 * LANES), 2, 8, LANES)
    embed_grad = embed_grad.transpose(2, 0, 1, 3).reshape(8, width)

    out_mine = dot(dlogits, mine, ((1,), (0,))).astype(BF16)
    out_other = dot(dlogits, other, ((1,), (0,))).astype(BF16)
    grad_hidden = jnp.concatenate(
        (jnp.where(core == 0, out_mine, out_other), jnp.where(core == 0, out_other, out_mine)), 1
    )
    return (token_loss, grad_hidden, head_grad, embed_grad)


def solution(mesh):
    sizes = (mesh.shape["dp"], 4, 2, 2, mesh.shape["tensor"])
    split = Mesh(mesh.devices.reshape(sizes), EVERY)
    token = EVERY[:4]
    return jax.shard_map(
        shards,
        mesh=split,
        in_specs=(
            P(token, "tensor"),
            P(token, "tensor"),
            P("tensor", None),
            P(token),
            P(token),
            P(token),
            P(token),
        ),
        out_specs=(P(token), P(token, "tensor"), P("tensor", "dp"), P("dp", "tensor")),
        check_vma=False,
    )
```

time: 149 us -> 161 us (1.081)
  the two profiles are of different devices: /device:TPU:1 before, /device:TPU:32 now
where the time goes in v2:
time: 161 us; the launch traced here: 160 us
  waiting for transfers between devices  70.7 us (44%)
  starting transfers between devices  65.7 us (41%)
  local copies, waits for them, and re-layouts  13.5 us (8%)
  matrix products  5.1 us (3%)
  other arithmetic  3.94 us (2%)
    all_to_all x7, waiting for transfers between devices, exchange(): return lax.all_to_all(value, axes, 0, 0)  55.4 us
    all_to_all x7, starting transfers between devices, exchange(): return lax.all_to_all(value, axes, 0, 0)  30 us
    ppermute x4, starting transfers between devices, shift(): lax.ppermute(value, RING, [(i, (i + by) % count) for i in range(count)])  19.7 us
    ppermute x1, starting transfers between devices, shards(): lax.ppermute(block, EVERY, owner(1)).astype(F32)  6.41 us
    ppermute x4, waiting for transfers between devices, shift(): lax.ppermute(value, RING, [(i, (i + by) % count) for i in range(count)])  6.27 us
    ppermute x2, starting transfers between devices, swap(): return lax.ppermute(value, axis, [(0, 1), (1, 0)])  5.29 us
    ppermute x1, waiting for transfers between devices, shards(): lax.ppermute(block, EVERY, owner(0)).astype(F32)  5.21 us
    dot_general x6, matrix products, dot(): return lax.dot_general(a, b, (dims, ((), ())), preferred_element_type=F32)  5.1 us
  transfers between devices with their start and end apart: 15, of which 11 were waited for; matrix products, arithmetic and copies ran while one was open for 8% of the time, Pallas kernels for 0%

profile of v2, /device:TPU:32, one launch (start us, length us, event | category | flops | bytes accessed | tf_op | source)
XLA Modules:
  0.0 160.0 jit_solution(319421647522928880)
XLA Ops:
  2.0 4.4 %collective-permute-start = (bf16[128,896]{1,0:T(8,128)(2,1)S(1)}, bf16[128,896]{1,0:T(8,128)(2,1)S(1)}, u32[]{:S(2)}, u32[]{:S(2)}) collective-permute-start(bf16[128,896]{1,0:T(8,128)(2,1)S(1)} %get-tuple-element.10), channel_id=1, source_target_pairs={{0,1},{1,2},{2,3},{3,8},{8,9},{9,10},{10,11},{11,0},{4,5},{5,6},{6... | collective-permute-start | bytes 688136 | tf_op jit(solution)/shard_map/ppermute | solution.py:20
  6.4 8.6 %collective-permute-start.1 = (bf16[128,896]{1,0:T(8,128)(2,1)S(1)}, bf16[128,896]{1,0:T(8,128)(2,1)S(1)}, u32[]{:S(2)}, u32[]{:S(2)}) collective-permute-start(bf16[128,896]{1,0:T(8,128)(2,1)S(1)} %get-tuple-element.9), channel_id=1, source_target_pairs={{0,11},{1,0},{2,1},{3,2},{8,3},{9,8},{10,9},{11,10},{4,15},{5,4},{... | collective-permute-start | bytes 688136 | tf_op jit(solution)/shard_map/ppermute | solution.py:20
  16.0 3.9 %collective-permute-start.3 = (bf16[64,896]{1,0:T(8,128)(2,1)S(1)}, bf16[64,896]{1,0:T(8,128)(2,1)S(1)}, u32[]{:S(2)}, u32[]{:S(2)}) collective-permute-start(bf16[64,896]{1,0:T(8,128)(2,1)S(1)} %get-tuple-element.11), channel_id=1, source_target_pairs={{0,10},{1,11},{2,0},{3,1},{8,2},{9,3},{10,8},{11,9},{4,14},{5,15},... | collective-permute-start | bytes 344072 | tf_op jit(solution)/shard_map/ppermute | solution.py:20
  19.9 2.8 %collective-permute-start.2 = (bf16[64,896]{1,0:T(8,128)(2,1)S(1)}, bf16[64,896]{1,0:T(8,128)(2,1)S(1)}, u32[]{:S(2)}, u32[]{:S(2)}) collective-permute-start(bf16[64,896]{1,0:T(8,128)(2,1)S(1)} %get-tuple-element.12), channel_id=1, source_target_pairs={{0,2},{1,3},{2,8},{3,9},{8,10},{9,11},{10,0},{11,1},{4,6},{5,7},{6... | collective-permute-start | bytes 344072 | tf_op jit(solution)/shard_map/ppermute | solution.py:20
  23.0 6.3 %collective-permute-done.2 = bf16[64,896]{1,0:T(8,128)(2,1)S(1)} collective-permute-done((bf16[64,896]{1,0:T(8,128)(2,1)S(1)}, bf16[64,896]{1,0:T(8,128)(2,1)S(1)}, u32[]{:S(2)}, u32[]{:S(2)}) %collective-permute-start.2) | collective-permute-done | bytes 114720 | tf_op jit(solution)/shard_map/ppermute | solution.py:20
  29.3 1.9 %collective-permute-start.4 = (bf16[512,896]{1,0:T(8,128)(2,1)S(1)}, bf16[512,896]{1,0:T(8,128)(2,1)S(1)}, u32[]{:S(2)}, u32[]{:S(2)}) collective-permute-start(bf16[512,896]{1,0:T(8,128)(2,1)S(1)} %bitcast.41), channel_id=1, source_target_pairs={{0,4},{4,0},{1,5},{5,1},{2,6},{6,2},{3,7},{7,3},{8,12},{12,8},{9,1... | collective-permute-start | bytes 2752520 | tf_op jit(solution)/shard_map/ppermute | solution.py:24
  31.3 2.4 %collective-permute-done.4 = bf16[512,896]{1,0:T(8,128)(2,1)S(1)} collective-permute-done((bf16[512,896]{1,0:T(8,128)(2,1)S(1)}, bf16[512,896]{1,0:T(8,128)(2,1)S(1)}, u32[]{:S(2)}, u32[]{:S(2)}) %collective-permute-start.4) | collective-permute-done | bytes 917536 | tf_op jit(solution)/shard_map/ppermute | solution.py:24
  35.3 4.1 %all-to-all-start = ((f32[4,32,512]{2,1,0:T(8,128)}), f32[4,32,512]{2,1,0:T(8,128)S(1)}, u32[]{:S(2)}, u32[]{:S(2)}) async-start(f32[4,32,512]{2,1,0:T(8,128)} %bitcast.6), calls=%async_computation | async-start | bytes 524288 | tf_op jit(solution)/shard_map/all_to_all | solution.py:28
  40.6 8.0 %all-to-all-done = f32[4,32,512]{2,1,0:T(8,128)S(1)} async-done(((f32[4,32,512]{2,1,0:T(8,128)}), f32[4,32,512]{2,1,0:T(8,128)S(1)}, u32[]{:S(2)}, u32[]{:S(2)}) %all-to-all-start) | async-done | bytes 262176 | tf_op jit(solution)/shard_map/all_to_all | solution.py:28
  48.6 4.3 %all-to-all-start.4 = ((bf16[8,64,256]{2,1,0:T(8,128)(2,1)}), bf16[8,64,256]{2,1,0:T(8,128)(2,1)S(1)}, u32[]{:S(2)}, u32[]{:S(2)}) async-start(bf16[8,64,256]{2,1,0:T(8,128)(2,1)} %bitcast.40), calls=%async_computation.4 | async-start | bytes 524288 | tf_op jit(solution)/shard_map/all_to_all | solution.py:28
  53.6 6.8 %all-to-all-done.4 = bf16[8,64,256]{2,1,0:T(8,128)(2,1)S(1)} async-done(((bf16[8,64,256]{2,1,0:T(8,128)(2,1)}), bf16[8,64,256]{2,1,0:T(8,128)(2,1)S(1)}, u32[]{:S(2)}, u32[]{:S(2)}) %all-to-all-start.4) | async-done | bytes 262176 | tf_op jit(solution)/shard_map/all_to_all | solution.py:28
  61.2 3.3 %all-to-all-start.1 = ((bf16[4,32,640]{2,1,0:T(8,128)(2,1)}), bf16[4,32,640]{2,1,0:T(8,128)(2,1)S(1)}, u32[]{:S(2)}, u32[]{:S(2)}) async-start(bf16[4,32,640]{2,1,0:T(8,128)(2,1)} %broadcast_in_dim.69), calls=%async_computation.1 | async-start | bytes 327680 | tf_op jit(solution)/shard_map/all_to_all | solution.py:28
  64.7 6.2 %all-to-all-done.1 = bf16[4,32,640]{2,1,0:T(8,128)(2,1)S(1)} async-done(((bf16[4,32,640]{2,1,0:T(8,128)(2,1)}), bf16[4,32,640]{2,1,0:T(8,128)(2,1)S(1)}, u32[]{:S(2)}, u32[]{:S(2)}) %all-to-all-start.1) | async-done | bytes 163872 | tf_op jit(solution)/shard_map/all_to_all | solution.py:28
  70.9 1.5 broadcast_in_dim.71
  72.4 3.6 %all-to-all-start.3 = ((bf16[8,128,896]{2,1,0:T(8,128)(2,1)}), bf16[8,128,896]{2,1,0:T(8,128)(2,1)S(1)}, u32[]{:S(2)}, u32[]{:S(2)}) async-start(bf16[8,128,896]{2,1,0:T(8,128)(2,1)} %bitcast.44), calls=%async_computation.3 | async-start | bytes 3670016 | tf_op jit(solution)/shard_map/all_to_all | solution.py:28
  77.0 3.4 %collective-permute-start.5 = (bf16[64,256]{1,0:T(8,128)(2,1)S(1)}, bf16[64,256]{1,0:T(8,128)(2,1)S(1)}, u32[]{:S(2)}, u32[]{:S(2)}) collective-permute-start(bf16[64,256]{1,0:T(8,128)(2,1)S(1)} %convert_element_type.61), channel_id=1, source_target_pairs={{0,8},{8,0},{1,9},{9,1},{2,10},{10,2},{3,11},{11,3},{4,12},{12,4},... | collective-permute-start | bytes 98312 | tf_op jit(solution)/shard_map/ppermute | solution.py:24
  81.1 1.6 reshape.278
  82.7 1.7 %copy.14 = bf16[4,128,128]{1,2,0:T(8,128)(2,1)} copy(bf16[4,128,128]{2,0,1:T(4,128)(2,1)} %bitcast.54) | data formatting | bytes 262144 | tf_op jit(solution)/shard_map/transpose | solution.py:138
  84.3 16.0 %all-to-all-done.3 = bf16[8,128,896]{2,1,0:T(8,128)(2,1)S(1)} async-done(((bf16[8,128,896]{2,1,0:T(8,128)(2,1)}), bf16[8,128,896]{2,1,0:T(8,128)(2,1)S(1)}, u32[]{:S(2)}, u32[]{:S(2)}) %all-to-all-start.3) | async-done | bytes 1835040 | tf_op jit(solution)/shard_map/all_to_all | solution.py:28
  100.3 1.6 %broadcast_in_dim.70 = bf16[4,2,128,128]{2,3,1,0:T(8,128)(2,1)} broadcast(bf16[4,128,128]{1,2,0:T(8,128)(2,1)} %copy.14), dimensions={0,2,3} | broadcast | bytes 393216 | tf_op jit(solution)/shard_map/broadcast_in_dim | solution.py:139
  102.0 4.0 %all-to-all-start.2 = ((bf16[8,128,128]{1,2,0:T(8,128)(2,1)}), bf16[8,128,128]{1,2,0:T(8,128)(2,1)}, u32[]{:S(2)}, u32[]{:S(2)}) async-start(bf16[8,128,128]{1,2,0:T(8,128)(2,1)} %bitcast.50), calls=%async_computation.2 | async-start | bytes 524288 | tf_op jit(solution)/shard_map/all_to_all | solution.py:28
  106.0 7.5 %all-to-all-done.2 = bf16[8,128,128]{1,2,0:T(8,128)(2,1)} async-done(((bf16[8,128,128]{1,2,0:T(8,128)(2,1)}), bf16[8,128,128]{1,2,0:T(8,128)(2,1)}, u32[]{:S(2)}, u32[]{:S(2)}) %all-to-all-start.2) | async-done | bytes 262176 | tf_op jit(solution)/shard_map/all_to_all | solution.py:28
  113.5 1.4 fusion
  115.7 7.2 %all-to-all-start.5 = ((bf16[8,16,1024]{2,1,0:T(8,128)(2,1)}), bf16[8,16,1024]{2,1,0:T(8,128)(2,1)S(1)}, u32[]{:S(2)}, u32[]{:S(2)}) async-start(bf16[8,16,1024]{2,1,0:T(8,128)(2,1)} %maximum_maximum_fusion), calls=%async_computation.5 | async-start | bytes 524288 | tf_op jit(solution)/shard_map/all_to_all | solution.py:28
  122.9 1.5 convolution_convert_fusion.1
  124.7 4.3 %all-to-all-done.5 = bf16[8,16,1024]{2,1,0:T(8,128)(2,1)S(1)} async-done(((bf16[8,16,1024]{2,1,0:T(8,128)(2,1)}), bf16[8,16,1024]{2,1,0:T(8,128)(2,1)S(1)}, u32[]{:S(2)}, u32[]{:S(2)}) %all-to-all-start.5) | async-done | bytes 262176 | tf_op jit(solution)/shard_map/all_to_all | solution.py:28
  129.1 6.4 %collective-permute-start.7 = (bf16[16,896]{1,0:T(8,128)(2,1)S(1)}, bf16[16,896]{1,0:T(8,128)(2,1)S(1)}, u32[]{:S(2)}, u32[]{:S(2)}) collective-permute-start(bf16[16,896]{1,0:T(8,128)(2,1)S(1)} %slice.44), channel_id=1, source_target_pairs={{0,8},{1,136},{2,264},{3,392},{4,72},{5,200},{6,328},{7,456},{8,0}... | collective-permute-start | bytes 86024 | tf_op jit(solution)/shard_map/ppermute | solution.py:146
  135.5 4.2 %collective-permute-start.6 = (bf16[16,896]{1,0:T(8,128)(2,1)S(1)}, bf16[16,896]{1,0:T(8,128)(2,1)S(1)}, u32[]{:S(2)}, u32[]{:S(2)}) collective-permute-start(bf16[16,896]{1,0:T(8,128)(2,1)S(1)} %slice.44), channel_id=1, source_target_pairs={{0,0},{1,128},{2,256},{3,384},{4,64},{5,192},{6,320},{7,448},{8,8}... | collective-permute-start | bytes 86024 | tf_op jit(solution)/shard_map/ppermute | solution.py:146
  140.4 1.4 collective-permute-done.7
  141.8 5.2 %collective-permute-done.6 = bf16[16,896]{1,0:T(8,128)(2,1)S(1)} collective-permute-done((bf16[16,896]{1,0:T(8,128)(2,1)S(1)}, bf16[16,896]{1,0:T(8,128)(2,1)S(1)}, u32[]{:S(2)}, u32[]{:S(2)}) %collective-permute-start.6) | collective-permute-done | bytes 28704 | tf_op jit(solution)/shard_map/ppermute | solution.py:146
  147.7 3.4 %all-to-all-start.6 = ((bf16[8,16,1024]{2,1,0:T(8,128)(2,1)}), bf16[8,16,1024]{2,1,0:T(8,128)(2,1)S(1)}, u32[]{:S(2)}, u32[]{:S(2)}) async-start(bf16[8,16,1024]{2,1,0:T(8,128)(2,1)} %broadcast_in_dim.72), calls=%async_computation.6 | async-start | bytes 524288 | tf_op jit(solution)/shard_map/all_to_all | solution.py:28
  151.9 6.7 %all-to-all-done.6 = bf16[8,16,1024]{2,1,0:T(8,128)(2,1)S(1)} async-done(((bf16[8,16,1024]{2,1,0:T(8,128)(2,1)}), bf16[8,16,1024]{2,1,0:T(8,128)(2,1)S(1)}, u32[]{:S(2)}, u32[]{:S(2)}) %all-to-all-start.6) | async-done | bytes 262176 | tf_op jit(solution)/shard_map/all_to_all | solution.py:28
  (67 shorter events, 13.3 us)
Async XLA Ops:
  0.6 38.7 %copy-start = (bf16[128,1792]{1,0:T(8,128)(2,1)S(1)}, bf16[128,1792]{1,0:T(8,128)(2,1)}, u32[]{:S(2)}) copy-start(bf16[128,1792]{1,0:T(8,128)(2,1)} %param.8) | copy-start | bytes 1376260
  2.0 31.7 %copy-start.2 = (bf16[128,1792]{1,0:T(8,128)(2,1)S(1)}, bf16[128,1792]{1,0:T(8,128)(2,1)}, u32[]{:S(2)}) copy-start(bf16[128,1792]{1,0:T(8,128)(2,1)} %param.7) | copy-start | bytes 1376260
  2.0 20.8 %collective-permute-start = (bf16[128,896]{1,0:T(8,128)(2,1)S(1)}, bf16[128,896]{1,0:T(8,128)(2,1)S(1)}, u32[]{:S(2)}, u32[]{:S(2)}) collective-permute-start(bf16[128,896]{1,0:T(8,128)(2,1)S(1)} %get-tuple-element.10), channel_id=1, source_target_pairs={{0,1},{1,2},{2,3},{3,8},{8,9},{9,10},{10,11},{11,0},{4,5},{5,6},{6... | collective-permute-start | bytes 688136 | tf_op jit(solution)/shard_map/ppermute | solution.py:20
  6.4 16.5 %collective-permute-start.1 = (bf16[128,896]{1,0:T(8,128)(2,1)S(1)}, bf16[128,896]{1,0:T(8,128)(2,1)S(1)}, u32[]{:S(2)}, u32[]{:S(2)}) collective-permute-start(bf16[128,896]{1,0:T(8,128)(2,1)S(1)} %get-tuple-element.9), channel_id=1, source_target_pairs={{0,11},{1,0},{2,1},{3,2},{8,3},{9,8},{10,9},{11,10},{4,15},{5,4},{... | collective-permute-start | bytes 688136 | tf_op jit(solution)/shard_map/ppermute | solution.py:20
  16.0 13.3 %collective-permute-start.3 = (bf16[64,896]{1,0:T(8,128)(2,1)S(1)}, bf16[64,896]{1,0:T(8,128)(2,1)S(1)}, u32[]{:S(2)}, u32[]{:S(2)}) collective-permute-start(bf16[64,896]{1,0:T(8,128)(2,1)S(1)} %get-tuple-element.11), channel_id=1, source_target_pairs={{0,10},{1,11},{2,0},{3,1},{8,2},{9,3},{10,8},{11,9},{4,14},{5,15},... | collective-permute-start | bytes 344072 | tf_op jit(solution)/shard_map/ppermute | solution.py:20
  19.9 9.3 %collective-permute-start.2 = (bf16[64,896]{1,0:T(8,128)(2,1)S(1)}, bf16[64,896]{1,0:T(8,128)(2,1)S(1)}, u32[]{:S(2)}, u32[]{:S(2)}) collective-permute-start(bf16[64,896]{1,0:T(8,128)(2,1)S(1)} %get-tuple-element.12), channel_id=1, source_target_pairs={{0,2},{1,3},{2,8},{3,9},{8,10},{9,11},{10,0},{11,1},{4,6},{5,7},{6... | collective-permute-start | bytes 344072 | tf_op jit(solution)/shard_map/ppermute | solution.py:20
  29.3 10.0 %copy-start.5 = (s32[128]{0:T(128)S(1)}, s32[128]{0:T(128)}, u32[]{:S(2)}) copy-start(s32[128]{0:T(128)} %param.13) | copy-start | bytes 1540
  29.3 4.4 %collective-permute-start.4 = (bf16[512,896]{1,0:T(8,128)(2,1)S(1)}, bf16[512,896]{1,0:T(8,128)(2,1)S(1)}, u32[]{:S(2)}, u32[]{:S(2)}) collective-permute-start(bf16[512,896]{1,0:T(8,128)(2,1)S(1)} %bitcast.41), channel_id=1, source_target_pairs={{0,4},{4,0},{1,5},{5,1},{2,6},{6,2},{3,7},{7,3},{8,12},{12,8},{9,1... | collective-permute-start | bytes 2752520 | tf_op jit(solution)/shard_map/ppermute | solution.py:24
  31.3 8.4 %copy-start.6 = (s32[128]{0:T(128)S(1)}, s32[128]{0:T(128)}, u32[]{:S(2)}) copy-start(s32[128]{0:T(128)} %param.12) | copy-start | bytes 1540
  31.3 8.5 %copy-start.7 = (f32[128]{0:T(128)S(1)}, f32[128]{0:T(128)}, u32[]{:S(2)}) copy-start(f32[128]{0:T(128)} %param.11) | copy-start | bytes 1540
  33.7 6.0 %copy-start.1 = (bf16[512,896]{1,0:T(8,128)(2,1)}, bf16[512,896]{1,0:T(8,128)(2,1)S(1)}, u32[]{:S(2)}) copy-start(bf16[512,896]{1,0:T(8,128)(2,1)S(1)} %collective-permute-done.4) | copy-start | bytes 2752516
  35.3 17.7 %copy-start.4 = (f32[128]{0:T(128)S(1)}, f32[128]{0:T(128)}, u32[]{:S(2)}) copy-start(f32[128]{0:T(128)} %param.10) | copy-start | bytes 1540
  35.3 13.3 %all-to-all-start = ((f32[4,32,512]{2,1,0:T(8,128)}), f32[4,32,512]{2,1,0:T(8,128)S(1)}, u32[]{:S(2)}, u32[]{:S(2)}) async-start(f32[4,32,512]{2,1,0:T(8,128)} %bitcast.6), calls=%async_computation | async-start | bytes 524288 | tf_op jit(solution)/shard_map/all_to_all | solution.py:28
  48.6 11.8 %all-to-all-start.4 = ((bf16[8,64,256]{2,1,0:T(8,128)(2,1)}), bf16[8,64,256]{2,1,0:T(8,128)(2,1)S(1)}, u32[]{:S(2)}, u32[]{:S(2)}) async-start(bf16[8,64,256]{2,1,0:T(8,128)(2,1)} %bitcast.40), calls=%async_computation.4 | async-start | bytes 524288 | tf_op jit(solution)/shard_map/all_to_all | solution.py:28
  60.4 4.2 %copy-start.3 = (bf16[8,64,256]{2,1,0:T(8,128)(2,1)}, bf16[8,64,256]{2,1,0:T(8,128)(2,1)S(1)}, u32[]{:S(2)}) copy-start(bf16[8,64,256]{2,1,0:T(8,128)(2,1)S(1)} %all-to-all-done.4) | copy-start | bytes 786436
  61.2 9.7 %all-to-all-start.1 = ((bf16[4,32,640]{2,1,0:T(8,128)(2,1)}), bf16[4,32,640]{2,1,0:T(8,128)(2,1)S(1)}, u32[]{:S(2)}, u32[]{:S(2)}) async-start(bf16[4,32,640]{2,1,0:T(8,128)(2,1)} %broadcast_in_dim.69), calls=%async_computation.1 | async-start | bytes 327680 | tf_op jit(solution)/shard_map/all_to_all | solution.py:28
  72.4 27.9 %all-to-all-start.3 = ((bf16[8,128,896]{2,1,0:T(8,128)(2,1)}), bf16[8,128,896]{2,1,0:T(8,128)(2,1)S(1)}, u32[]{:S(2)}, u32[]{:S(2)}) async-start(bf16[8,128,896]{2,1,0:T(8,128)(2,1)} %bitcast.44), calls=%async_computation.3 | async-start | bytes 3670016 | tf_op jit(solution)/shard_map/all_to_all | solution.py:28
  77.0 29.0 %collective-permute-start.5 = (bf16[64,256]{1,0:T(8,128)(2,1)S(1)}, bf16[64,256]{1,0:T(8,128)(2,1)S(1)}, u32[]{:S(2)}, u32[]{:S(2)}) collective-permute-start(bf16[64,256]{1,0:T(8,128)(2,1)S(1)} %convert_element_type.61), channel_id=1, source_target_pairs={{0,8},{8,0},{1,9},{9,1},{2,10},{10,2},{3,11},{11,3},{4,12},{12,4},... | collective-permute-start | bytes 98312 | tf_op jit(solution)/shard_map/ppermute | solution.py:24
  102.0 11.6 %all-to-all-start.2 = ((bf16[8,128,128]{1,2,0:T(8,128)(2,1)}), bf16[8,128,128]{1,2,0:T(8,128)(2,1)}, u32[]{:S(2)}, u32[]{:S(2)}) async-start(bf16[8,128,128]{1,2,0:T(8,128)(2,1)} %bitcast.50), calls=%async_computation.2 | async-start | bytes 524288 | tf_op jit(solution)/shard_map/all_to_all | solution.py:28
  115.7 13.3 %all-to-all-start.5 = ((bf16[8,16,1024]{2,1,0:T(8,128)(2,1)}), bf16[8,16,1024]{2,1,0:T(8,128)(2,1)S(1)}, u32[]{:S(2)}, u32[]{:S(2)}) async-start(bf16[8,16,1024]{2,1,0:T(8,128)(2,1)} %maximum_maximum_fusion), calls=%async_computation.5 | async-start | bytes 524288 | tf_op jit(solution)/shard_map/all_to_all | solution.py:28
  129.1 12.7 %collective-permute-start.7 = (bf16[16,896]{1,0:T(8,128)(2,1)S(1)}, bf16[16,896]{1,0:T(8,128)(2,1)S(1)}, u32[]{:S(2)}, u32[]{:S(2)}) collective-permute-start(bf16[16,896]{1,0:T(8,128)(2,1)S(1)} %slice.44), channel_id=1, source_target_pairs={{0,8},{1,136},{2,264},{3,392},{4,72},{5,200},{6,328},{7,456},{8,0}... | collective-permute-start | bytes 86024 | tf_op jit(solution)/shard_map/ppermute | solution.py:146
  135.5 11.5 %collective-permute-start.6 = (bf16[16,896]{1,0:T(8,128)(2,1)S(1)}, bf16[16,896]{1,0:T(8,128)(2,1)S(1)}, u32[]{:S(2)}, u32[]{:S(2)}) collective-permute-start(bf16[16,896]{1,0:T(8,128)(2,1)S(1)} %slice.44), channel_id=1, source_target_pairs={{0,0},{1,128},{2,256},{3,384},{4,64},{5,192},{6,320},{7,448},{8,8}... | collective-permute-start | bytes 86024 | tf_op jit(solution)/shard_map/ppermute | solution.py:146
  147.7 10.9 %all-to-all-start.6 = ((bf16[8,16,1024]{2,1,0:T(8,128)(2,1)}), bf16[8,16,1024]{2,1,0:T(8,128)(2,1)S(1)}, u32[]{:S(2)}, u32[]{:S(2)}) async-start(bf16[8,16,1024]{2,1,0:T(8,128)(2,1)} %broadcast_in_dim.72), calls=%async_computation.6 | async-start | bytes 524288 | tf_op jit(solution)/shard_map/all_to_all | solution.py:28

commit v3 on v2

--- a/solution.py
+++ b/solution.py
@@ -15,9 +15,21 @@
     return lax.dot_general(a, b, (dims, ((), ())), preferred_element_type=F32)
 
 
-def shift(value, by):
+def forward(at):
+    return at + 1
+
+
+def backward(at):
+    return at - 1
+
+
+def across(at):
+    return at + 2 if at % 2 == 0 else at - 2
+
+
+def shift(value, step):
     count = lax.axis_size(RING)
-    return lax.ppermute(value, RING, [(i, (i + by) % count) for i in range(count)])
+    return lax.ppermute(value, RING, [(i, step(i) % count) for i in range(count)])
 
 
 def swap(value, axis):
@@ -47,18 +59,16 @@
         at = (rank + ahead) % 4 * (2 * half) + core * half
         return lax.dynamic_slice_in_dim(head, at, half, 1)
 
-    across, middle = block(2), rows // 2
     pieces = (
-        (shift(block(1), 1), 3, 0),
-        (shift(block(3), -1), 1, 0),
-        (shift(across[:middle], 2), 2, 0),
-        (shift(across[middle:], -2), 2, 2),
-        (block(0), 0, 0),
+        (shift(block(1), forward), 3),
+        (shift(block(3), backward), 1),
+        (shift(block(2), across), 2),
+        (block(0), 0),
     )
     whole = jnp.zeros((4, 4, chunk, half), head.dtype)
-    for piece, ahead, first in pieces:
-        piece = piece.reshape(-1, 1, chunk, half)
-        whole = lax.dynamic_update_slice(whole, piece, (first, (rank + ahead) % 4, 0, 0))
+    for piece, ahead in pieces:
+        piece = piece.reshape(4, 1, chunk, half)
+        whole = lax.dynamic_update_slice(whole, piece, (0, (rank + ahead) % 4, 0, 0))
     return whole.reshape(4 * rows, half)
 
 
@@ -95,24 +105,17 @@
     )
     logits = exchange(logits.reshape(4, part, vocab), "tensor").sum(0)
 
-    halves = final_normed.reshape(tokens, 2, half).swapaxes(0, 1)
-    normed = exchange(
-        jnp.broadcast_to(halves[None], (4, 2, tokens, half)).reshape(8, tokens, half), GROUP
-    ).reshape(8 * tokens, half)
+    normed = lax.all_gather(final_normed, "x", axis=0, tiled=True)
 
     embed_rows = 8 * replicas
     onehot = (embed_ids[:, None] == lax.broadcasted_iota(jnp.int32, (1, embed_rows), 1)).astype(BF16)
-    embed = dot(onehot, embed_cot, ((0,), (0,))).astype(BF16)
+    embed = dot(onehot, embed_cot, ((0,), (0,)))
     embed = jnp.pad(embed, ((0, 0), (0, 16 * LANES - width)))
-    embed = exchange(embed.reshape(embed_rows, 8, 2 * LANES).swapaxes(0, 1), GROUP).astype(F32).sum(0)
+    pairs = [embed[:, i * 4 * LANES : (i + 1) * 4 * LANES] for i in range(4)]
+    embed = jnp.stack([half_of(pair, core) for pair in pairs])
+    embed = embed + swap(jnp.stack([half_of(pair, 1 - core) for pair in pairs]), "core")
     embed = (embed + swap(embed.astype(BF16), "zhi").astype(F32)).astype(BF16)
-    embed = jnp.concatenate(
-        (
-            embed[:, :LANES].reshape(replicas, 8, LANES),
-            embed[:, LANES:].reshape(replicas, 8, LANES),
-        ),
-        1,
-    )
+    embed = jnp.concatenate((embed[:, :, :LANES], embed[:, :, LANES:]), 1)
 
     def own_part(value):
         return lax.dynamic_slice_in_dim(value, rank * part, part, 0)[:, None]
@@ -135,11 +138,13 @@
     dlogits = gathered[:, :vocab]
     token_loss = jnp.sum(gathered[:, vocab : vocab + 3].astype(F32), axis=1)
 
-    quarters = dlogits.reshape(tokens, 4, vocab // 4).swapaxes(0, 1)
-    quarters = jnp.broadcast_to(quarters[:, None], (4, 2, tokens, vocab // 4))
-    quarter = exchange(quarters.reshape(8, tokens, vocab // 4), GROUP).reshape(8 * tokens, vocab // 4)
-    term = dot(quarter, normed, ((0,), (0,))).astype(BF16)
-    term = jnp.concatenate((term.reshape(replicas, 16, half), embed), 2)
+    quarters = jnp.stack([dlogits[:, i * LANES : (i + 1) * LANES] for i in range(4)])
+    quarters = exchange(jnp.concatenate((quarters, embed), 1), "x")
+    term = dot(quarters[:, :tokens].reshape(4 * tokens, LANES), normed, ((0,), (0,)))
+    embed = quarters[:, tokens:].astype(F32).sum(0).astype(BF16).reshape(2, replicas, 8, LANES)
+    embed = jnp.concatenate((embed[0], embed[1]), 1)
+    term = half_of(term, core) + swap(half_of(term, 1 - core).astype(BF16), "core").astype(F32)
+    term = jnp.concatenate((term.astype(BF16).reshape(replicas, 16, half), embed), 2)
     term = exchange(term, "dp").astype(F32).sum(0).astype(BF16)
 
     block = term[:, :half]

time: 161 us -> 140 us (0.87)
  waiting for transfers between devices: 70.7 us -> 39.4 us
  between operations: 1.13 us -> 14.5 us
  blocking collectives: 0 us -> 12.9 us
  starting transfers between devices: 65.7 us -> 56.1 us
  local copies, waits for them, and re-layouts: 13.5 us -> 6.21 us
  other arithmetic: 3.94 us -> 5.67 us
    all_to_all x7 -> x4, waiting for transfers between devices: 55.4 us -> 21.6 us  [exchange(): return lax.all_to_all(value, axes, 0, 0)]
    all_to_all x0 -> x1, blocking collectives: none -> 12.9 us  [exchange(): return lax.all_to_all(value, axes, 0, 0)]
    all_to_all x7 -> x4, starting transfers between devices: 30 us -> 17.9 us  [exchange(): return lax.all_to_all(value, axes, 0, 0)]
    ppermute x2 -> x4, starting transfers between devices: 5.29 us -> 11.2 us  [swap(): return lax.ppermute(value, axis, [(0, 1), (1, 0)])]
    ppermute x4 -> x3, starting transfers between devices: 19.7 us -> 14.8 us  [shift(): lax.ppermute(value, RING, [(i, step(i) % count) for i in range(count)])]
    broadcast_in_dim x2 -> x0, local copies, waits for them, and re-layouts: 3.14 us -> none  [the longest x1 1.64 us: shards(): quarters = jnp.broadcast_to(quarters[:, None], (4, 2, tokens, vocab // 4))]
    ppermute x4 -> x3, waiting for transfers between devices: 6.27 us -> 8.95 us  [shift(): lax.ppermute(value, RING, [(i, step(i) % count) for i in range(count)])]
    reshape x4 -> x0, local copies, waits for them, and re-layouts: 2.43 us -> none  [the longest x1 1.59 us: shards(): quarters = dlogits.reshape(tokens, 4, vocab // 4).swapaxes(0, 1)]
  transfers between devices with their start and end apart: 15 -> 14, of which waited for: 11 -> 9; matrix products, arithmetic and copies ran while one was open for 8% -> 6% of each run, Pallas kernels for 0% -> 0%
where the time goes in v3:
time: 140 us; the launch traced here: 139 us
  starting transfers between devices  56.1 us (40%)
  waiting for transfers between devices  39.4 us (28%)
  between operations  14.5 us (10%)
  blocking collectives  12.9 us (9%)
  local copies, waits for them, and re-layouts  6.21 us (4%)
  other arithmetic  5.67 us (4%)
  matrix products  4.46 us (3%)
    all_to_all x4, waiting for transfers between devices, exchange(): return lax.all_to_all(value, axes, 0, 0)  21.6 us
    all_to_all x4, starting transfers between devices, exchange(): return lax.all_to_all(value, axes, 0, 0)  17.9 us
    ppermute x3, starting transfers between devices, shift(): lax.ppermute(value, RING, [(i, step(i) % count) for i in range(count)])  14.8 us
    all_to_all x1, blocking collectives, exchange(): return lax.all_to_all(value, axes, 0, 0)  12.9 us
    ppermute x4, starting transfers between devices, swap(): return lax.ppermute(value, axis, [(0, 1), (1, 0)])  11.2 us
    ppermute x3, waiting for transfers between devices, shift(): lax.ppermute(value, RING, [(i, step(i) % count) for i in range(count)])  8.95 us
    ppermute x1, starting transfers between devices, shards(): lax.ppermute(block, EVERY, owner(1)).astype(F32)  8.37 us
    ppermute x1, waiting for transfers between devices, shards(): lax.ppermute(block, EVERY, owner(0)).astype(F32)  7.1 us
  transfers between devices with their start and end apart: 14, of which 9 were waited for; matrix products, arithmetic and copies ran while one was open for 6% of the time, Pallas kernels for 0%

profile of v3, /device:TPU:32, one launch (start us, length us, event | category | flops | bytes accessed | tf_op | source)
XLA Modules:
  0.0 139.3 jit_solution(9703174177413807703)
XLA Ops:
  7.3 1.4 constant_dynamic-slice_fusion
  8.7 4.3 %collective-permute-start = (bf16[128,896]{1,0:T(8,128)(2,1)S(1)}, bf16[128,896]{1,0:T(8,128)(2,1)S(1)}, u32[]{:S(2)}, u32[]{:S(2)}) collective-permute-start(bf16[128,896]{1,0:T(8,128)(2,1)S(1)} %get-tuple-element.10), channel_id=1, source_target_pairs={{0,1},{1,2},{2,3},{3,8},{8,9},{9,10},{10,11},{11,0},{4,5},{5,6},{6... | collective-permute-start | bytes 688136 | tf_op jit(solution)/shard_map/ppermute | solution.py:32
  13.0 8.6 %collective-permute-start.1 = (bf16[128,896]{1,0:T(8,128)(2,1)S(1)}, bf16[128,896]{1,0:T(8,128)(2,1)S(1)}, u32[]{:S(2)}, u32[]{:S(2)}) collective-permute-start(bf16[128,896]{1,0:T(8,128)(2,1)S(1)} %get-tuple-element.9), channel_id=1, source_target_pairs={{0,11},{1,0},{2,1},{3,2},{8,3},{9,8},{10,9},{11,10},{4,15},{5,4},{... | collective-permute-start | bytes 688136 | tf_op jit(solution)/shard_map/ppermute | solution.py:32
  21.6 1.9 %collective-permute-start.2 = (bf16[128,896]{1,0:T(8,128)(2,1)S(1)}, bf16[128,896]{1,0:T(8,128)(2,1)S(1)}, u32[]{:S(2)}, u32[]{:S(2)}) collective-permute-start(bf16[128,896]{1,0:T(8,128)(2,1)S(1)} %get-tuple-element.11), channel_id=1, source_target_pairs={{0,2},{1,11},{2,8},{3,1},{8,10},{9,3},{10,0},{11,9},{4,6},{5,15},{... | collective-permute-start | bytes 688136 | tf_op jit(solution)/shard_map/ppermute | solution.py:32
  23.5 1.7 %collective-permute-done = bf16[128,896]{1,0:T(8,128)(2,1)S(1)} collective-permute-done((bf16[128,896]{1,0:T(8,128)(2,1)S(1)}, bf16[128,896]{1,0:T(8,128)(2,1)S(1)}, u32[]{:S(2)}, u32[]{:S(2)}) %collective-permute-start) | collective-permute-done | bytes 229408 | tf_op jit(solution)/shard_map/ppermute | solution.py:32
  25.4 6.0 %collective-permute-done.1 = bf16[128,896]{1,0:T(8,128)(2,1)S(1)} collective-permute-done((bf16[128,896]{1,0:T(8,128)(2,1)S(1)}, bf16[128,896]{1,0:T(8,128)(2,1)S(1)}, u32[]{:S(2)}, u32[]{:S(2)}) %collective-permute-start.1) | collective-permute-done | bytes 229408 | tf_op jit(solution)/shard_map/ppermute | solution.py:32
  31.4 1.2 collective-permute-done.2
  32.7 1.9 %collective-permute-start.3 = (bf16[512,896]{1,0:T(8,128)(2,1)S(1)}, bf16[512,896]{1,0:T(8,128)(2,1)S(1)}, u32[]{:S(2)}, u32[]{:S(2)}) collective-permute-start(bf16[512,896]{1,0:T(8,128)(2,1)S(1)} %bitcast.50), channel_id=1, source_target_pairs={{0,4},{4,0},{1,5},{5,1},{2,6},{6,2},{3,7},{7,3},{8,12},{12,8},{9,1... | collective-permute-start | bytes 2752520 | tf_op jit(solution)/shard_map/ppermute | solution.py:36
  35.2 2.4 %collective-permute-start.4 = (f32[4,64,256]{2,1,0:T(8,128)S(1)}, f32[4,64,256]{2,1,0:T(8,128)S(1)}, u32[]{:S(2)}, u32[]{:S(2)}) collective-permute-start(f32[4,64,256]{2,1,0:T(8,128)S(1)} %pad_maximum_fusion.1), channel_id=1, source_target_pairs={{0,4},{4,0},{1,5},{5,1},{2,6},{6,2},{3,7},{7,3},{8,12},{12,8},{9,1... | collective-permute-start | bytes 786440 | tf_op jit(solution)/shard_map/ppermute | solution.py:36
  38.6 1.1 convolution_add_fusion
  39.7 3.9 %all-to-all-start = ((f32[4,32,512]{2,1,0:T(8,128)}), f32[4,32,512]{2,1,0:T(8,128)S(1)}, u32[]{:S(2)}, u32[]{:S(2)}) async-start(f32[4,32,512]{2,1,0:T(8,128)} %bitcast.5), calls=%async_computation | async-start | bytes 524288 | tf_op jit(solution)/shard_map/all_to_all | solution.py:40
  45.0 4.9 %collective-permute-start.5 = (bf16[4,64,256]{2,1,0:T(8,128)(2,1)S(1)}, bf16[4,64,256]{2,1,0:T(8,128)(2,1)S(1)}, u32[]{:S(2)}, u32[]{:S(2)}) collective-permute-start(bf16[4,64,256]{2,1,0:T(8,128)(2,1)S(1)} %fusion.11), channel_id=1, source_target_pairs={{0,8},{8,0},{1,9},{9,1},{2,10},{10,2},{3,11},{11,3},{4,12},{12,4},... | collective-permute-start | bytes 393224 | tf_op jit(solution)/shard_map/ppermute | solution.py:36
  50.0 2.9 %all-to-all-done = f32[4,32,512]{2,1,0:T(8,128)S(1)} async-done(((f32[4,32,512]{2,1,0:T(8,128)}), f32[4,32,512]{2,1,0:T(8,128)S(1)}, u32[]{:S(2)}, u32[]{:S(2)}) %all-to-all-start) | async-done | bytes 262176 | tf_op jit(solution)/shard_map/all_to_all | solution.py:40
  53.5 0.8 select_convert_fusion
  55.0 3.3 %all-to-all-start.1 = ((bf16[4,32,640]{2,1,0:T(8,128)(2,1)}), bf16[4,32,640]{2,1,0:T(8,128)(2,1)S(1)}, u32[]{:S(2)}, u32[]{:S(2)}) async-start(bf16[4,32,640]{2,1,0:T(8,128)(2,1)} %broadcast_in_dim.57), calls=%async_computation.1 | async-start | bytes 327680 | tf_op jit(solution)/shard_map/all_to_all | solution.py:40
  58.4 5.9 %all-to-all-done.1 = bf16[4,32,640]{2,1,0:T(8,128)(2,1)S(1)} async-done(((bf16[4,32,640]{2,1,0:T(8,128)(2,1)}), bf16[4,32,640]{2,1,0:T(8,128)(2,1)S(1)}, u32[]{:S(2)}, u32[]{:S(2)}) %all-to-all-start.1) | async-done | bytes 163872 | tf_op jit(solution)/shard_map/all_to_all | solution.py:40
  64.3 12.9 %all_to_all.25 = bf16[4,256,128]{2,1,0:T(8,128)(2,1)S(1)} all-to-all(bf16[4,256,128]{2,1,0:T(8,128)(2,1)S(1)} %pad_maximum_fusion.2), channel_id=1, replica_groups=mesh['dp'=8,'x'=4,'zhi'=2,'core'=2,'tensor'=4] {'x'}, dimensions={0} | all-to-all | bytes 524288 | tf_op jit(solution)/shard_map/all_to_all | solution.py:40
  77.3 1.9 %fusion.30 = f32[128,1792]{1,0:T(8,128)S(1)} fusion(bf16[512,128]{1,0:T(8,128)(2,1)S(1)} %bitcast.59, bf16[512,1792]{1,0:T(8,128)(2,1)} %all-gather.2.cloned.1.call-done), kind=kOutput, calls=%fused_computation.94 | convolution fusion | flops 234881024 | bytes 2883584 | tf_op jit(solution)/shard_map/dot_general | solution.py:15
  80.0 1.9 %collective-permute-start.6 = (bf16[128,896]{1,0:T(8,128)(2,1)}, bf16[128,896]{1,0:T(8,128)(2,1)}, u32[]{:S(2)}, u32[]{:S(2)}) collective-permute-start(bf16[128,896]{1,0:T(8,128)(2,1)} %dynamic-slice_convert_fusion), channel_id=1, source_target_pairs={{0,4},{4,0},{1,5},{5,1},{2,6},{6,2},{3,7},{7,3},{8,12},{12,8},{9,1... | collective-permute-start | bytes 688136 | tf_op jit(solution)/shard_map/ppermute | solution.py:36
  82.0 1.7 %collective-permute-done.6 = bf16[128,896]{1,0:T(8,128)(2,1)} collective-permute-done((bf16[128,896]{1,0:T(8,128)(2,1)}, bf16[128,896]{1,0:T(8,128)(2,1)}, u32[]{:S(2)}, u32[]{:S(2)}) %collective-permute-start.6) | collective-permute-done | bytes 229408 | tf_op jit(solution)/shard_map/ppermute | solution.py:36
  83.7 1.0 add_convert_fusion
  84.7 0.7 maximum_maximum_fusion
  85.4 7.2 %all-to-all-start.3 = ((bf16[8,16,1024]{2,1,0:T(8,128)(2,1)}), bf16[8,16,1024]{2,1,0:T(8,128)(2,1)S(1)}, u32[]{:S(2)}, u32[]{:S(2)}) async-start(bf16[8,16,1024]{2,1,0:T(8,128)(2,1)} %maximum_maximum_fusion), calls=%async_computation.3 | async-start | bytes 524288 | tf_op jit(solution)/shard_map/all_to_all | solution.py:40
  93.3 6.2 %all-to-all-done.3 = bf16[8,16,1024]{2,1,0:T(8,128)(2,1)S(1)} async-done(((bf16[8,16,1024]{2,1,0:T(8,128)(2,1)}), bf16[8,16,1024]{2,1,0:T(8,128)(2,1)S(1)}, u32[]{:S(2)}, u32[]{:S(2)}) %all-to-all-start.3) | async-done | bytes 262176 | tf_op jit(solution)/shard_map/all_to_all | solution.py:40
  99.5 8.4 %collective-permute-start.8 = (bf16[16,896]{1,0:T(8,128)(2,1)S(1)}, bf16[16,896]{1,0:T(8,128)(2,1)S(1)}, u32[]{:S(2)}, u32[]{:S(2)}) collective-permute-start(bf16[16,896]{1,0:T(8,128)(2,1)S(1)} %slice.104), channel_id=1, source_target_pairs={{0,8},{1,136},{2,264},{3,392},{4,72},{5,200},{6,328},{7,456},{8,0}... | collective-permute-start | bytes 86024 | tf_op jit(solution)/shard_map/ppermute | solution.py:151
  107.9 3.8 %collective-permute-start.7 = (bf16[16,896]{1,0:T(8,128)(2,1)S(1)}, bf16[16,896]{1,0:T(8,128)(2,1)S(1)}, u32[]{:S(2)}, u32[]{:S(2)}) collective-permute-start(bf16[16,896]{1,0:T(8,128)(2,1)S(1)} %slice.104), channel_id=1, source_target_pairs={{0,0},{1,128},{2,256},{3,384},{4,64},{5,192},{6,320},{7,448},{8,8}... | collective-permute-start | bytes 86024 | tf_op jit(solution)/shard_map/ppermute | solution.py:151
  112.3 7.1 %collective-permute-done.7 = bf16[16,896]{1,0:T(8,128)(2,1)S(1)} collective-permute-done((bf16[16,896]{1,0:T(8,128)(2,1)S(1)}, bf16[16,896]{1,0:T(8,128)(2,1)S(1)}, u32[]{:S(2)}, u32[]{:S(2)}) %collective-permute-start.7) | collective-permute-done | bytes 28704 | tf_op jit(solution)/shard_map/ppermute | solution.py:151
  119.4 0.7 broadcast_in_dim.58
  120.1 3.4 %all-to-all-start.4 = ((bf16[8,16,1024]{2,1,0:T(8,128)(2,1)}), bf16[8,16,1024]{2,1,0:T(8,128)(2,1)S(1)}, u32[]{:S(2)}, u32[]{:S(2)}) async-start(bf16[8,16,1024]{2,1,0:T(8,128)(2,1)} %broadcast_in_dim.58), calls=%async_computation.4 | async-start | bytes 524288 | tf_op jit(solution)/shard_map/all_to_all | solution.py:40
  123.5 0.8 pad_maximum_fusion
  124.3 6.7 %all-to-all-done.4 = bf16[8,16,1024]{2,1,0:T(8,128)(2,1)S(1)} async-done(((bf16[8,16,1024]{2,1,0:T(8,128)(2,1)}), bf16[8,16,1024]{2,1,0:T(8,128)(2,1)S(1)}, u32[]{:S(2)}, u32[]{:S(2)}) %all-to-all-start.4) | async-done | bytes 262176 | tf_op jit(solution)/shard_map/all_to_all | solution.py:40
  131.0 0.8 slice.106
  (61 shorter events, 7.2 us)
Async XLA Ops:
  7.2 27.5 %copy-start = (bf16[128,1792]{1,0:T(8,128)(2,1)S(1)}, bf16[128,1792]{1,0:T(8,128)(2,1)}, u32[]{:S(2)}) copy-start(bf16[128,1792]{1,0:T(8,128)(2,1)} %param.8) | copy-start | bytes 1376260
  7.2 70.1 %all-gather.2.cloned.1.call-start = ((), (), s32[]{:S(2)}) async-start(), calls=%async_computation.5 | async-start | bytes 2293760 | tf_op jit(solution)/shard_map/all_gather | solution.py:108
  8.7 26.0 %copy-start.3 = (s32[128]{0:T(128)S(1)}, s32[128]{0:T(128)}, u32[]{:S(2)}) copy-start(s32[128]{0:T(128)} %param.13) | copy-start | bytes 1540
  8.7 16.5 %collective-permute-start = (bf16[128,896]{1,0:T(8,128)(2,1)S(1)}, bf16[128,896]{1,0:T(8,128)(2,1)S(1)}, u32[]{:S(2)}, u32[]{:S(2)}) collective-permute-start(bf16[128,896]{1,0:T(8,128)(2,1)S(1)} %get-tuple-element.10), channel_id=1, source_target_pairs={{0,1},{1,2},{2,3},{3,8},{8,9},{9,10},{10,11},{11,0},{4,5},{5,6},{6... | collective-permute-start | bytes 688136 | tf_op jit(solution)/shard_map/ppermute | solution.py:32
  13.0 18.4 %collective-permute-start.1 = (bf16[128,896]{1,0:T(8,128)(2,1)S(1)}, bf16[128,896]{1,0:T(8,128)(2,1)S(1)}, u32[]{:S(2)}, u32[]{:S(2)}) collective-permute-start(bf16[128,896]{1,0:T(8,128)(2,1)S(1)} %get-tuple-element.9), channel_id=1, source_target_pairs={{0,11},{1,0},{2,1},{3,2},{8,3},{9,8},{10,9},{11,10},{4,15},{5,4},{... | collective-permute-start | bytes 688136 | tf_op jit(solution)/shard_map/ppermute | solution.py:32
  21.6 11.1 %collective-permute-start.2 = (bf16[128,896]{1,0:T(8,128)(2,1)S(1)}, bf16[128,896]{1,0:T(8,128)(2,1)S(1)}, u32[]{:S(2)}, u32[]{:S(2)}) collective-permute-start(bf16[128,896]{1,0:T(8,128)(2,1)S(1)} %get-tuple-element.11), channel_id=1, source_target_pairs={{0,2},{1,11},{2,8},{3,1},{8,10},{9,3},{10,0},{11,9},{4,6},{5,15},{... | collective-permute-start | bytes 688136 | tf_op jit(solution)/shard_map/ppermute | solution.py:32
  32.7 5.4 %collective-permute-start.3 = (bf16[512,896]{1,0:T(8,128)(2,1)S(1)}, bf16[512,896]{1,0:T(8,128)(2,1)S(1)}, u32[]{:S(2)}, u32[]{:S(2)}) collective-permute-start(bf16[512,896]{1,0:T(8,128)(2,1)S(1)} %bitcast.50), channel_id=1, source_target_pairs={{0,4},{4,0},{1,5},{5,1},{2,6},{6,2},{3,7},{7,3},{8,12},{12,8},{9,1... | collective-permute-start | bytes 2752520 | tf_op jit(solution)/shard_map/ppermute | solution.py:36
  35.0 3.1 %copy-start.1 = (bf16[128,1792]{1,0:T(8,128)(2,1)S(1)}, bf16[128,1792]{1,0:T(8,128)(2,1)}, u32[]{:S(2)}) copy-start(bf16[128,1792]{1,0:T(8,128)(2,1)} %param.7) | copy-start | bytes 1376260
  35.2 9.8 %collective-permute-start.4 = (f32[4,64,256]{2,1,0:T(8,128)S(1)}, f32[4,64,256]{2,1,0:T(8,128)S(1)}, u32[]{:S(2)}, u32[]{:S(2)}) collective-permute-start(f32[4,64,256]{2,1,0:T(8,128)S(1)} %pad_maximum_fusion.1), channel_id=1, source_target_pairs={{0,4},{4,0},{1,5},{5,1},{2,6},{6,2},{3,7},{7,3},{8,12},{12,8},{9,1... | collective-permute-start | bytes 786440 | tf_op jit(solution)/shard_map/ppermute | solution.py:36
  37.6 6.6 %copy-start.4 = (s32[128]{0:T(128)S(1)}, s32[128]{0:T(128)}, u32[]{:S(2)}) copy-start(s32[128]{0:T(128)} %param.12) | copy-start | bytes 1540
  38.6 14.4 %copy-start.2 = (f32[128]{0:T(128)S(1)}, f32[128]{0:T(128)}, u32[]{:S(2)}) copy-start(f32[128]{0:T(128)} %param.10) | copy-start | bytes 1540
  39.7 13.1 %all-to-all-start = ((f32[4,32,512]{2,1,0:T(8,128)}), f32[4,32,512]{2,1,0:T(8,128)S(1)}, u32[]{:S(2)}, u32[]{:S(2)}) async-start(f32[4,32,512]{2,1,0:T(8,128)} %bitcast.5), calls=%async_computation | async-start | bytes 524288 | tf_op jit(solution)/shard_map/all_to_all | solution.py:40
  45.0 13.3 %collective-permute-start.5 = (bf16[4,64,256]{2,1,0:T(8,128)(2,1)S(1)}, bf16[4,64,256]{2,1,0:T(8,128)(2,1)S(1)}, u32[]{:S(2)}, u32[]{:S(2)}) collective-permute-start(bf16[4,64,256]{2,1,0:T(8,128)(2,1)S(1)} %fusion.11), channel_id=1, source_target_pairs={{0,8},{8,0},{1,9},{9,1},{2,10},{10,2},{3,11},{11,3},{4,12},{12,4},... | collective-permute-start | bytes 393224 | tf_op jit(solution)/shard_map/ppermute | solution.py:36
  55.0 9.3 %all-to-all-start.1 = ((bf16[4,32,640]{2,1,0:T(8,128)(2,1)}), bf16[4,32,640]{2,1,0:T(8,128)(2,1)S(1)}, u32[]{:S(2)}, u32[]{:S(2)}) async-start(bf16[4,32,640]{2,1,0:T(8,128)(2,1)} %broadcast_in_dim.57), calls=%async_computation.1 | async-start | bytes 327680 | tf_op jit(solution)/shard_map/all_to_all | solution.py:40
  80.0 3.7 %collective-permute-start.6 = (bf16[128,896]{1,0:T(8,128)(2,1)}, bf16[128,896]{1,0:T(8,128)(2,1)}, u32[]{:S(2)}, u32[]{:S(2)}) collective-permute-start(bf16[128,896]{1,0:T(8,128)(2,1)} %dynamic-slice_convert_fusion), channel_id=1, source_target_pairs={{0,4},{4,0},{1,5},{5,1},{2,6},{6,2},{3,7},{7,3},{8,12},{12,8},{9,1... | collective-permute-start | bytes 688136 | tf_op jit(solution)/shard_map/ppermute | solution.py:36
  85.4 14.0 %all-to-all-start.3 = ((bf16[8,16,1024]{2,1,0:T(8,128)(2,1)}), bf16[8,16,1024]{2,1,0:T(8,128)(2,1)S(1)}, u32[]{:S(2)}, u32[]{:S(2)}) async-start(bf16[8,16,1024]{2,1,0:T(8,128)(2,1)} %maximum_maximum_fusion), calls=%async_computation.3 | async-start | bytes 524288 | tf_op jit(solution)/shard_map/all_to_all | solution.py:40
  99.5 12.8 %collective-permute-start.8 = (bf16[16,896]{1,0:T(8,128)(2,1)S(1)}, bf16[16,896]{1,0:T(8,128)(2,1)S(1)}, u32[]{:S(2)}, u32[]{:S(2)}) collective-permute-start(bf16[16,896]{1,0:T(8,128)(2,1)S(1)} %slice.104), channel_id=1, source_target_pairs={{0,8},{1,136},{2,264},{3,392},{4,72},{5,200},{6,328},{7,456},{8,0}... | collective-permute-start | bytes 86024 | tf_op jit(solution)/shard_map/ppermute | solution.py:151
  107.9 11.5 %collective-permute-start.7 = (bf16[16,896]{1,0:T(8,128)(2,1)S(1)}, bf16[16,896]{1,0:T(8,128)(2,1)S(1)}, u32[]{:S(2)}, u32[]{:S(2)}) collective-permute-start(bf16[16,896]{1,0:T(8,128)(2,1)S(1)} %slice.104), channel_id=1, source_target_pairs={{0,0},{1,128},{2,256},{3,384},{4,64},{5,192},{6,320},{7,448},{8,8}... | collective-permute-start | bytes 86024 | tf_op jit(solution)/shard_map/ppermute | solution.py:151
  120.1 10.9 %all-to-all-start.4 = ((bf16[8,16,1024]{2,1,0:T(8,128)(2,1)}), bf16[8,16,1024]{2,1,0:T(8,128)(2,1)S(1)}, u32[]{:S(2)}, u32[]{:S(2)}) async-start(bf16[8,16,1024]{2,1,0:T(8,128)(2,1)} %broadcast_in_dim.58), calls=%async_computation.4 | async-start | bytes 524288 | tf_op jit(solution)/shard_map/all_to_all | solution.py:40
Sparse Core Ops, SparseCore 0:
  37.7 33.0 all-gather.1

commit v4 on v3

--- a/solution.py
+++ b/solution.py
@@ -72,6 +72,10 @@
     return whole.reshape(4 * rows, half)
 
 
+def by_core(own, other, core):
+    return jnp.concatenate((jnp.where(core == 0, own, other), jnp.where(core == 0, other, own)), 0)
+
+
 def three_parts(value):
     first = lax.reduce_precision(value, 8, 7)
     second = lax.reduce_precision(value - first, 8, 7)
@@ -103,19 +107,17 @@
     logits = dot(half_of(final_normed, core), mine, ((1,), (1,))) + dot(
         half_of(final_normed, 1 - core), other, ((1,), (1,))
     )
-    logits = exchange(logits.reshape(4, part, vocab), "tensor").sum(0)
 
-    normed = lax.all_gather(final_normed, "x", axis=0, tiled=True)
+    normed = swap(half_of(final_normed, 1 - core), "core")
+    logits = exchange(logits.reshape(4, part, vocab), "tensor")
+    logits, normed = lax.optimization_barrier((logits, normed))
+    logits = logits.sum(0)
+    normed = by_core(half_of(final_normed, core), normed, core)
 
-    embed_rows = 8 * replicas
-    onehot = (embed_ids[:, None] == lax.broadcasted_iota(jnp.int32, (1, embed_rows), 1)).astype(BF16)
+    onehot = (embed_ids[:, None] == lax.broadcasted_iota(jnp.int32, (1, 8 * replicas), 1)).astype(BF16)
     embed = dot(onehot, embed_cot, ((0,), (0,)))
-    embed = jnp.pad(embed, ((0, 0), (0, 16 * LANES - width)))
-    pairs = [embed[:, i * 4 * LANES : (i + 1) * 4 * LANES] for i in range(4)]
-    embed = jnp.stack([half_of(pair, core) for pair in pairs])
-    embed = embed + swap(jnp.stack([half_of(pair, 1 - core) for pair in pairs]), "core")
+    embed = half_of(embed, core) + swap(half_of(embed, 1 - core), "core")
     embed = (embed + swap(embed.astype(BF16), "zhi").astype(F32)).astype(BF16)
-    embed = jnp.concatenate((embed[:, :, :LANES], embed[:, :, LANES:]), 1)
 
     def own_part(value):
         return lax.dynamic_slice_in_dim(value, rank * part, part, 0)[:, None]
@@ -134,27 +136,26 @@
     first, second, third = three_parts(loss)
     extra = jnp.where(lane == 0, first, jnp.where(lane == 1, second, jnp.where(lane == 2, third, 0.0)))
     sent = jnp.concatenate((dlogits, extra), 1).astype(BF16)
+
     gathered = spread(sent, "tensor").reshape(tokens, vocab + LANES)
     dlogits = gathered[:, :vocab]
     token_loss = jnp.sum(gathered[:, vocab : vocab + 3].astype(F32), axis=1)
 
-    quarters = jnp.stack([dlogits[:, i * LANES : (i + 1) * LANES] for i in range(4)])
-    quarters = exchange(jnp.concatenate((quarters, embed), 1), "x")
-    term = dot(quarters[:, :tokens].reshape(4 * tokens, LANES), normed, ((0,), (0,)))
-    embed = quarters[:, tokens:].astype(F32).sum(0).astype(BF16).reshape(2, replicas, 8, LANES)
-    embed = jnp.concatenate((embed[0], embed[1]), 1)
-    term = half_of(term, core) + swap(half_of(term, 1 - core).astype(BF16), "core").astype(F32)
-    term = jnp.concatenate((term.astype(BF16).reshape(replicas, 16, half), embed), 2)
+    term = by_core(dlogits, swap(dlogits, "core"), core)
+    term = dot(term, normed, ((0,), (0,))).astype(BF16).reshape(4, vocab // 4, half)
+    term = exchange(term, "x").reshape(4, replicas, 16, half)
+    embed = jnp.stack([embed.reshape(replicas, 8, half)] + [jnp.zeros((replicas, 8, half), BF16)] * 3)
+    term = jnp.concatenate((term, embed), 2).astype(F32).sum(0).astype(BF16)
     term = exchange(term, "dp").astype(F32).sum(0).astype(BF16)
 
-    block = term[:, :half]
+    block = term[:16]
     moved = lax.ppermute(block, EVERY, owner(0)).astype(F32) + lax.ppermute(
         block, EVERY, owner(1)
     ).astype(F32)
-    pieces = spread(jnp.concatenate((moved.astype(BF16), term[:, half:]), 1), GROUP).astype(F32)
-    head_grad = pieces[:, :, :half].reshape(vocab // 4, half)
-    embed_grad = pieces[: width // (2 * LANES), :, half:].reshape(width // (2 * LANES), 2, 8, LANES)
-    embed_grad = embed_grad.transpose(2, 0, 1, 3).reshape(8, width)
+    pieces = spread(jnp.concatenate((moved.astype(BF16), term[16:]), 0), GROUP).astype(F32)
+    head_grad = pieces[:, :16].reshape(vocab // 4, half)
+    embed_grad = pieces[:, 16:].reshape(4, 2, 8, half).sum(0)
+    embed_grad = jnp.concatenate((embed_grad[0], embed_grad[1]), 1)
 
     out_mine = dot(dlogits, mine, ((1,), (0,))).astype(BF16)
     out_other = dot(dlogits, other, ((1,), (0,))).astype(BF16)

time: 140 us -> 132 us (0.943)
  the two profiles are of different devices: /device:TPU:32 before, /device:TPU:16 now
where the time goes in v4:
time: 132 us; the launch traced here: 131 us
  starting transfers between devices  61.6 us (47%)
  waiting for transfers between devices  49.3 us (37%)
  other arithmetic  8.43 us (6%)
  local copies, waits for them, and re-layouts  6.32 us (5%)
  matrix products  3.9 us (3%)
    all_to_all x5, waiting for transfers between devices, exchange(): return lax.all_to_all(value, axes, 0, 0)  23.5 us
    all_to_all x5, starting transfers between devices, exchange(): return lax.all_to_all(value, axes, 0, 0)  23.5 us
    ppermute x3, starting transfers between devices, shift(): lax.ppermute(value, RING, [(i, step(i) % count) for i in range(count)])  14.9 us
    ppermute x5, starting transfers between devices, swap(): return lax.ppermute(value, axis, [(0, 1), (1, 0)])  12.6 us
    ppermute x5, waiting for transfers between devices, swap(): return lax.ppermute(value, axis, [(0, 1), (1, 0)])  11.7 us
    ppermute x3, waiting for transfers between devices, shift(): lax.ppermute(value, RING, [(i, step(i) % count) for i in range(count)])  8.95 us
    ppermute x1, starting transfers between devices, shards(): lax.ppermute(block, EVERY, owner(1)).astype(F32)  8.71 us
    ppermute x1, waiting for transfers between devices, shards(): lax.ppermute(block, EVERY, owner(0)).astype(F32)  5.2 us
  transfers between devices with their start and end apart: 15, of which 11 were waited for; matrix products, arithmetic and copies ran while one was open for 7% of the time, Pallas kernels for 0%

profile of v4, /device:TPU:16, one launch (start us, length us, event | category | flops | bytes accessed | tf_op | source)
XLA Modules:
  0.0 130.7 jit_solution(3524139489027932624)
XLA Ops:
  0.7 1.4 %constant_dynamic-slice_fusion.2 = (bf16[128,896]{1,0:T(8,128)(2,1)S(1)}, bf16[128,896]{1,0:T(8,128)(2,1)S(1)}, bf16[128,896]{1,0:T(8,128)(2,1)S(1)}, bf16[128,896]{1,0:T(8,128)(2,1)S(1)}) fusion(bf16[128,7168]{1,0:T(8,128)(2,1)} %param.9, s32[]{:T(128)S(6)} %select_n.169, s32[]{:T(128)S(6)} %select_n.163, s32[]{:T(128)S(6)} %select_n.160, s32[]{:T(128)S(6)} %select_n.166), kind=kLoop, calls=%fused_computation.57 | loop fusion | bytes 1835024 | tf_op jit(solution)/shard_map/dynamic_slice | solution.py:60
  2.1 4.4 %collective-permute-start = (bf16[128,896]{1,0:T(8,128)(2,1)S(1)}, bf16[128,896]{1,0:T(8,128)(2,1)S(1)}, u32[]{:S(2)}, u32[]{:S(2)}) collective-permute-start(bf16[128,896]{1,0:T(8,128)(2,1)S(1)} %get-tuple-element.14), channel_id=1, source_target_pairs={{0,1},{1,2},{2,3},{3,8},{8,9},{9,10},{10,11},{11,0},{4,5},{5,6},{6... | collective-permute-start | bytes 688136 | tf_op jit(solution)/shard_map/ppermute | solution.py:32
  6.5 8.6 %collective-permute-start.1 = (bf16[128,896]{1,0:T(8,128)(2,1)S(1)}, bf16[128,896]{1,0:T(8,128)(2,1)S(1)}, u32[]{:S(2)}, u32[]{:S(2)}) collective-permute-start(bf16[128,896]{1,0:T(8,128)(2,1)S(1)} %get-tuple-element.13), channel_id=1, source_target_pairs={{0,11},{1,0},{2,1},{3,2},{8,3},{9,8},{10,9},{11,10},{4,15},{5,4},{... | collective-permute-start | bytes 688136 | tf_op jit(solution)/shard_map/ppermute | solution.py:32
  15.1 1.9 %collective-permute-start.2 = (bf16[128,896]{1,0:T(8,128)(2,1)S(1)}, bf16[128,896]{1,0:T(8,128)(2,1)S(1)}, u32[]{:S(2)}, u32[]{:S(2)}) collective-permute-start(bf16[128,896]{1,0:T(8,128)(2,1)S(1)} %get-tuple-element.15), channel_id=1, source_target_pairs={{0,2},{1,11},{2,8},{3,1},{8,10},{9,3},{10,0},{11,9},{4,6},{5,15},{... | collective-permute-start | bytes 688136 | tf_op jit(solution)/shard_map/ppermute | solution.py:32
  17.1 1.7 %collective-permute-done = bf16[128,896]{1,0:T(8,128)(2,1)S(1)} collective-permute-done((bf16[128,896]{1,0:T(8,128)(2,1)S(1)}, bf16[128,896]{1,0:T(8,128)(2,1)S(1)}, u32[]{:S(2)}, u32[]{:S(2)}) %collective-permute-start) | collective-permute-done | bytes 229408 | tf_op jit(solution)/shard_map/ppermute | solution.py:32
  18.9 6.0 %collective-permute-done.1 = bf16[128,896]{1,0:T(8,128)(2,1)S(1)} collective-permute-done((bf16[128,896]{1,0:T(8,128)(2,1)S(1)}, bf16[128,896]{1,0:T(8,128)(2,1)S(1)}, u32[]{:S(2)}, u32[]{:S(2)}) %collective-permute-start.1) | collective-permute-done | bytes 229408 | tf_op jit(solution)/shard_map/ppermute | solution.py:32
  25.0 1.2 collective-permute-done.2
  26.3 1.9 %collective-permute-start.3 = (bf16[512,896]{1,0:T(8,128)(2,1)S(1)}, bf16[512,896]{1,0:T(8,128)(2,1)S(1)}, u32[]{:S(2)}, u32[]{:S(2)}) collective-permute-start(bf16[512,896]{1,0:T(8,128)(2,1)S(1)} %bitcast.23), channel_id=1, source_target_pairs={{0,4},{4,0},{1,5},{5,1},{2,6},{6,2},{3,7},{7,3},{8,12},{12,8},{9,1... | collective-permute-start | bytes 2752520 | tf_op jit(solution)/shard_map/ppermute | solution.py:36
  28.3 2.4 %collective-permute-done.3 = bf16[512,896]{1,0:T(8,128)(2,1)S(1)} collective-permute-done((bf16[512,896]{1,0:T(8,128)(2,1)S(1)}, bf16[512,896]{1,0:T(8,128)(2,1)S(1)}, u32[]{:S(2)}, u32[]{:S(2)}) %collective-permute-start.3) | collective-permute-done | bytes 917536 | tf_op jit(solution)/shard_map/ppermute | solution.py:36
  31.1 1.1 convolution_add_fusion
  32.2 3.9 %all-to-all-start = ((f32[4,32,512]{2,1,0:T(8,128)}), f32[4,32,512]{2,1,0:T(8,128)S(1)}, u32[]{:S(2)}, u32[]{:S(2)}) async-start(f32[4,32,512]{2,1,0:T(8,128)} %bitcast.5), calls=%async_computation | async-start | bytes 524288 | tf_op jit(solution)/shard_map/all_to_all | solution.py:40
  36.2 1.9 %collective-permute-start.4 = (bf16[128,896]{1,0:T(8,128)(2,1)S(1)}, bf16[128,896]{1,0:T(8,128)(2,1)S(1)}, u32[]{:S(2)}, u32[]{:S(2)}) collective-permute-start(bf16[128,896]{1,0:T(8,128)(2,1)S(1)} %constant_dynamic-slice_fusion.1), channel_id=1, source_target_pairs={{0,4},{4,0},{1,5},{5,1},{2,6},{6,2},{3,7},{7,3},{8,12},{12,8},{9,1... | collective-permute-start | bytes 688136 | tf_op jit(solution)/shard_map/ppermute | solution.py:36
  39.8 5.6 %all-to-all-done = f32[4,32,512]{2,1,0:T(8,128)S(1)} async-done(((f32[4,32,512]{2,1,0:T(8,128)}), f32[4,32,512]{2,1,0:T(8,128)S(1)}, u32[]{:S(2)}, u32[]{:S(2)}) %all-to-all-start) | async-done | bytes 262176 | tf_op jit(solution)/shard_map/all_to_all | solution.py:40
  48.1 3.3 %all-to-all-start.1 = ((bf16[4,32,640]{2,1,0:T(8,128)(2,1)}), bf16[4,32,640]{2,1,0:T(8,128)(2,1)S(1)}, u32[]{:S(2)}, u32[]{:S(2)}) async-start(bf16[4,32,640]{2,1,0:T(8,128)(2,1)} %broadcast_in_dim.57), calls=%async_computation.1 | async-start | bytes 327680 | tf_op jit(solution)/shard_map/all_to_all | solution.py:40
  53.3 1.9 %collective-permute-start.6 = (f32[64,896]{1,0:T(8,128)}, f32[64,896]{1,0:T(8,128)}, u32[]{:S(2)}, u32[]{:S(2)}) collective-permute-start(f32[64,896]{1,0:T(8,128)} %constant_dynamic-slice_fusion), channel_id=1, source_target_pairs={{0,4},{4,0},{1,5},{5,1},{2,6},{6,2},{3,7},{7,3},{8,12},{12,8},{9,1... | collective-permute-start | bytes 688136 | tf_op jit(solution)/shard_map/ppermute | solution.py:36
  55.2 2.2 %all-to-all-done.1 = bf16[4,32,640]{2,1,0:T(8,128)(2,1)S(1)} async-done(((bf16[4,32,640]{2,1,0:T(8,128)(2,1)}), bf16[4,32,640]{2,1,0:T(8,128)(2,1)S(1)}, u32[]{:S(2)}, u32[]{:S(2)}) %all-to-all-start.1) | async-done | bytes 163872 | tf_op jit(solution)/shard_map/all_to_all | solution.py:40
  57.4 1.9 %collective-permute-start.5 = (bf16[128,512]{1,0:T(8,128)(2,1)S(1)}, bf16[128,512]{1,0:T(8,128)(2,1)S(1)}, u32[]{:S(2)}, u32[]{:S(2)}) collective-permute-start(bf16[128,512]{1,0:T(8,128)(2,1)S(1)} %slice.33), channel_id=1, source_target_pairs={{0,4},{4,0},{1,5},{5,1},{2,6},{6,2},{3,7},{7,3},{8,12},{12,8},{9,1... | collective-permute-start | bytes 393224 | tf_op jit(solution)/shard_map/ppermute | solution.py:36
  59.5 1.2 collective-permute-done.5
  60.7 1.4 %convolution_convert_fusion = bf16[512,896]{1,0:T(8,128)(2,1)} fusion(bf16[128,896]{1,0:T(8,128)(2,1)S(1)} %get-tuple-element.17, bf16[128,896]{1,0:T(8,128)(2,1)S(1)} %get-tuple-element.16, bf16[128,512]{1,0:T(8,128)(2,1)S(1)} %get-tuple-element.21, bf16[128,512]{1,0:T(8,128)(2,1)S(1)} %get-tuple-element.20), kind=kOutput, calls=%fused_computation | convolution fusion | flops 236781568 | bytes 1638400 | tf_op jit(solution)/shard_map/dot_general | solution.py:15
  62.1 4.3 %all-to-all-start.2 = ((bf16[4,128,896]{2,1,0:T(8,128)(2,1)}), bf16[4,128,896]{2,1,0:T(8,128)(2,1)S(1)}, u32[]{:S(2)}, u32[]{:S(2)}) async-start(bf16[4,128,896]{2,1,0:T(8,128)(2,1)} %bitcast.32), calls=%async_computation.2 | async-start | bytes 1835008 | tf_op jit(solution)/shard_map/all_to_all | solution.py:40
  66.4 1.1 fusion.8
  67.5 4.9 %collective-permute-start.7 = (bf16[64,896]{1,0:T(8,128)(2,1)S(1)}, bf16[64,896]{1,0:T(8,128)(2,1)S(1)}, u32[]{:S(2)}, u32[]{:S(2)}) collective-permute-start(bf16[64,896]{1,0:T(8,128)(2,1)S(1)} %fusion.8), channel_id=1, source_target_pairs={{0,8},{8,0},{1,9},{9,1},{2,10},{10,2},{3,11},{11,3},{4,12},{12,4},... | collective-permute-start | bytes 344072 | tf_op jit(solution)/shard_map/ppermute | solution.py:36
  72.6 8.1 %collective-permute-done.7 = bf16[64,896]{1,0:T(8,128)(2,1)S(1)} collective-permute-done((bf16[64,896]{1,0:T(8,128)(2,1)S(1)}, bf16[64,896]{1,0:T(8,128)(2,1)S(1)}, u32[]{:S(2)}, u32[]{:S(2)}) %collective-permute-start.7) | collective-permute-done | bytes 114720 | tf_op jit(solution)/shard_map/ppermute | solution.py:36
  80.7 1.1 fusion.7
  81.8 1.1 maximum_reduce_fusion
  82.9 7.4 %all-to-all-start.3 = ((bf16[8,24,896]{2,1,0:T(8,128)(2,1)}), bf16[8,24,896]{2,1,0:T(8,128)(2,1)S(1)}, u32[]{:S(2)}, u32[]{:S(2)}) async-start(bf16[8,24,896]{2,1,0:T(8,128)(2,1)} %maximum_reduce_fusion), calls=%async_computation.3 | async-start | bytes 688128 | tf_op jit(solution)/shard_map/all_to_all | solution.py:40
  90.6 8.6 %all-to-all-done.3 = bf16[8,24,896]{2,1,0:T(8,128)(2,1)S(1)} async-done(((bf16[8,24,896]{2,1,0:T(8,128)(2,1)}), bf16[8,24,896]{2,1,0:T(8,128)(2,1)S(1)}, u32[]{:S(2)}, u32[]{:S(2)}) %all-to-all-start.3) | async-done | bytes 344096 | tf_op jit(solution)/shard_map/all_to_all | solution.py:40
  99.3 8.7 %collective-permute-start.9 = (bf16[16,896]{1,0:T(8,128)(2,1)S(1)}, bf16[16,896]{1,0:T(8,128)(2,1)S(1)}, u32[]{:S(2)}, u32[]{:S(2)}) collective-permute-start(bf16[16,896]{1,0:T(8,128)(2,1)S(1)} %slice.34), channel_id=1, source_target_pairs={{0,8},{1,136},{2,264},{3,392},{4,72},{5,200},{6,328},{7,456},{8,0}... | collective-permute-start | bytes 86024 | tf_op jit(solution)/shard_map/ppermute | solution.py:152
  108.0 1.9 %collective-permute-start.8 = (bf16[16,896]{1,0:T(8,128)(2,1)S(1)}, bf16[16,896]{1,0:T(8,128)(2,1)S(1)}, u32[]{:S(2)}, u32[]{:S(2)}) collective-permute-start(bf16[16,896]{1,0:T(8,128)(2,1)S(1)} %slice.34), channel_id=1, source_target_pairs={{0,0},{1,128},{2,256},{3,384},{4,64},{5,192},{6,320},{7,448},{8,8}... | collective-permute-start | bytes 86024 | tf_op jit(solution)/shard_map/ppermute | solution.py:152
  110.4 5.2 %collective-permute-done.8 = bf16[16,896]{1,0:T(8,128)(2,1)S(1)} collective-permute-done((bf16[16,896]{1,0:T(8,128)(2,1)S(1)}, bf16[16,896]{1,0:T(8,128)(2,1)S(1)}, u32[]{:S(2)}, u32[]{:S(2)}) %collective-permute-start.8) | collective-permute-done | bytes 28704 | tf_op jit(solution)/shard_map/ppermute | solution.py:152
  116.3 4.5 %all-to-all-start.4 = ((bf16[8,24,896]{2,1,0:T(8,128)(2,1)}), bf16[8,24,896]{2,1,0:T(8,128)(2,1)S(1)}, u32[]{:S(2)}, u32[]{:S(2)}) async-start(bf16[8,24,896]{2,1,0:T(8,128)(2,1)} %broadcast_in_dim.58), calls=%async_computation.4 | async-start | bytes 688128 | tf_op jit(solution)/shard_map/all_to_all | solution.py:40
  122.2 7.1 %all-to-all-done.4 = bf16[8,24,896]{2,1,0:T(8,128)(2,1)S(1)} async-done(((bf16[8,24,896]{2,1,0:T(8,128)(2,1)}), bf16[8,24,896]{2,1,0:T(8,128)(2,1)S(1)}, u32[]{:S(2)}, u32[]{:S(2)}) %all-to-all-start.4) | async-done | bytes 344096 | tf_op jit(solution)/shard_map/all_to_all | solution.py:40
  (66 shorter events, 11.5 us)
Async XLA Ops:
  0.6 50.8 %copy-start = (bf16[128,1792]{1,0:T(8,128)(2,1)S(1)}, bf16[128,1792]{1,0:T(8,128)(2,1)}, u32[]{:S(2)}) copy-start(bf16[128,1792]{1,0:T(8,128)(2,1)} %param.8) | copy-start | bytes 1376260
  2.1 26.1 %copy-start.2 = (bf16[128,1792]{1,0:T(8,128)(2,1)S(1)}, bf16[128,1792]{1,0:T(8,128)(2,1)}, u32[]{:S(2)}) copy-start(bf16[128,1792]{1,0:T(8,128)(2,1)} %param.7) | copy-start | bytes 1376260
  2.1 16.7 %collective-permute-start = (bf16[128,896]{1,0:T(8,128)(2,1)S(1)}, bf16[128,896]{1,0:T(8,128)(2,1)S(1)}, u32[]{:S(2)}, u32[]{:S(2)}) collective-permute-start(bf16[128,896]{1,0:T(8,128)(2,1)S(1)} %get-tuple-element.14), channel_id=1, source_target_pairs={{0,1},{1,2},{2,3},{3,8},{8,9},{9,10},{10,11},{11,0},{4,5},{5,6},{6... | collective-permute-start | bytes 688136 | tf_op jit(solution)/shard_map/ppermute | solution.py:32
  6.5 18.4 %collective-permute-start.1 = (bf16[128,896]{1,0:T(8,128)(2,1)S(1)}, bf16[128,896]{1,0:T(8,128)(2,1)S(1)}, u32[]{:S(2)}, u32[]{:S(2)}) collective-permute-start(bf16[128,896]{1,0:T(8,128)(2,1)S(1)} %get-tuple-element.13), channel_id=1, source_target_pairs={{0,11},{1,0},{2,1},{3,2},{8,3},{9,8},{10,9},{11,10},{4,15},{5,4},{... | collective-permute-start | bytes 688136 | tf_op jit(solution)/shard_map/ppermute | solution.py:32
  15.1 11.1 %collective-permute-start.2 = (bf16[128,896]{1,0:T(8,128)(2,1)S(1)}, bf16[128,896]{1,0:T(8,128)(2,1)S(1)}, u32[]{:S(2)}, u32[]{:S(2)}) collective-permute-start(bf16[128,896]{1,0:T(8,128)(2,1)S(1)} %get-tuple-element.15), channel_id=1, source_target_pairs={{0,2},{1,11},{2,8},{3,1},{8,10},{9,3},{10,0},{11,9},{4,6},{5,15},{... | collective-permute-start | bytes 688136 | tf_op jit(solution)/shard_map/ppermute | solution.py:32
  26.3 4.4 %collective-permute-start.3 = (bf16[512,896]{1,0:T(8,128)(2,1)S(1)}, bf16[512,896]{1,0:T(8,128)(2,1)S(1)}, u32[]{:S(2)}, u32[]{:S(2)}) collective-permute-start(bf16[512,896]{1,0:T(8,128)(2,1)S(1)} %bitcast.23), channel_id=1, source_target_pairs={{0,4},{4,0},{1,5},{5,1},{2,6},{6,2},{3,7},{7,3},{8,12},{12,8},{9,1... | collective-permute-start | bytes 2752520 | tf_op jit(solution)/shard_map/ppermute | solution.py:36
  28.3 10.4 %copy-start.5 = (s32[128]{0:T(128)S(1)}, s32[128]{0:T(128)}, u32[]{:S(2)}) copy-start(s32[128]{0:T(128)} %param.12) | copy-start | bytes 1540
  28.3 10.4 %copy-start.6 = (f32[128]{0:T(128)S(1)}, f32[128]{0:T(128)}, u32[]{:S(2)}) copy-start(f32[128]{0:T(128)} %param.11) | copy-start | bytes 1540
  28.3 17.3 %copy-start.3 = (f32[128]{0:T(128)S(1)}, f32[128]{0:T(128)}, u32[]{:S(2)}) copy-start(f32[128]{0:T(128)} %param.10) | copy-start | bytes 1540
  31.1 20.4 %copy-start.4 = (s32[128]{0:T(128)S(1)}, s32[128]{0:T(128)}, u32[]{:S(2)}) copy-start(s32[128]{0:T(128)} %param.13) | copy-start | bytes 1540
  32.2 13.2 %all-to-all-start = ((f32[4,32,512]{2,1,0:T(8,128)}), f32[4,32,512]{2,1,0:T(8,128)S(1)}, u32[]{:S(2)}, u32[]{:S(2)}) async-start(f32[4,32,512]{2,1,0:T(8,128)} %bitcast.5), calls=%async_computation | async-start | bytes 524288 | tf_op jit(solution)/shard_map/all_to_all | solution.py:40
  36.2 3.6 %collective-permute-start.4 = (bf16[128,896]{1,0:T(8,128)(2,1)S(1)}, bf16[128,896]{1,0:T(8,128)(2,1)S(1)}, u32[]{:S(2)}, u32[]{:S(2)}) collective-permute-start(bf16[128,896]{1,0:T(8,128)(2,1)S(1)} %constant_dynamic-slice_fusion.1), channel_id=1, source_target_pairs={{0,4},{4,0},{1,5},{5,1},{2,6},{6,2},{3,7},{7,3},{8,12},{12,8},{9,1... | collective-permute-start | bytes 688136 | tf_op jit(solution)/shard_map/ppermute | solution.py:36
  48.1 9.3 %all-to-all-start.1 = ((bf16[4,32,640]{2,1,0:T(8,128)(2,1)}), bf16[4,32,640]{2,1,0:T(8,128)(2,1)S(1)}, u32[]{:S(2)}, u32[]{:S(2)}) async-start(bf16[4,32,640]{2,1,0:T(8,128)(2,1)} %broadcast_in_dim.57), calls=%async_computation.1 | async-start | bytes 327680 | tf_op jit(solution)/shard_map/all_to_all | solution.py:40
  51.8 0.8 copy-start.1
  53.3 13.1 %collective-permute-start.6 = (f32[64,896]{1,0:T(8,128)}, f32[64,896]{1,0:T(8,128)}, u32[]{:S(2)}, u32[]{:S(2)}) collective-permute-start(f32[64,896]{1,0:T(8,128)} %constant_dynamic-slice_fusion), channel_id=1, source_target_pairs={{0,4},{4,0},{1,5},{5,1},{2,6},{6,2},{3,7},{7,3},{8,12},{12,8},{9,1... | collective-permute-start | bytes 688136 | tf_op jit(solution)/shard_map/ppermute | solution.py:36
  57.4 3.2 %collective-permute-start.5 = (bf16[128,512]{1,0:T(8,128)(2,1)S(1)}, bf16[128,512]{1,0:T(8,128)(2,1)S(1)}, u32[]{:S(2)}, u32[]{:S(2)}) collective-permute-start(bf16[128,512]{1,0:T(8,128)(2,1)S(1)} %slice.33), channel_id=1, source_target_pairs={{0,4},{4,0},{1,5},{5,1},{2,6},{6,2},{3,7},{7,3},{8,12},{12,8},{9,1... | collective-permute-start | bytes 393224 | tf_op jit(solution)/shard_map/ppermute | solution.py:36
  62.1 19.7 %all-to-all-start.2 = ((bf16[4,128,896]{2,1,0:T(8,128)(2,1)}), bf16[4,128,896]{2,1,0:T(8,128)(2,1)S(1)}, u32[]{:S(2)}, u32[]{:S(2)}) async-start(bf16[4,128,896]{2,1,0:T(8,128)(2,1)} %bitcast.32), calls=%async_computation.2 | async-start | bytes 1835008 | tf_op jit(solution)/shard_map/all_to_all | solution.py:40
  67.5 13.2 %collective-permute-start.7 = (bf16[64,896]{1,0:T(8,128)(2,1)S(1)}, bf16[64,896]{1,0:T(8,128)(2,1)S(1)}, u32[]{:S(2)}, u32[]{:S(2)}) collective-permute-start(bf16[64,896]{1,0:T(8,128)(2,1)S(1)} %fusion.8), channel_id=1, source_target_pairs={{0,8},{8,0},{1,9},{9,1},{2,10},{10,2},{3,11},{11,3},{4,12},{12,4},... | collective-permute-start | bytes 344072 | tf_op jit(solution)/shard_map/ppermute | solution.py:36
  82.9 16.4 %all-to-all-start.3 = ((bf16[8,24,896]{2,1,0:T(8,128)(2,1)}), bf16[8,24,896]{2,1,0:T(8,128)(2,1)S(1)}, u32[]{:S(2)}, u32[]{:S(2)}) async-start(bf16[8,24,896]{2,1,0:T(8,128)(2,1)} %maximum_reduce_fusion), calls=%async_computation.3 | async-start | bytes 688128 | tf_op jit(solution)/shard_map/all_to_all | solution.py:40
  99.3 11.1 %collective-permute-start.9 = (bf16[16,896]{1,0:T(8,128)(2,1)S(1)}, bf16[16,896]{1,0:T(8,128)(2,1)S(1)}, u32[]{:S(2)}, u32[]{:S(2)}) collective-permute-start(bf16[16,896]{1,0:T(8,128)(2,1)S(1)} %slice.34), channel_id=1, source_target_pairs={{0,8},{1,136},{2,264},{3,392},{4,72},{5,200},{6,328},{7,456},{8,0}... | collective-permute-start | bytes 86024 | tf_op jit(solution)/shard_map/ppermute | solution.py:152
  108.0 7.6 %collective-permute-start.8 = (bf16[16,896]{1,0:T(8,128)(2,1)S(1)}, bf16[16,896]{1,0:T(8,128)(2,1)S(1)}, u32[]{:S(2)}, u32[]{:S(2)}) collective-permute-start(bf16[16,896]{1,0:T(8,128)(2,1)S(1)} %slice.34), channel_id=1, source_target_pairs={{0,0},{1,128},{2,256},{3,384},{4,64},{5,192},{6,320},{7,448},{8,8}... | collective-permute-start | bytes 86024 | tf_op jit(solution)/shard_map/ppermute | solution.py:152
  116.3 12.9 %all-to-all-start.4 = ((bf16[8,24,896]{2,1,0:T(8,128)(2,1)}), bf16[8,24,896]{2,1,0:T(8,128)(2,1)S(1)}, u32[]{:S(2)}, u32[]{:S(2)}) async-start(bf16[8,24,896]{2,1,0:T(8,128)(2,1)} %broadcast_in_dim.58), calls=%async_computation.4 | async-start | bytes 688128 | tf_op jit(solution)/shard_map/all_to_all | solution.py:40

commit v5 on v4

--- a/solution.py
+++ b/solution.py
@@ -108,19 +108,21 @@
         half_of(final_normed, 1 - core), other, ((1,), (1,))
     )
 
-    normed = swap(half_of(final_normed, 1 - core), "core")
-    logits = exchange(logits.reshape(4, part, vocab), "tensor")
-    logits, normed = lax.optimization_barrier((logits, normed))
-    logits = logits.sum(0)
-    normed = by_core(half_of(final_normed, core), normed, core)
-
     onehot = (embed_ids[:, None] == lax.broadcasted_iota(jnp.int32, (1, 8 * replicas), 1)).astype(BF16)
     embed = dot(onehot, embed_cot, ((0,), (0,)))
-    embed = half_of(embed, core) + swap(half_of(embed, 1 - core), "core")
-    embed = (embed + swap(embed.astype(BF16), "zhi").astype(F32)).astype(BF16)
+    given = (half_of(final_normed, 1 - core), half_of(embed, 1 - core))
+    logits, given = lax.optimization_barrier((logits, given))
+    logits = exchange(logits.reshape(4, part, vocab), "tensor")
+    taken = (swap(given[0], "core"), swap(given[1], "core"))
+    logits, taken = lax.optimization_barrier((logits, taken))
+    logits = logits.sum(0)
+    normed = by_core(half_of(final_normed, core), taken[0], core)
+    embed = half_of(embed, core) + taken[1]
 
     def own_part(value):
-        return lax.dynamic_slice_in_dim(value, rank * part, part, 0)[:, None]
+        pieces = [value[i * part : (i + 1) * part] for i in range(4)]
+        low, high = (jnp.where(rank % 2 == 0, pieces[i], pieces[i + 1]) for i in (0, 2))
+        return jnp.where(rank < 2, low, high)[:, None]
 
     lse_rest = own_part(rest_lse)
     column = lax.broadcasted_iota(jnp.int32, (1, vocab), 1)
@@ -132,9 +134,7 @@
     loss = lse - jnp.sum(jnp.where(hits, logits, 0.0), axis=1, keepdims=True)
     dlogits = own_part(loss_grad) * (jnp.exp(logits - lse) - hits.astype(F32))
 
-    lane = lax.broadcasted_iota(jnp.int32, (part, LANES), 1)
-    first, second, third = three_parts(loss)
-    extra = jnp.where(lane == 0, first, jnp.where(lane == 1, second, jnp.where(lane == 2, third, 0.0)))
+    extra = jnp.concatenate(three_parts(loss) + (jnp.zeros((part, LANES - 3), F32),), 1)
     sent = jnp.concatenate((dlogits, extra), 1).astype(BF16)
 
     gathered = spread(sent, "tensor").reshape(tokens, vocab + LANES)
@@ -144,6 +144,7 @@
     term = by_core(dlogits, swap(dlogits, "core"), core)
     term = dot(term, normed, ((0,), (0,))).astype(BF16).reshape(4, vocab // 4, half)
     term = exchange(term, "x").reshape(4, replicas, 16, half)
+    embed = (embed + swap(embed.astype(BF16), "zhi").astype(F32)).astype(BF16)
     embed = jnp.stack([embed.reshape(replicas, 8, half)] + [jnp.zeros((replicas, 8, half), BF16)] * 3)
     term = jnp.concatenate((term, embed), 2).astype(F32).sum(0).astype(BF16)
     term = exchange(term, "dp").astype(F32).sum(0).astype(BF16)

time: 132 us -> 131 us (level)
  other arithmetic: 8.43 us -> 6.93 us
    all_to_all x5, waiting for transfers between devices: 23.5 us -> 25.3 us  [exchange(): return lax.all_to_all(value, axes, 0, 0)]
    ppermute x5, waiting for transfers between devices: 11.7 us -> 10.2 us  [swap(): return lax.ppermute(value, axis, [(0, 1), (1, 0)])]
    another operation x2 -> x1, other arithmetic: 1.48 us -> 0.09 us
  transfers between devices with their start and end apart: 15 -> 15, of which waited for: 11 -> 12; matrix products, arithmetic and copies ran while one was open for 7% -> 5% of each run, Pallas kernels for 0% -> 0%
where the time goes in v5:
time: 131 us; the launch traced here: 130 us
  starting transfers between devices  62.2 us (47%)
  waiting for transfers between devices  49.7 us (38%)
  other arithmetic  6.93 us (5%)
  local copies, waits for them, and re-layouts  6.05 us (5%)
  matrix products  3.91 us (3%)
    all_to_all x5, waiting for transfers between devices, exchange(): return lax.all_to_all(value, axes, 0, 0)  25.3 us
    all_to_all x5, starting transfers between devices, exchange(): return lax.all_to_all(value, axes, 0, 0)  23.5 us
    ppermute x3, starting transfers between devices, shift(): lax.ppermute(value, RING, [(i, step(i) % count) for i in range(count)])  14.9 us
    ppermute x5, starting transfers between devices, swap(): return lax.ppermute(value, axis, [(0, 1), (1, 0)])  13.1 us
    ppermute x5, waiting for transfers between devices, swap(): return lax.ppermute(value, axis, [(0, 1), (1, 0)])  10.2 us
    ppermute x3, waiting for transfers between devices, shift(): lax.ppermute(value, RING, [(i, step(i) % count) for i in range(count)])  8.95 us
    ppermute x1, starting transfers between devices, shards(): lax.ppermute(block, EVERY, owner(1)).astype(F32)  8.82 us
    ppermute x1, waiting for transfers between devices, shards(): lax.ppermute(block, EVERY, owner(0)).astype(F32)  5.2 us
  transfers between devices with their start and end apart: 15, of which 12 were waited for; matrix products, arithmetic and copies ran while one was open for 5% of the time, Pallas kernels for 0%

profile of v5, /device:TPU:16, one launch (start us, length us, event | category | flops | bytes accessed | tf_op | source)
XLA Modules:
  0.0 129.9 jit_solution(55348716495220688)
XLA Ops:
  0.7 1.4 %constant_dynamic-slice_fusion.2 = (bf16[128,896]{1,0:T(8,128)(2,1)S(1)}, bf16[128,896]{1,0:T(8,128)(2,1)S(1)}, bf16[128,896]{1,0:T(8,128)(2,1)S(1)}, bf16[128,896]{1,0:T(8,128)(2,1)S(1)}) fusion(bf16[128,7168]{1,0:T(8,128)(2,1)} %param.9, s32[]{:T(128)S(6)} %select_n.210, s32[]{:T(128)S(6)} %select_n.204, s32[]{:T(128)S(6)} %select_n.201, s32[]{:T(128)S(6)} %select_n.207), kind=kLoop, calls=%fused_computation.55 | loop fusion | bytes 1835024 | tf_op jit(solution)/shard_map/dynamic_slice | solution.py:60
  2.1 4.4 %collective-permute-start = (bf16[128,896]{1,0:T(8,128)(2,1)S(1)}, bf16[128,896]{1,0:T(8,128)(2,1)S(1)}, u32[]{:S(2)}, u32[]{:S(2)}) collective-permute-start(bf16[128,896]{1,0:T(8,128)(2,1)S(1)} %get-tuple-element.24), channel_id=1, source_target_pairs={{0,1},{1,2},{2,3},{3,8},{8,9},{9,10},{10,11},{11,0},{4,5},{5,6},{6... | collective-permute-start | bytes 688136 | tf_op jit(solution)/shard_map/ppermute | solution.py:32
  6.6 8.6 %collective-permute-start.1 = (bf16[128,896]{1,0:T(8,128)(2,1)S(1)}, bf16[128,896]{1,0:T(8,128)(2,1)S(1)}, u32[]{:S(2)}, u32[]{:S(2)}) collective-permute-start(bf16[128,896]{1,0:T(8,128)(2,1)S(1)} %get-tuple-element.23), channel_id=1, source_target_pairs={{0,11},{1,0},{2,1},{3,2},{8,3},{9,8},{10,9},{11,10},{4,15},{5,4},{... | collective-permute-start | bytes 688136 | tf_op jit(solution)/shard_map/ppermute | solution.py:32
  15.2 1.9 %collective-permute-start.2 = (bf16[128,896]{1,0:T(8,128)(2,1)S(1)}, bf16[128,896]{1,0:T(8,128)(2,1)S(1)}, u32[]{:S(2)}, u32[]{:S(2)}) collective-permute-start(bf16[128,896]{1,0:T(8,128)(2,1)S(1)} %get-tuple-element.25), channel_id=1, source_target_pairs={{0,2},{1,11},{2,8},{3,1},{8,10},{9,3},{10,0},{11,9},{4,6},{5,15},{... | collective-permute-start | bytes 688136 | tf_op jit(solution)/shard_map/ppermute | solution.py:32
  17.1 1.7 %collective-permute-done = bf16[128,896]{1,0:T(8,128)(2,1)S(1)} collective-permute-done((bf16[128,896]{1,0:T(8,128)(2,1)S(1)}, bf16[128,896]{1,0:T(8,128)(2,1)S(1)}, u32[]{:S(2)}, u32[]{:S(2)}) %collective-permute-start) | collective-permute-done | bytes 229408 | tf_op jit(solution)/shard_map/ppermute | solution.py:32
  18.9 6.0 %collective-permute-done.1 = bf16[128,896]{1,0:T(8,128)(2,1)S(1)} collective-permute-done((bf16[128,896]{1,0:T(8,128)(2,1)S(1)}, bf16[128,896]{1,0:T(8,128)(2,1)S(1)}, u32[]{:S(2)}, u32[]{:S(2)}) %collective-permute-start.1) | collective-permute-done | bytes 229408 | tf_op jit(solution)/shard_map/ppermute | solution.py:32
  25.0 1.2 collective-permute-done.2
  26.3 1.9 %collective-permute-start.3 = (bf16[512,896]{1,0:T(8,128)(2,1)S(1)}, bf16[512,896]{1,0:T(8,128)(2,1)S(1)}, u32[]{:S(2)}, u32[]{:S(2)}) collective-permute-start(bf16[512,896]{1,0:T(8,128)(2,1)S(1)} %bitcast.29), channel_id=1, source_target_pairs={{0,4},{4,0},{1,5},{5,1},{2,6},{6,2},{3,7},{7,3},{8,12},{12,8},{9,1... | collective-permute-start | bytes 2752520 | tf_op jit(solution)/shard_map/ppermute | solution.py:36
  31.1 1.1 convolution_add_fusion
  32.2 3.9 %all-to-all-start = ((f32[4,32,512]{2,1,0:T(8,128)}), f32[4,32,512]{2,1,0:T(8,128)S(1)}, u32[]{:S(2)}, u32[]{:S(2)}) async-start(f32[4,32,512]{2,1,0:T(8,128)} %bitcast.5), calls=%async_computation | async-start | bytes 524288 | tf_op jit(solution)/shard_map/all_to_all | solution.py:40
  36.2 1.9 %collective-permute-start.4 = (bf16[128,896]{1,0:T(8,128)(2,1)S(1)}, bf16[128,896]{1,0:T(8,128)(2,1)}, u32[]{:S(2)}, u32[]{:S(2)}) collective-permute-start(bf16[128,896]{1,0:T(8,128)(2,1)S(1)} %constant_dynamic-slice_fusion.1), channel_id=1, source_target_pairs={{0,4},{4,0},{1,5},{5,1},{2,6},{6,2},{3,7},{7,3},{8,12},{12,8},{9,1... | collective-permute-start | bytes 688136 | tf_op jit(solution)/shard_map/ppermute | solution.py:36
  38.1 2.4 %collective-permute-start.5 = (f32[64,896]{1,0:T(8,128)}, f32[64,896]{1,0:T(8,128)S(1)}, u32[]{:S(2)}, u32[]{:S(2)}) collective-permute-start(f32[64,896]{1,0:T(8,128)} %constant_dynamic-slice_fusion), channel_id=1, source_target_pairs={{0,4},{4,0},{1,5},{5,1},{2,6},{6,2},{3,7},{7,3},{8,12},{12,8},{9,1... | collective-permute-start | bytes 688136 | tf_op jit(solution)/shard_map/ppermute | solution.py:36
  40.6 1.2 collective-permute-done.5
  41.8 3.6 %all-to-all-done = f32[4,32,512]{2,1,0:T(8,128)S(1)} async-done(((f32[4,32,512]{2,1,0:T(8,128)}), f32[4,32,512]{2,1,0:T(8,128)S(1)}, u32[]{:S(2)}, u32[]{:S(2)}) %all-to-all-start) | async-done | bytes 262176 | tf_op jit(solution)/shard_map/all_to_all | solution.py:40
  47.0 3.3 %all-to-all-start.1 = ((bf16[4,32,640]{2,1,0:T(8,128)(2,1)}), bf16[4,32,640]{2,1,0:T(8,128)(2,1)S(1)}, u32[]{:S(2)}, u32[]{:S(2)}) async-start(bf16[4,32,640]{2,1,0:T(8,128)(2,1)} %broadcast_in_dim.15), calls=%async_computation.1 | async-start | bytes 327680 | tf_op jit(solution)/shard_map/all_to_all | solution.py:40
  50.4 6.0 %all-to-all-done.1 = bf16[4,32,640]{2,1,0:T(8,128)(2,1)S(1)} async-done(((bf16[4,32,640]{2,1,0:T(8,128)(2,1)}), bf16[4,32,640]{2,1,0:T(8,128)(2,1)S(1)}, u32[]{:S(2)}, u32[]{:S(2)}) %all-to-all-start.1) | async-done | bytes 163872 | tf_op jit(solution)/shard_map/all_to_all | solution.py:40
  56.4 1.9 %collective-permute-start.6 = (bf16[128,512]{1,0:T(8,128)(2,1)S(1)}, bf16[128,512]{1,0:T(8,128)(2,1)S(1)}, u32[]{:S(2)}, u32[]{:S(2)}) collective-permute-start(bf16[128,512]{1,0:T(8,128)(2,1)S(1)} %slice.81), channel_id=1, source_target_pairs={{0,4},{4,0},{1,5},{5,1},{2,6},{6,2},{3,7},{7,3},{8,12},{12,8},{9,1... | collective-permute-start | bytes 393224 | tf_op jit(solution)/shard_map/ppermute | solution.py:36
  58.3 1.0 broadcast_select_fusion.1
  59.7 1.4 %convolution_convert_fusion = bf16[512,896]{1,0:T(8,128)(2,1)} fusion(bf16[128,896]{1,0:T(8,128)(2,1)S(1)} %get-tuple-element.27, bf16[128,896]{1,0:T(8,128)(2,1)S(1)} %get-tuple-element.26, bf16[128,512]{1,0:T(8,128)(2,1)S(1)} %get-tuple-element.31, bf16[128,512]{1,0:T(8,128)(2,1)S(1)} %get-tuple-element.30), kind=kOutput, calls=%fused_computation | convolution fusion | flops 236781568 | bytes 1638400 | tf_op jit(solution)/shard_map/dot_general | solution.py:15
  61.0 4.3 %all-to-all-start.2 = ((bf16[4,128,896]{2,1,0:T(8,128)(2,1)}), bf16[4,128,896]{2,1,0:T(8,128)(2,1)S(1)}, u32[]{:S(2)}, u32[]{:S(2)}) async-start(bf16[4,128,896]{2,1,0:T(8,128)(2,1)} %bitcast.38), calls=%async_computation.2 | async-start | bytes 1835008 | tf_op jit(solution)/shard_map/all_to_all | solution.py:40
  65.3 1.1 fusion.8
  66.4 4.9 %collective-permute-start.7 = (bf16[64,896]{1,0:T(8,128)(2,1)S(1)}, bf16[64,896]{1,0:T(8,128)(2,1)S(1)}, u32[]{:S(2)}, u32[]{:S(2)}) collective-permute-start(bf16[64,896]{1,0:T(8,128)(2,1)S(1)} %fusion.8), channel_id=1, source_target_pairs={{0,8},{8,0},{1,9},{9,1},{2,10},{10,2},{3,11},{11,3},{4,12},{12,4},... | collective-permute-start | bytes 344072 | tf_op jit(solution)/shard_map/ppermute | solution.py:36
  71.5 8.2 %collective-permute-done.7 = bf16[64,896]{1,0:T(8,128)(2,1)S(1)} collective-permute-done((bf16[64,896]{1,0:T(8,128)(2,1)S(1)}, bf16[64,896]{1,0:T(8,128)(2,1)S(1)}, u32[]{:S(2)}, u32[]{:S(2)}) %collective-permute-start.7) | collective-permute-done | bytes 114720 | tf_op jit(solution)/shard_map/ppermute | solution.py:36
  79.7 1.1 fusion.7
  80.8 1.1 maximum_reduce_fusion
  81.9 7.4 %all-to-all-start.3 = ((bf16[8,24,896]{2,1,0:T(8,128)(2,1)}), bf16[8,24,896]{2,1,0:T(8,128)(2,1)S(1)}, u32[]{:S(2)}, u32[]{:S(2)}) async-start(bf16[8,24,896]{2,1,0:T(8,128)(2,1)} %maximum_reduce_fusion), calls=%async_computation.3 | async-start | bytes 688128 | tf_op jit(solution)/shard_map/all_to_all | solution.py:40
  89.6 8.6 %all-to-all-done.3 = bf16[8,24,896]{2,1,0:T(8,128)(2,1)S(1)} async-done(((bf16[8,24,896]{2,1,0:T(8,128)(2,1)}), bf16[8,24,896]{2,1,0:T(8,128)(2,1)S(1)}, u32[]{:S(2)}, u32[]{:S(2)}) %all-to-all-start.3) | async-done | bytes 344096 | tf_op jit(solution)/shard_map/all_to_all | solution.py:40
  98.4 8.8 %collective-permute-start.9 = (bf16[16,896]{1,0:T(8,128)(2,1)S(1)}, bf16[16,896]{1,0:T(8,128)(2,1)S(1)}, u32[]{:S(2)}, u32[]{:S(2)}) collective-permute-start(bf16[16,896]{1,0:T(8,128)(2,1)S(1)} %slice.82), channel_id=1, source_target_pairs={{0,8},{1,136},{2,264},{3,392},{4,72},{5,200},{6,328},{7,456},{8,0}... | collective-permute-start | bytes 86024 | tf_op jit(solution)/shard_map/ppermute | solution.py:153
  107.2 1.9 %collective-permute-start.8 = (bf16[16,896]{1,0:T(8,128)(2,1)S(1)}, bf16[16,896]{1,0:T(8,128)(2,1)S(1)}, u32[]{:S(2)}, u32[]{:S(2)}) collective-permute-start(bf16[16,896]{1,0:T(8,128)(2,1)S(1)} %slice.82), channel_id=1, source_target_pairs={{0,0},{1,128},{2,256},{3,384},{4,64},{5,192},{6,320},{7,448},{8,8}... | collective-permute-start | bytes 86024 | tf_op jit(solution)/shard_map/ppermute | solution.py:153
  109.6 5.2 %collective-permute-done.8 = bf16[16,896]{1,0:T(8,128)(2,1)S(1)} collective-permute-done((bf16[16,896]{1,0:T(8,128)(2,1)S(1)}, bf16[16,896]{1,0:T(8,128)(2,1)S(1)}, u32[]{:S(2)}, u32[]{:S(2)}) %collective-permute-start.8) | collective-permute-done | bytes 28704 | tf_op jit(solution)/shard_map/ppermute | solution.py:153
  115.5 4.5 %all-to-all-start.4 = ((bf16[8,24,896]{2,1,0:T(8,128)(2,1)}), bf16[8,24,896]{2,1,0:T(8,128)(2,1)S(1)}, u32[]{:S(2)}, u32[]{:S(2)}) async-start(bf16[8,24,896]{2,1,0:T(8,128)(2,1)} %broadcast_in_dim.16), calls=%async_computation.4 | async-start | bytes 688128 | tf_op jit(solution)/shard_map/all_to_all | solution.py:40
  121.4 7.1 %all-to-all-done.4 = bf16[8,24,896]{2,1,0:T(8,128)(2,1)S(1)} async-done(((bf16[8,24,896]{2,1,0:T(8,128)(2,1)}), bf16[8,24,896]{2,1,0:T(8,128)(2,1)S(1)}, u32[]{:S(2)}, u32[]{:S(2)}) %all-to-all-start.4) | async-done | bytes 344096 | tf_op jit(solution)/shard_map/all_to_all | solution.py:40
  (68 shorter events, 9.6 us)
Async XLA Ops:
  0.6 27.6 %copy-start = (bf16[128,1792]{1,0:T(8,128)(2,1)S(1)}, bf16[128,1792]{1,0:T(8,128)(2,1)}, u32[]{:S(2)}) copy-start(bf16[128,1792]{1,0:T(8,128)(2,1)} %param.8) | copy-start | bytes 1376260
  2.1 26.1 %copy-start.2 = (bf16[128,1792]{1,0:T(8,128)(2,1)S(1)}, bf16[128,1792]{1,0:T(8,128)(2,1)}, u32[]{:S(2)}) copy-start(bf16[128,1792]{1,0:T(8,128)(2,1)} %param.7) | copy-start | bytes 1376260
  2.1 26.2 %copy-start.7 = (s32[128]{0:T(128)S(1)}, s32[128]{0:T(128)}, u32[]{:S(2)}) copy-start(s32[128]{0:T(128)} %param.13) | copy-start | bytes 1540
  2.1 16.7 %collective-permute-start = (bf16[128,896]{1,0:T(8,128)(2,1)S(1)}, bf16[128,896]{1,0:T(8,128)(2,1)S(1)}, u32[]{:S(2)}, u32[]{:S(2)}) collective-permute-start(bf16[128,896]{1,0:T(8,128)(2,1)S(1)} %get-tuple-element.24), channel_id=1, source_target_pairs={{0,1},{1,2},{2,3},{3,8},{8,9},{9,10},{10,11},{11,0},{4,5},{5,6},{6... | collective-permute-start | bytes 688136 | tf_op jit(solution)/shard_map/ppermute | solution.py:32
  6.6 18.4 %collective-permute-start.1 = (bf16[128,896]{1,0:T(8,128)(2,1)S(1)}, bf16[128,896]{1,0:T(8,128)(2,1)S(1)}, u32[]{:S(2)}, u32[]{:S(2)}) collective-permute-start(bf16[128,896]{1,0:T(8,128)(2,1)S(1)} %get-tuple-element.23), channel_id=1, source_target_pairs={{0,11},{1,0},{2,1},{3,2},{8,3},{9,8},{10,9},{11,10},{4,15},{5,4},{... | collective-permute-start | bytes 688136 | tf_op jit(solution)/shard_map/ppermute | solution.py:32
  15.2 11.1 %collective-permute-start.2 = (bf16[128,896]{1,0:T(8,128)(2,1)S(1)}, bf16[128,896]{1,0:T(8,128)(2,1)S(1)}, u32[]{:S(2)}, u32[]{:S(2)}) collective-permute-start(bf16[128,896]{1,0:T(8,128)(2,1)S(1)} %get-tuple-element.25), channel_id=1, source_target_pairs={{0,2},{1,11},{2,8},{3,1},{8,10},{9,3},{10,0},{11,9},{4,6},{5,15},{... | collective-permute-start | bytes 688136 | tf_op jit(solution)/shard_map/ppermute | solution.py:32
  26.3 4.4 %collective-permute-start.3 = (bf16[512,896]{1,0:T(8,128)(2,1)S(1)}, bf16[512,896]{1,0:T(8,128)(2,1)S(1)}, u32[]{:S(2)}, u32[]{:S(2)}) collective-permute-start(bf16[512,896]{1,0:T(8,128)(2,1)S(1)} %bitcast.29), channel_id=1, source_target_pairs={{0,4},{4,0},{1,5},{5,1},{2,6},{6,2},{3,7},{7,3},{8,12},{12,8},{9,1... | collective-permute-start | bytes 2752520 | tf_op jit(solution)/shard_map/ppermute | solution.py:36
  28.6 0.8 copy-start.1
  30.1 10.4 %copy-start.6 = (s32[128]{0:T(128)S(1)}, s32[128]{0:T(128)}, u32[]{:S(2)}) copy-start(s32[128]{0:T(128)} %param.12) | copy-start | bytes 1540
  30.1 15.4 %copy-start.4 = (f32[128]{0:T(128)S(1)}, f32[128]{0:T(128)}, u32[]{:S(2)}) copy-start(f32[128]{0:T(128)} %param.10) | copy-start | bytes 1540
  30.1 15.4 %copy-start.5 = (f32[128]{0:T(128)S(1)}, f32[128]{0:T(128)}, u32[]{:S(2)}) copy-start(f32[128]{0:T(128)} %param.11) | copy-start | bytes 1540
  32.2 13.2 %all-to-all-start = ((f32[4,32,512]{2,1,0:T(8,128)}), f32[4,32,512]{2,1,0:T(8,128)S(1)}, u32[]{:S(2)}, u32[]{:S(2)}) async-start(f32[4,32,512]{2,1,0:T(8,128)} %bitcast.5), calls=%async_computation | async-start | bytes 524288 | tf_op jit(solution)/shard_map/all_to_all | solution.py:40
  36.2 4.4 %collective-permute-start.4 = (bf16[128,896]{1,0:T(8,128)(2,1)S(1)}, bf16[128,896]{1,0:T(8,128)(2,1)}, u32[]{:S(2)}, u32[]{:S(2)}) collective-permute-start(bf16[128,896]{1,0:T(8,128)(2,1)S(1)} %constant_dynamic-slice_fusion.1), channel_id=1, source_target_pairs={{0,4},{4,0},{1,5},{5,1},{2,6},{6,2},{3,7},{7,3},{8,12},{12,8},{9,1... | collective-permute-start | bytes 688136 | tf_op jit(solution)/shard_map/ppermute | solution.py:36
  38.1 3.7 %collective-permute-start.5 = (f32[64,896]{1,0:T(8,128)}, f32[64,896]{1,0:T(8,128)S(1)}, u32[]{:S(2)}, u32[]{:S(2)}) collective-permute-start(f32[64,896]{1,0:T(8,128)} %constant_dynamic-slice_fusion), channel_id=1, source_target_pairs={{0,4},{4,0},{1,5},{5,1},{2,6},{6,2},{3,7},{7,3},{8,12},{12,8},{9,1... | collective-permute-start | bytes 688136 | tf_op jit(solution)/shard_map/ppermute | solution.py:36
  41.8 19.2 %copy-start.3 = (f32[64,896]{1,0:T(8,128)}, f32[64,896]{1,0:T(8,128)S(1)}, u32[]{:S(2)}) copy-start(f32[64,896]{1,0:T(8,128)S(1)} %collective-permute-done.5) | copy-start | bytes 688132
  47.0 9.3 %all-to-all-start.1 = ((bf16[4,32,640]{2,1,0:T(8,128)(2,1)}), bf16[4,32,640]{2,1,0:T(8,128)(2,1)S(1)}, u32[]{:S(2)}, u32[]{:S(2)}) async-start(bf16[4,32,640]{2,1,0:T(8,128)(2,1)} %broadcast_in_dim.15), calls=%async_computation.1 | async-start | bytes 327680 | tf_op jit(solution)/shard_map/all_to_all | solution.py:40
  56.4 3.2 %collective-permute-start.6 = (bf16[128,512]{1,0:T(8,128)(2,1)S(1)}, bf16[128,512]{1,0:T(8,128)(2,1)S(1)}, u32[]{:S(2)}, u32[]{:S(2)}) collective-permute-start(bf16[128,512]{1,0:T(8,128)(2,1)S(1)} %slice.81), channel_id=1, source_target_pairs={{0,4},{4,0},{1,5},{5,1},{2,6},{6,2},{3,7},{7,3},{8,12},{12,8},{9,1... | collective-permute-start | bytes 393224 | tf_op jit(solution)/shard_map/ppermute | solution.py:36
  61.0 19.8 %all-to-all-start.2 = ((bf16[4,128,896]{2,1,0:T(8,128)(2,1)}), bf16[4,128,896]{2,1,0:T(8,128)(2,1)S(1)}, u32[]{:S(2)}, u32[]{:S(2)}) async-start(bf16[4,128,896]{2,1,0:T(8,128)(2,1)} %bitcast.38), calls=%async_computation.2 | async-start | bytes 1835008 | tf_op jit(solution)/shard_map/all_to_all | solution.py:40
  66.4 13.3 %collective-permute-start.7 = (bf16[64,896]{1,0:T(8,128)(2,1)S(1)}, bf16[64,896]{1,0:T(8,128)(2,1)S(1)}, u32[]{:S(2)}, u32[]{:S(2)}) collective-permute-start(bf16[64,896]{1,0:T(8,128)(2,1)S(1)} %fusion.8), channel_id=1, source_target_pairs={{0,8},{8,0},{1,9},{9,1},{2,10},{10,2},{3,11},{11,3},{4,12},{12,4},... | collective-permute-start | bytes 344072 | tf_op jit(solution)/shard_map/ppermute | solution.py:36
  81.9 16.4 %all-to-all-start.3 = ((bf16[8,24,896]{2,1,0:T(8,128)(2,1)}), bf16[8,24,896]{2,1,0:T(8,128)(2,1)S(1)}, u32[]{:S(2)}, u32[]{:S(2)}) async-start(bf16[8,24,896]{2,1,0:T(8,128)(2,1)} %maximum_reduce_fusion), calls=%async_computation.3 | async-start | bytes 688128 | tf_op jit(solution)/shard_map/all_to_all | solution.py:40
  98.4 11.2 %collective-permute-start.9 = (bf16[16,896]{1,0:T(8,128)(2,1)S(1)}, bf16[16,896]{1,0:T(8,128)(2,1)S(1)}, u32[]{:S(2)}, u32[]{:S(2)}) collective-permute-start(bf16[16,896]{1,0:T(8,128)(2,1)S(1)} %slice.82), channel_id=1, source_target_pairs={{0,8},{1,136},{2,264},{3,392},{4,72},{5,200},{6,328},{7,456},{8,0}... | collective-permute-start | bytes 86024 | tf_op jit(solution)/shard_map/ppermute | solution.py:153
  107.2 7.6 %collective-permute-start.8 = (bf16[16,896]{1,0:T(8,128)(2,1)S(1)}, bf16[16,896]{1,0:T(8,128)(2,1)S(1)}, u32[]{:S(2)}, u32[]{:S(2)}) collective-permute-start(bf16[16,896]{1,0:T(8,128)(2,1)S(1)} %slice.82), channel_id=1, source_target_pairs={{0,0},{1,128},{2,256},{3,384},{4,64},{5,192},{6,320},{7,448},{8,8}... | collective-permute-start | bytes 86024 | tf_op jit(solution)/shard_map/ppermute | solution.py:153
  115.5 12.9 %all-to-all-start.4 = ((bf16[8,24,896]{2,1,0:T(8,128)(2,1)}), bf16[8,24,896]{2,1,0:T(8,128)(2,1)S(1)}, u32[]{:S(2)}, u32[]{:S(2)}) async-start(bf16[8,24,896]{2,1,0:T(8,128)(2,1)} %broadcast_in_dim.16), calls=%async_computation.4 | async-start | bytes 688128 | tf_op jit(solution)/shard_map/all_to_all | solution.py:40

commit v6 on v5

--- a/solution.py
+++ b/solution.py
@@ -102,22 +102,28 @@
     vocab = 4 * head.shape[0]
     replicas = lax.axis_size("dp")
 
+    onehot = (embed_ids[:, None] == lax.broadcasted_iota(jnp.int32, (1, 8 * replicas), 1)).astype(BF16)
+    embed = dot(onehot, embed_cot, ((0,), (0,)))
+    taken = (swap(half_of(final_normed, 1 - core), "core"), swap(half_of(embed, 1 - core), "core"))
+
     mine = window_half(head, core, rank)
+    mine, taken = lax.optimization_barrier((mine, taken))
     other = swap(mine, "core")
     logits = dot(half_of(final_normed, core), mine, ((1,), (1,))) + dot(
         half_of(final_normed, 1 - core), other, ((1,), (1,))
     )
-
-    onehot = (embed_ids[:, None] == lax.broadcasted_iota(jnp.int32, (1, 8 * replicas), 1)).astype(BF16)
-    embed = dot(onehot, embed_cot, ((0,), (0,)))
-    given = (half_of(final_normed, 1 - core), half_of(embed, 1 - core))
-    logits, given = lax.optimization_barrier((logits, given))
-    logits = exchange(logits.reshape(4, part, vocab), "tensor")
-    taken = (swap(given[0], "core"), swap(given[1], "core"))
-    logits, taken = lax.optimization_barrier((logits, taken))
-    logits = logits.sum(0)
     normed = by_core(half_of(final_normed, core), taken[0], core)
     embed = half_of(embed, core) + taken[1]
+
+    def from_x(value, ahead):
+        return lax.ppermute(value, "x", [((i + ahead) % 4, i) for i in range(4)])
+
+    far = from_x(normed, 2)
+    logits, own = lax.optimization_barrier((logits, normed))
+    logits = exchange(logits.reshape(4, part, vocab), "tensor")
+    after, before = from_x(own, 1), from_x(own, 3)
+    logits, far = lax.optimization_barrier((logits, far))
+    logits = logits.sum(0)
 
     def own_part(value):
         pieces = [value[i * part : (i + 1) * part] for i in range(4)]
@@ -137,23 +143,36 @@
     extra = jnp.concatenate(three_parts(loss) + (jnp.zeros((part, LANES - 3), F32),), 1)
     sent = jnp.concatenate((dlogits, extra), 1).astype(BF16)
 
-    gathered = spread(sent, "tensor").reshape(tokens, vocab + LANES)
+    quarters = jnp.stack([sent[:, i * LANES : (i + 1) * LANES] for i in range(4)])
+    quarters = jnp.broadcast_to(quarters[:, None], (4, 8, part, LANES)).reshape(32, part, LANES)
+    def joined(value, step):
+        other = lax.ppermute(value, "tensor", [(i, i ^ step) for i in range(4)])
+        first = (rank & step) == 0
+        return jnp.concatenate((jnp.where(first, value, other), jnp.where(first, other, value)), 0)
+
+    quarters, sent = lax.optimization_barrier((quarters, sent))
+    quarter = exchange(quarters, GROUP + ("tensor",)).reshape(4, 2 * tokens, LANES)
+    sent = joined(sent, 1)
+    normed = jnp.concatenate((own, after, far, before), 0)
+    quarter, normed, sent = lax.optimization_barrier((quarter, normed, sent))
+    quarter = lax.dynamic_slice_in_dim(jnp.concatenate((quarter, quarter[:3]), 0), lax.axis_index("x"), 4, 0)
+    term = dot(quarter.reshape(8 * tokens, LANES), normed, ((0,), (0,))).astype(BF16)
+    embed = embed.astype(BF16)
+    term = jnp.concatenate((term.reshape(replicas, 16, half), embed.reshape(replicas, 8, half)), 1)
+    term, sent = lax.optimization_barrier((term, sent))
+    term = exchange(term, "dp")
+    gathered = joined(sent, 2)
+    term, gathered = lax.optimization_barrier((term, gathered))
+    term = term.astype(F32).sum(0)
     dlogits = gathered[:, :vocab]
     token_loss = jnp.sum(gathered[:, vocab : vocab + 3].astype(F32), axis=1)
 
-    term = by_core(dlogits, swap(dlogits, "core"), core)
-    term = dot(term, normed, ((0,), (0,))).astype(BF16).reshape(4, vocab // 4, half)
-    term = exchange(term, "x").reshape(4, replicas, 16, half)
-    embed = (embed + swap(embed.astype(BF16), "zhi").astype(F32)).astype(BF16)
-    embed = jnp.stack([embed.reshape(replicas, 8, half)] + [jnp.zeros((replicas, 8, half), BF16)] * 3)
-    term = jnp.concatenate((term, embed), 2).astype(F32).sum(0).astype(BF16)
-    term = exchange(term, "dp").astype(F32).sum(0).astype(BF16)
-
-    block = term[:16]
+    block, embed = term[:16].astype(BF16), term[16:]
     moved = lax.ppermute(block, EVERY, owner(0)).astype(F32) + lax.ppermute(
         block, EVERY, owner(1)
     ).astype(F32)
-    pieces = spread(jnp.concatenate((moved.astype(BF16), term[16:]), 0), GROUP).astype(F32)
+    embed = embed + swap(embed.astype(BF16), "zhi").astype(F32)
+    pieces = spread(jnp.concatenate((moved, embed), 0).astype(BF16), GROUP).astype(F32)
     head_grad = pieces[:, :16].reshape(vocab // 4, half)
     embed_grad = pieces[:, 16:].reshape(4, 2, 8, half).sum(0)
     embed_grad = jnp.concatenate((embed_grad[0], embed_grad[1]), 1)

time: 131 us -> 124 us (0.947)
  the two profiles are of different devices: /device:TPU:16 before, /device:TPU:128 now
where the time goes in v6:
time: 124 us; the launch traced here: 123 us
  starting transfers between devices  78.6 us (63%)
  waiting for transfers between devices  23.6 us (19%)
  local copies, waits for them, and re-layouts  8.6 us (7%)
  other arithmetic  7.97 us (6%)
  matrix products  2.98 us (2%)
  between operations  1.39 us (1%)
    all_to_all x4, starting transfers between devices, exchange(): return lax.all_to_all(value, axes, 0, 0)  21.5 us
    ppermute x3, starting transfers between devices, shift(): lax.ppermute(value, RING, [(i, step(i) % count) for i in range(count)])  14.3 us
    all_to_all x4, waiting for transfers between devices, exchange(): return lax.all_to_all(value, axes, 0, 0)  13.8 us
    ppermute x3, starting transfers between devices, from_x(): return lax.ppermute(value, 'x', [((i + ahead) % 4, i) for i in range(4)])  12.1 us
    ppermute x4, starting transfers between devices, swap(): return lax.ppermute(value, axis, [(0, 1), (1, 0)])  11 us
    ppermute x1, starting transfers between devices, shards(): lax.ppermute(block, EVERY, owner(0)).astype(F32)  7.54 us
    ppermute x2, starting transfers between devices, joined(): other = lax.ppermute(value, 'tensor', [(i, i ^ step) for i in range(4)])  7.47 us
    ppermute x2, waiting for transfers between devices, joined(): other = lax.ppermute(value, 'tensor', [(i, i ^ step) for i in range(4)])  5.77 us
  transfers between devices with their start and end apart: 18, of which 5 were waited for; matrix products, arithmetic and copies ran while one was open for 10% of the time, Pallas kernels for 0%

profile of v6, /device:TPU:128, one launch (start us, length us, event | category | flops | bytes accessed | tf_op | source)
XLA Modules:
  0.0 123.1 jit_solution(5194301987336846909)
XLA Ops:
  0.7 2.2 %constant_dynamic-slice_fusion.2 = (bf16[128,896]{1,0:T(8,128)(2,1)S(1)}, bf16[128,896]{1,0:T(8,128)(2,1)}, bf16[128,896]{1,0:T(8,128)(2,1)S(1)}, bf16[128,896]{1,0:T(8,128)(2,1)}) fusion(bf16[128,7168]{1,0:T(8,128)(2,1)} %param.9, s32[]{:T(128)S(6)} %select_n.225, s32[]{:T(128)S(6)} %select_n.219, s32[]{:T(128)S(6)} %select_n.216, s32[]{:T(128)S(6)} %select_n.222), kind=kLoop, calls=%fused_computation.62 | loop fusion | bytes 1835024 | tf_op jit(solution)/shard_map/dynamic_slice | solution.py:60
  2.9 4.3 %collective-permute-start = (bf16[128,896]{1,0:T(8,128)(2,1)S(1)}, bf16[128,896]{1,0:T(8,128)(2,1)S(1)}, u32[]{:S(2)}, u32[]{:S(2)}) collective-permute-start(bf16[128,896]{1,0:T(8,128)(2,1)S(1)} %get-tuple-element.44), channel_id=1, source_target_pairs={{0,1},{1,2},{2,3},{3,8},{8,9},{9,10},{10,11},{11,0},{4,5},{5,6},{6... | collective-permute-start | bytes 688136 | tf_op jit(solution)/shard_map/ppermute | solution.py:32
  7.2 1.9 %collective-permute-start.1 = (bf16[128,896]{1,0:T(8,128)(2,1)}, bf16[128,896]{1,0:T(8,128)(2,1)S(1)}, u32[]{:S(2)}, u32[]{:S(2)}) collective-permute-start(bf16[128,896]{1,0:T(8,128)(2,1)} %get-tuple-element.43), channel_id=1, source_target_pairs={{0,11},{1,0},{2,1},{3,2},{8,3},{9,8},{10,9},{11,10},{4,15},{5,4},{... | collective-permute-start | bytes 688136 | tf_op jit(solution)/shard_map/ppermute | solution.py:32
  9.2 8.2 %collective-permute-start.2 = (bf16[128,896]{1,0:T(8,128)(2,1)}, bf16[128,896]{1,0:T(8,128)(2,1)S(1)}, u32[]{:S(2)}, u32[]{:S(2)}) collective-permute-start(bf16[128,896]{1,0:T(8,128)(2,1)} %get-tuple-element.45), channel_id=1, source_target_pairs={{0,2},{1,11},{2,8},{3,1},{8,10},{9,3},{10,0},{11,9},{4,6},{5,15},{... | collective-permute-start | bytes 688136 | tf_op jit(solution)/shard_map/ppermute | solution.py:32
  17.4 1.9 %collective-permute-start.3 = (bf16[128,896]{1,0:T(8,128)(2,1)S(1)}, bf16[128,896]{1,0:T(8,128)(2,1)S(1)}, u32[]{:S(2)}, u32[]{:S(2)}) collective-permute-start(bf16[128,896]{1,0:T(8,128)(2,1)S(1)} %constant_dynamic-slice_fusion.1), channel_id=1, source_target_pairs={{0,4},{4,0},{1,5},{5,1},{2,6},{6,2},{3,7},{7,3},{8,12},{12,8},{9,1... | collective-permute-start | bytes 688136 | tf_op jit(solution)/shard_map/ppermute | solution.py:36
  20.4 2.4 %collective-permute-start.4 = (f32[64,896]{1,0:T(8,128)}, f32[64,896]{1,0:T(8,128)}, u32[]{:S(2)}, u32[]{:S(2)}) collective-permute-start(f32[64,896]{1,0:T(8,128)} %constant_dynamic-slice_fusion), channel_id=1, source_target_pairs={{0,4},{4,0},{1,5},{5,1},{2,6},{6,2},{3,7},{7,3},{8,12},{12,8},{9,1... | collective-permute-start | bytes 688136 | tf_op jit(solution)/shard_map/ppermute | solution.py:36
  23.6 1.0 constant_dynamic-update-slice_fusion.3
  25.4 1.9 %collective-permute-start.5 = (bf16[512,896]{1,0:T(8,128)(2,1)S(1)}, bf16[512,896]{1,0:T(8,128)(2,1)S(1)}, u32[]{:S(2)}, u32[]{:S(2)}) collective-permute-start(bf16[512,896]{1,0:T(8,128)(2,1)S(1)} %bitcast.40), channel_id=1, source_target_pairs={{0,4},{4,0},{1,5},{5,1},{2,6},{6,2},{3,7},{7,3},{8,12},{12,8},{9,1... | collective-permute-start | bytes 2752520 | tf_op jit(solution)/shard_map/ppermute | solution.py:36
  27.3 1.1 broadcast_select_fusion.3
  28.5 5.1 %collective-permute-start.6 = (bf16[256,896]{1,0:T(8,128)(2,1)S(1)}, bf16[256,896]{1,0:T(8,128)(2,1)}, u32[]{:S(2)}, u32[]{:S(2)}) collective-permute-start(bf16[256,896]{1,0:T(8,128)(2,1)S(1)} %pad_maximum_fusion.1), channel_id=1, source_target_pairs={{32,0},{48,16},{0,32},{16,48},{33,1},{49,17},{1,33},{17,49},{34,2}... | collective-permute-start | bytes 1376264 | tf_op jit(solution)/shard_map/ppermute | solution.py:119
  34.0 1.1 convolution_add_fusion
  35.2 5.2 %all-to-all-start = ((f32[4,32,512]{2,1,0:T(8,128)}), f32[4,32,512]{2,1,0:T(8,128)S(1)}, u32[]{:S(2)}, u32[]{:S(2)}) async-start(f32[4,32,512]{2,1,0:T(8,128)} %bitcast.46), calls=%async_computation | async-start | bytes 524288 | tf_op jit(solution)/shard_map/all_to_all | solution.py:40
  40.5 2.5 %collective-permute-start.8 = (bf16[256,896]{1,0:T(8,128)(2,1)S(1)}, bf16[256,896]{1,0:T(8,128)(2,1)}, u32[]{:S(2)}, u32[]{:S(2)}) collective-permute-start(bf16[256,896]{1,0:T(8,128)(2,1)S(1)} %pad_maximum_fusion.1), channel_id=1, source_target_pairs={{48,0},{0,16},{16,32},{32,48},{49,1},{1,17},{17,33},{33,49},{50,2}... | collective-permute-start | bytes 1376264 | tf_op jit(solution)/shard_map/ppermute | solution.py:119
  43.0 4.5 %collective-permute-start.7 = (bf16[256,896]{1,0:T(8,128)(2,1)S(1)}, bf16[256,896]{1,0:T(8,128)(2,1)}, u32[]{:S(2)}, u32[]{:S(2)}) collective-permute-start(bf16[256,896]{1,0:T(8,128)(2,1)S(1)} %pad_maximum_fusion.1), channel_id=1, source_target_pairs={{16,0},{32,16},{48,32},{0,48},{17,1},{33,17},{49,33},{1,49},{18,2}... | collective-permute-start | bytes 1376264 | tf_op jit(solution)/shard_map/ppermute | solution.py:119
  49.4 5.7 %all-to-all-start.1 = ((bf16[32,32,128]{2,1,0:T(8,128)(2,1)}), bf16[32,32,128]{2,1,0:T(8,128)(2,1)S(1)}, u32[]{:S(2)}, u32[]{:S(2)}) async-start(bf16[32,32,128]{2,1,0:T(8,128)(2,1)} %bitcast.10), calls=%async_computation.1 | async-start | bytes 524288 | tf_op jit(solution)/shard_map/all_to_all | solution.py:40
  55.1 3.4 %collective-permute-start.9 = (bf16[32,640]{1,0:T(8,128)(2,1)S(1)}, bf16[32,640]{1,0:T(8,128)(2,1)S(1)}, u32[]{:S(2)}, u32[]{:S(2)}) collective-permute-start(bf16[32,640]{1,0:T(8,128)(2,1)S(1)} %concatenate.37), channel_id=1, source_target_pairs={{0,1},{1,0},{2,3},{3,2},{4,5},{5,4},{6,7},{7,6},{8,9},{9,8},{10,11... | collective-permute-start | bytes 122888 | tf_op jit(solution)/shard_map/ppermute | solution.py:149
  58.5 1.6 %fusion.4 = bf16[8,8,896]{2,1,0:T(8,128)(2,1)} fusion(f32[64,896]{1,0:T(8,128)} %collective-permute-done.4, f32[64,1792]{1,0:T(8,128)S(1)} %fusion.9, s32[]{:T(128)S(6)} %select_n.214), kind=kLoop, calls=%fused_computation.21 | loop fusion | flops 114688 | bytes 573444 | tf_op jit(solution)/shard_map/reshape | solution.py:161
  60.1 2.7 %collective-permute-done.9 = bf16[32,640]{1,0:T(8,128)(2,1)S(1)} collective-permute-done((bf16[32,640]{1,0:T(8,128)(2,1)S(1)}, bf16[32,640]{1,0:T(8,128)(2,1)S(1)}, u32[]{:S(2)}, u32[]{:S(2)}) %collective-permute-start.9) | collective-permute-done | bytes 40992 | tf_op jit(solution)/shard_map/ppermute | solution.py:149
  62.8 1.6 %pad_maximum_fusion = bf16[1024,896]{1,0:T(8,128)(2,1)S(1)} fusion(bf16[256,896]{1,0:T(8,128)(2,1)} %collective-permute-done.8, bf16[256,896]{1,0:T(8,128)(2,1)} %collective-permute-done.6, bf16[256,896]{1,0:T(8,128)(2,1)} %collective-permute-done.7, bf16[256,896]{1,0:T(8,128)(2,1)} %copy-done.3), kind=kLoop, calls=%fused_computation | loop fusion | flops 7340032 | bytes 3670016 | tf_op jit(solution)/shard_map/concatenate | solution.py:156
  65.3 0.8 pad_maximum_fusion.3
  66.0 7.1 %all-to-all-start.2 = ((bf16[8,24,896]{2,1,0:T(8,128)(2,1)}), bf16[8,24,896]{2,1,0:T(8,128)(2,1)S(1)}, u32[]{:S(2)}, u32[]{:S(2)}) async-start(bf16[8,24,896]{2,1,0:T(8,128)(2,1)} %pad_maximum_fusion.3), calls=%async_computation.2 | async-start | bytes 688128 | tf_op jit(solution)/shard_map/all_to_all | solution.py:40
  73.1 4.1 %collective-permute-start.10 = (bf16[64,640]{1,0:T(8,128)(2,1)S(1)}, bf16[64,640]{1,0:T(8,128)(2,1)S(1)}, u32[]{:S(2)}, u32[]{:S(2)}) collective-permute-start(bf16[64,640]{1,0:T(8,128)(2,1)S(1)} %pad_maximum_fusion.5), channel_id=1, source_target_pairs={{0,2},{1,3},{2,0},{3,1},{4,6},{5,7},{6,4},{7,5},{8,10},{9,11},{10,... | collective-permute-start | bytes 245768 | tf_op jit(solution)/shard_map/ppermute | solution.py:149
  77.2 3.1 %collective-permute-done.10 = bf16[64,640]{1,0:T(8,128)(2,1)S(1)} collective-permute-done((bf16[64,640]{1,0:T(8,128)(2,1)S(1)}, bf16[64,640]{1,0:T(8,128)(2,1)S(1)}, u32[]{:S(2)}, u32[]{:S(2)}) %collective-permute-start.10) | collective-permute-done | bytes 81952 | tf_op jit(solution)/shard_map/ppermute | solution.py:149
  80.4 6.7 %all-to-all-done.2 = bf16[8,24,896]{2,1,0:T(8,128)(2,1)S(1)} async-done(((bf16[8,24,896]{2,1,0:T(8,128)(2,1)}), bf16[8,24,896]{2,1,0:T(8,128)(2,1)S(1)}, u32[]{:S(2)}, u32[]{:S(2)}) %all-to-all-start.2) | async-done | bytes 344096 | tf_op jit(solution)/shard_map/all_to_all | solution.py:40
  87.2 4.7 %collective-permute-start.12 = (bf16[16,896]{1,0:T(8,128)(2,1)S(1)}, bf16[16,896]{1,0:T(8,128)(2,1)S(1)}, u32[]{:S(2)}, u32[]{:S(2)}) collective-permute-start(bf16[16,896]{1,0:T(8,128)(2,1)S(1)} %slice.140), channel_id=1, source_target_pairs={{0,8},{1,136},{2,264},{3,392},{4,72},{5,200},{6,328},{7,456},{8,0}... | collective-permute-start | bytes 86024 | tf_op jit(solution)/shard_map/ppermute | solution.py:171
  91.9 7.5 %collective-permute-start.11 = (bf16[16,896]{1,0:T(8,128)(2,1)S(1)}, bf16[16,896]{1,0:T(8,128)(2,1)S(1)}, u32[]{:S(2)}, u32[]{:S(2)}) collective-permute-start(bf16[16,896]{1,0:T(8,128)(2,1)S(1)} %slice.140), channel_id=1, source_target_pairs={{0,0},{1,128},{2,256},{3,384},{4,64},{5,192},{6,320},{7,448},{8,8}... | collective-permute-start | bytes 86024 | tf_op jit(solution)/shard_map/ppermute | solution.py:171
  99.4 4.8 %collective-permute-start.13 = (bf16[8,896]{1,0:T(8,128)(2,1)S(1)}, bf16[8,896]{1,0:T(8,128)(2,1)S(1)}, u32[]{:S(2)}, u32[]{:S(2)}) collective-permute-start(bf16[8,896]{1,0:T(8,128)(2,1)S(1)} %slice.141), channel_id=1, source_target_pairs={{0,8},{8,0},{1,9},{9,1},{2,10},{10,2},{3,11},{11,3},{4,12},{12,4},... | collective-permute-start | bytes 43016 | tf_op jit(solution)/shard_map/ppermute | solution.py:36
  105.0 4.0 %collective-permute-done.13 = bf16[8,896]{1,0:T(8,128)(2,1)S(1)} collective-permute-done((bf16[8,896]{1,0:T(8,128)(2,1)S(1)}, bf16[8,896]{1,0:T(8,128)(2,1)S(1)}, u32[]{:S(2)}, u32[]{:S(2)}) %collective-permute-start.13) | collective-permute-done | bytes 14368 | tf_op jit(solution)/shard_map/ppermute | solution.py:36
  109.8 3.5 %all-to-all-start.3 = ((bf16[8,24,896]{2,1,0:T(8,128)(2,1)}), bf16[8,24,896]{2,1,0:T(8,128)(2,1)S(1)}, u32[]{:S(2)}, u32[]{:S(2)}) async-start(bf16[8,24,896]{2,1,0:T(8,128)(2,1)} %broadcast_in_dim.16), calls=%async_computation.3 | async-start | bytes 688128 | tf_op jit(solution)/shard_map/all_to_all | solution.py:40
  113.8 0.8 pad_maximum_fusion.2
  114.6 7.1 %all-to-all-done.3 = bf16[8,24,896]{2,1,0:T(8,128)(2,1)S(1)} async-done(((bf16[8,24,896]{2,1,0:T(8,128)(2,1)}), bf16[8,24,896]{2,1,0:T(8,128)(2,1)S(1)}, u32[]{:S(2)}, u32[]{:S(2)}) %all-to-all-start.3) | async-done | bytes 344096 | tf_op jit(solution)/shard_map/all_to_all | solution.py:40
  122.3 0.8 slice.111
  (89 shorter events, 8.6 us)
Async XLA Ops:
  0.6 18.7 %copy-start = (bf16[128,1792]{1,0:T(8,128)(2,1)S(1)}, bf16[128,1792]{1,0:T(8,128)(2,1)}, u32[]{:S(2)}) copy-start(bf16[128,1792]{1,0:T(8,128)(2,1)} %param.8) | copy-start | bytes 1376260
  0.6 16.7 %copy-start.4 = (bf16[128,1792]{1,0:T(8,128)(2,1)S(1)}, bf16[128,1792]{1,0:T(8,128)(2,1)}, u32[]{:S(2)}) copy-start(bf16[128,1792]{1,0:T(8,128)(2,1)} %param.7) | copy-start | bytes 1376260
  0.7 18.6 %copy-start.12 = (s32[128]{0:T(128)S(1)}, s32[128]{0:T(128)}, u32[]{:S(2)}) copy-start(s32[128]{0:T(128)} %param.13) | copy-start | bytes 1540
  2.9 19.8 %collective-permute-start = (bf16[128,896]{1,0:T(8,128)(2,1)S(1)}, bf16[128,896]{1,0:T(8,128)(2,1)S(1)}, u32[]{:S(2)}, u32[]{:S(2)}) collective-permute-start(bf16[128,896]{1,0:T(8,128)(2,1)S(1)} %get-tuple-element.44), channel_id=1, source_target_pairs={{0,1},{1,2},{2,3},{3,8},{8,9},{9,10},{10,11},{11,0},{4,5},{5,6},{6... | collective-permute-start | bytes 688136 | tf_op jit(solution)/shard_map/ppermute | solution.py:32
  7.2 17.3 %collective-permute-start.1 = (bf16[128,896]{1,0:T(8,128)(2,1)}, bf16[128,896]{1,0:T(8,128)(2,1)S(1)}, u32[]{:S(2)}, u32[]{:S(2)}) collective-permute-start(bf16[128,896]{1,0:T(8,128)(2,1)} %get-tuple-element.43), channel_id=1, source_target_pairs={{0,11},{1,0},{2,1},{3,2},{8,3},{9,8},{10,9},{11,10},{4,15},{5,4},{... | collective-permute-start | bytes 688136 | tf_op jit(solution)/shard_map/ppermute | solution.py:32
  9.2 15.4 %collective-permute-start.2 = (bf16[128,896]{1,0:T(8,128)(2,1)}, bf16[128,896]{1,0:T(8,128)(2,1)S(1)}, u32[]{:S(2)}, u32[]{:S(2)}) collective-permute-start(bf16[128,896]{1,0:T(8,128)(2,1)} %get-tuple-element.45), channel_id=1, source_target_pairs={{0,2},{1,11},{2,8},{3,1},{8,10},{9,3},{10,0},{11,9},{4,6},{5,15},{... | collective-permute-start | bytes 688136 | tf_op jit(solution)/shard_map/ppermute | solution.py:32
  17.4 7.3 %collective-permute-start.3 = (bf16[128,896]{1,0:T(8,128)(2,1)S(1)}, bf16[128,896]{1,0:T(8,128)(2,1)S(1)}, u32[]{:S(2)}, u32[]{:S(2)}) collective-permute-start(bf16[128,896]{1,0:T(8,128)(2,1)S(1)} %constant_dynamic-slice_fusion.1), channel_id=1, source_target_pairs={{0,4},{4,0},{1,5},{5,1},{2,6},{6,2},{3,7},{7,3},{8,12},{12,8},{9,1... | collective-permute-start | bytes 688136 | tf_op jit(solution)/shard_map/ppermute | solution.py:36
  20.4 4.3 %collective-permute-start.4 = (f32[64,896]{1,0:T(8,128)}, f32[64,896]{1,0:T(8,128)}, u32[]{:S(2)}, u32[]{:S(2)}) collective-permute-start(f32[64,896]{1,0:T(8,128)} %constant_dynamic-slice_fusion), channel_id=1, source_target_pairs={{0,4},{4,0},{1,5},{5,1},{2,6},{6,2},{3,7},{7,3},{8,12},{12,8},{9,1... | collective-permute-start | bytes 688136 | tf_op jit(solution)/shard_map/ppermute | solution.py:36
  22.8 0.7 copy-start.8
  24.7 0.7 copy-start.7
  25.4 8.2 %collective-permute-start.5 = (bf16[512,896]{1,0:T(8,128)(2,1)S(1)}, bf16[512,896]{1,0:T(8,128)(2,1)S(1)}, u32[]{:S(2)}, u32[]{:S(2)}) collective-permute-start(bf16[512,896]{1,0:T(8,128)(2,1)S(1)} %bitcast.40), channel_id=1, source_target_pairs={{0,4},{4,0},{1,5},{5,1},{2,6},{6,2},{3,7},{7,3},{8,12},{12,8},{9,1... | collective-permute-start | bytes 2752520 | tf_op jit(solution)/shard_map/ppermute | solution.py:36
  27.3 6.7 %copy-start.5 = (bf16[128,1792]{1,0:T(8,128)(2,1)S(1)}, bf16[128,1792]{1,0:T(8,128)(2,1)}, u32[]{:S(2)}) copy-start(bf16[128,1792]{1,0:T(8,128)(2,1)} %param.7) | copy-start | bytes 1376260
  28.5 19.2 %copy-start.3 = (bf16[256,896]{1,0:T(8,128)(2,1)}, bf16[256,896]{1,0:T(8,128)(2,1)S(1)}, u32[]{:S(2)}) copy-start(bf16[256,896]{1,0:T(8,128)(2,1)S(1)} %pad_maximum_fusion.1) | copy-start | bytes 1376260
  28.5 11.9 %copy-start.9 = (s32[128]{0:T(128)S(1)}, s32[128]{0:T(128)}, u32[]{:S(2)}) copy-start(s32[128]{0:T(128)} %param.12) | copy-start | bytes 1540
  28.5 12.0 %copy-start.10 = (f32[128]{0:T(128)S(1)}, f32[128]{0:T(128)}, u32[]{:S(2)}) copy-start(f32[128]{0:T(128)} %param.11) | copy-start | bytes 1540
  28.5 19.3 %copy-start.11 = (f32[128]{0:T(128)S(1)}, f32[128]{0:T(128)}, u32[]{:S(2)}) copy-start(f32[128]{0:T(128)} %param.10) | copy-start | bytes 1540
  28.5 19.1 %collective-permute-start.6 = (bf16[256,896]{1,0:T(8,128)(2,1)S(1)}, bf16[256,896]{1,0:T(8,128)(2,1)}, u32[]{:S(2)}, u32[]{:S(2)}) collective-permute-start(bf16[256,896]{1,0:T(8,128)(2,1)S(1)} %pad_maximum_fusion.1), channel_id=1, source_target_pairs={{32,0},{48,16},{0,32},{16,48},{33,1},{49,17},{1,33},{17,49},{34,2}... | collective-permute-start | bytes 1376264 | tf_op jit(solution)/shard_map/ppermute | solution.py:119
  33.6 14.0 %copy-start.1 = (bf16[512,896]{1,0:T(8,128)(2,1)}, bf16[512,896]{1,0:T(8,128)(2,1)S(1)}, u32[]{:S(2)}) copy-start(bf16[512,896]{1,0:T(8,128)(2,1)S(1)} %collective-permute-done.5) | copy-start | bytes 2752516
  35.2 12.4 %all-to-all-start = ((f32[4,32,512]{2,1,0:T(8,128)}), f32[4,32,512]{2,1,0:T(8,128)S(1)}, u32[]{:S(2)}, u32[]{:S(2)}) async-start(f32[4,32,512]{2,1,0:T(8,128)} %bitcast.46), calls=%async_computation | async-start | bytes 524288 | tf_op jit(solution)/shard_map/all_to_all | solution.py:40
  40.5 22.2 %collective-permute-start.8 = (bf16[256,896]{1,0:T(8,128)(2,1)S(1)}, bf16[256,896]{1,0:T(8,128)(2,1)}, u32[]{:S(2)}, u32[]{:S(2)}) collective-permute-start(bf16[256,896]{1,0:T(8,128)(2,1)S(1)} %pad_maximum_fusion.1), channel_id=1, source_target_pairs={{48,0},{0,16},{16,32},{32,48},{49,1},{1,17},{17,33},{33,49},{50,2}... | collective-permute-start | bytes 1376264 | tf_op jit(solution)/shard_map/ppermute | solution.py:119
  43.0 19.7 %collective-permute-start.7 = (bf16[256,896]{1,0:T(8,128)(2,1)S(1)}, bf16[256,896]{1,0:T(8,128)(2,1)}, u32[]{:S(2)}, u32[]{:S(2)}) collective-permute-start(bf16[256,896]{1,0:T(8,128)(2,1)S(1)} %pad_maximum_fusion.1), channel_id=1, source_target_pairs={{16,0},{32,16},{48,32},{0,48},{17,1},{33,17},{49,33},{1,49},{18,2}... | collective-permute-start | bytes 1376264 | tf_op jit(solution)/shard_map/ppermute | solution.py:119
  49.4 15.0 %all-to-all-start.1 = ((bf16[32,32,128]{2,1,0:T(8,128)(2,1)}), bf16[32,32,128]{2,1,0:T(8,128)(2,1)S(1)}, u32[]{:S(2)}, u32[]{:S(2)}) async-start(bf16[32,32,128]{2,1,0:T(8,128)(2,1)} %bitcast.10), calls=%async_computation.1 | async-start | bytes 524288 | tf_op jit(solution)/shard_map/all_to_all | solution.py:40
  55.1 7.6 %collective-permute-start.9 = (bf16[32,640]{1,0:T(8,128)(2,1)S(1)}, bf16[32,640]{1,0:T(8,128)(2,1)S(1)}, u32[]{:S(2)}, u32[]{:S(2)}) collective-permute-start(bf16[32,640]{1,0:T(8,128)(2,1)S(1)} %concatenate.37), channel_id=1, source_target_pairs={{0,1},{1,0},{2,3},{3,2},{4,5},{5,4},{6,7},{7,6},{8,9},{9,8},{10,11... | collective-permute-start | bytes 122888 | tf_op jit(solution)/shard_map/ppermute | solution.py:149
  64.4 0.9 copy-start.6
  65.0 39.3 %copy-start.2 = (bf16[512,896]{1,0:T(8,128)(2,1)S(1)}, bf16[512,896]{1,0:T(8,128)(2,1)}, u32[]{:S(2)}) copy-start(bf16[512,896]{1,0:T(8,128)(2,1)} %copy-done.1) | copy-start | bytes 2752516
  66.0 21.1 %all-to-all-start.2 = ((bf16[8,24,896]{2,1,0:T(8,128)(2,1)}), bf16[8,24,896]{2,1,0:T(8,128)(2,1)S(1)}, u32[]{:S(2)}, u32[]{:S(2)}) async-start(bf16[8,24,896]{2,1,0:T(8,128)(2,1)} %pad_maximum_fusion.3), calls=%async_computation.2 | async-start | bytes 688128 | tf_op jit(solution)/shard_map/all_to_all | solution.py:40
  73.1 7.2 %collective-permute-start.10 = (bf16[64,640]{1,0:T(8,128)(2,1)S(1)}, bf16[64,640]{1,0:T(8,128)(2,1)S(1)}, u32[]{:S(2)}, u32[]{:S(2)}) collective-permute-start(bf16[64,640]{1,0:T(8,128)(2,1)S(1)} %pad_maximum_fusion.5), channel_id=1, source_target_pairs={{0,2},{1,3},{2,0},{3,1},{4,6},{5,7},{6,4},{7,5},{8,10},{9,11},{10,... | collective-permute-start | bytes 245768 | tf_op jit(solution)/shard_map/ppermute | solution.py:149
  87.2 21.8 %collective-permute-start.12 = (bf16[16,896]{1,0:T(8,128)(2,1)S(1)}, bf16[16,896]{1,0:T(8,128)(2,1)S(1)}, u32[]{:S(2)}, u32[]{:S(2)}) collective-permute-start(bf16[16,896]{1,0:T(8,128)(2,1)S(1)} %slice.140), channel_id=1, source_target_pairs={{0,8},{1,136},{2,264},{3,392},{4,72},{5,200},{6,328},{7,456},{8,0}... | collective-permute-start | bytes 86024 | tf_op jit(solution)/shard_map/ppermute | solution.py:171
  91.9 17.1 %collective-permute-start.11 = (bf16[16,896]{1,0:T(8,128)(2,1)S(1)}, bf16[16,896]{1,0:T(8,128)(2,1)S(1)}, u32[]{:S(2)}, u32[]{:S(2)}) collective-permute-start(bf16[16,896]{1,0:T(8,128)(2,1)S(1)} %slice.140), channel_id=1, source_target_pairs={{0,0},{1,128},{2,256},{3,384},{4,64},{5,192},{6,320},{7,448},{8,8}... | collective-permute-start | bytes 86024 | tf_op jit(solution)/shard_map/ppermute | solution.py:171
  99.4 9.5 %collective-permute-start.13 = (bf16[8,896]{1,0:T(8,128)(2,1)S(1)}, bf16[8,896]{1,0:T(8,128)(2,1)S(1)}, u32[]{:S(2)}, u32[]{:S(2)}) collective-permute-start(bf16[8,896]{1,0:T(8,128)(2,1)S(1)} %slice.141), channel_id=1, source_target_pairs={{0,8},{8,0},{1,9},{9,1},{2,10},{10,2},{3,11},{11,3},{4,12},{12,4},... | collective-permute-start | bytes 43016 | tf_op jit(solution)/shard_map/ppermute | solution.py:36
  109.8 11.9 %all-to-all-start.3 = ((bf16[8,24,896]{2,1,0:T(8,128)(2,1)}), bf16[8,24,896]{2,1,0:T(8,128)(2,1)S(1)}, u32[]{:S(2)}, u32[]{:S(2)}) async-start(bf16[8,24,896]{2,1,0:T(8,128)(2,1)} %broadcast_in_dim.16), calls=%async_computation.3 | async-start | bytes 688128 | tf_op jit(solution)/shard_map/all_to_all | solution.py:40

commit v7 on v6

--- a/solution.py
+++ b/solution.py
@@ -72,23 +72,18 @@
     return whole.reshape(4 * rows, half)
 
 
-def by_core(own, other, core):
-    return jnp.concatenate((jnp.where(core == 0, own, other), jnp.where(core == 0, other, own)), 0)
-
-
 def three_parts(value):
     first = lax.reduce_precision(value, 8, 7)
     second = lax.reduce_precision(value - first, 8, 7)
     return first, second, value - first - second
 
 
-def owner(flip):
+def owner():
     def place(source):
         source, quarter = divmod(source, 4)
         source, at_core = divmod(source, 2)
         source, at_zhi = divmod(source, 2)
         at_dp, at_x = divmod(source, 4)
-        at_zhi = at_zhi ^ flip
         return ((((2 * quarter + at_core) * 4 + at_x) * 2 + at_zhi) * 2 + at_dp % 2) * 4 + at_dp // 2
 
     return [(i, place(i)) for i in range(lax.axis_size(EVERY))]
@@ -103,17 +98,18 @@
     replicas = lax.axis_size("dp")
 
     onehot = (embed_ids[:, None] == lax.broadcasted_iota(jnp.int32, (1, 8 * replicas), 1)).astype(BF16)
-    embed = dot(onehot, embed_cot, ((0,), (0,)))
-    taken = (swap(half_of(final_normed, 1 - core), "core"), swap(half_of(embed, 1 - core), "core"))
+    embed = dot(onehot, embed_cot, ((0,), (0,))).astype(BF16)
+    normed = jnp.concatenate(
+        (half_of(final_normed, core), swap(half_of(final_normed, 1 - core), "core")), 0
+    )
+    taken = swap(half_of(embed, 1 - core), "core")
 
     mine = window_half(head, core, rank)
-    mine, taken = lax.optimization_barrier((mine, taken))
+    mine, normed, taken = lax.optimization_barrier((mine, normed, taken))
     other = swap(mine, "core")
     logits = dot(half_of(final_normed, core), mine, ((1,), (1,))) + dot(
         half_of(final_normed, 1 - core), other, ((1,), (1,))
     )
-    normed = by_core(half_of(final_normed, core), taken[0], core)
-    embed = half_of(embed, core) + taken[1]
 
     def from_x(value, ahead):
         return lax.ppermute(value, "x", [((i + ahead) % 4, i) for i in range(4)])
@@ -145,34 +141,38 @@
 
     quarters = jnp.stack([sent[:, i * LANES : (i + 1) * LANES] for i in range(4)])
     quarters = jnp.broadcast_to(quarters[:, None], (4, 8, part, LANES)).reshape(32, part, LANES)
-    def joined(value, step):
-        other = lax.ppermute(value, "tensor", [(i, i ^ step) for i in range(4)])
+    def joined(value, other, step):
         first = (rank & step) == 0
         return jnp.concatenate((jnp.where(first, value, other), jnp.where(first, other, value)), 0)
 
-    quarters, sent = lax.optimization_barrier((quarters, sent))
+    def partner(value, step):
+        return lax.ppermute(value, "tensor", [(i, i ^ step) for i in range(4)])
+
+    quarters, sent, taken = lax.optimization_barrier((quarters, sent, taken))
     quarter = exchange(quarters, GROUP + ("tensor",)).reshape(4, 2 * tokens, LANES)
-    sent = joined(sent, 1)
+    pair = partner(sent, 1)
     normed = jnp.concatenate((own, after, far, before), 0)
+    pair, normed = lax.optimization_barrier((pair, normed))
+    sent = joined(sent, pair, 1)
     quarter, normed, sent = lax.optimization_barrier((quarter, normed, sent))
     quarter = lax.dynamic_slice_in_dim(jnp.concatenate((quarter, quarter[:3]), 0), lax.axis_index("x"), 4, 0)
+    turned = jnp.concatenate((quarter[:, tokens:], quarter[:, :tokens]), 1)
+    quarter = jnp.where(core == 0, quarter, turned)
     term = dot(quarter.reshape(8 * tokens, LANES), normed, ((0,), (0,))).astype(BF16)
-    embed = embed.astype(BF16)
+    embed = (half_of(embed, core).astype(F32) + taken.astype(F32)).astype(BF16)
     term = jnp.concatenate((term.reshape(replicas, 16, half), embed.reshape(replicas, 8, half)), 1)
     term, sent = lax.optimization_barrier((term, sent))
     term = exchange(term, "dp")
-    gathered = joined(sent, 2)
-    term, gathered = lax.optimization_barrier((term, gathered))
+    pair = partner(sent, 2)
+    term, pair = lax.optimization_barrier((term, pair))
+    gathered = joined(sent, pair, 2)
     term = term.astype(F32).sum(0)
     dlogits = gathered[:, :vocab]
     token_loss = jnp.sum(gathered[:, vocab : vocab + 3].astype(F32), axis=1)
 
-    block, embed = term[:16].astype(BF16), term[16:]
-    moved = lax.ppermute(block, EVERY, owner(0)).astype(F32) + lax.ppermute(
-        block, EVERY, owner(1)
-    ).astype(F32)
-    embed = embed + swap(embed.astype(BF16), "zhi").astype(F32)
-    pieces = spread(jnp.concatenate((moved, embed), 0).astype(BF16), GROUP).astype(F32)
+    term = (term + swap(term.astype(BF16), "zhi").astype(F32)).astype(BF16)
+    block = lax.ppermute(term[:16], EVERY, owner())
+    pieces = spread(jnp.concatenate((block, term[16:]), 0), GROUP).astype(F32)
     head_grad = pieces[:, :16].reshape(vocab // 4, half)
     embed_grad = pieces[:, 16:].reshape(4, 2, 8, half).sum(0)
     embed_grad = jnp.concatenate((embed_grad[0], embed_grad[1]), 1)

time: 124 us -> 121 us (0.976)
  waiting for transfers between devices: 23.6 us -> 31.6 us
  starting transfers between devices: 78.6 us -> 71.4 us
  local copies, waits for them, and re-layouts: 8.6 us -> 5.61 us
    ppermute x4 -> x3, starting transfers between devices: 19.7 us -> 11.6 us  [the longest x2 7.6 us: partner(): return lax.ppermute(value, 'tensor', [(i, i ^ step) for i in range(4)])]
    ppermute x4 -> x3, waiting for transfers between devices: 5.77 us -> 11.4 us  [the longest x1 7.36 us: shards(): block = lax.ppermute(term[:16], EVERY, owner())]
    all_to_all x4, waiting for transfers between devices: 13.8 us -> 15.3 us  [exchange(): return lax.all_to_all(value, axes, 0, 0)]
  transfers between devices with their start and end apart: 18 -> 17, of which waited for: 5 -> 8; matrix products, arithmetic and copies ran while one was open for 10% -> 8% of each run, Pallas kernels for 0% -> 0%
where the time goes in v7:
time: 121 us; the launch traced here: 120 us
  starting transfers between devices  71.4 us (59%)
  waiting for transfers between devices  31.6 us (26%)
  other arithmetic  6.99 us (6%)
  local copies, waits for them, and re-layouts  5.61 us (5%)
  matrix products  3 us (2%)
  between operations  1.34 us (1%)
    all_to_all x4, starting transfers between devices, exchange(): return lax.all_to_all(value, axes, 0, 0)  21.9 us
    all_to_all x4, waiting for transfers between devices, exchange(): return lax.all_to_all(value, axes, 0, 0)  15.3 us
    ppermute x3, starting transfers between devices, shift(): lax.ppermute(value, RING, [(i, step(i) % count) for i in range(count)])  14.4 us
    ppermute x3, starting transfers between devices, from_x(): return lax.ppermute(value, 'x', [((i + ahead) % 4, i) for i in range(4)])  12 us
    ppermute x4, starting transfers between devices, swap(): return lax.ppermute(value, axis, [(0, 1), (1, 0)])  11.5 us
    ppermute x2, starting transfers between devices, partner(): return lax.ppermute(value, 'tensor', [(i, i ^ step) for i in range(4)])  7.6 us
    ppermute x1, waiting for transfers between devices, shards(): block = lax.ppermute(term[:16], EVERY, owner())  7.36 us
    ppermute x4, waiting for transfers between devices, swap(): return lax.ppermute(value, axis, [(0, 1), (1, 0)])  4.88 us
  transfers between devices with their start and end apart: 17, of which 8 were waited for; matrix products, arithmetic and copies ran while one was open for 8% of the time, Pallas kernels for 0%

profile of v7, /device:TPU:128, one launch (start us, length us, event | category | flops | bytes accessed | tf_op | source)
XLA Modules:
  0.0 120.0 jit_solution(6678813626514325202)
XLA Ops:
  0.7 1.4 %constant_dynamic-slice_fusion.2 = (bf16[128,896]{1,0:T(8,128)(2,1)S(1)}, bf16[128,896]{1,0:T(8,128)(2,1)S(1)}, bf16[128,896]{1,0:T(8,128)(2,1)S(1)}, bf16[128,896]{1,0:T(8,128)(2,1)S(1)}) fusion(bf16[128,7168]{1,0:T(8,128)(2,1)} %param.9, s32[]{:T(128)S(6)} %select_n.227, s32[]{:T(128)S(6)} %select_n.221, s32[]{:T(128)S(6)} %select_n.218, s32[]{:T(128)S(6)} %select_n.224), kind=kLoop, calls=%fused_computation.56 | loop fusion | bytes 1835024 | tf_op jit(solution)/shard_map/dynamic_slice | solution.py:60
  2.2 4.3 %collective-permute-start = (bf16[128,896]{1,0:T(8,128)(2,1)S(1)}, bf16[128,896]{1,0:T(8,128)(2,1)S(1)}, u32[]{:S(2)}, u32[]{:S(2)}) collective-permute-start(bf16[128,896]{1,0:T(8,128)(2,1)S(1)} %get-tuple-element.50), channel_id=1, source_target_pairs={{0,1},{1,2},{2,3},{3,8},{8,9},{9,10},{10,11},{11,0},{4,5},{5,6},{6... | collective-permute-start | bytes 688136 | tf_op jit(solution)/shard_map/ppermute | solution.py:32
  6.5 1.9 %collective-permute-start.1 = (bf16[128,896]{1,0:T(8,128)(2,1)S(1)}, bf16[128,896]{1,0:T(8,128)(2,1)S(1)}, u32[]{:S(2)}, u32[]{:S(2)}) collective-permute-start(bf16[128,896]{1,0:T(8,128)(2,1)S(1)} %get-tuple-element.49), channel_id=1, source_target_pairs={{0,11},{1,0},{2,1},{3,2},{8,3},{9,8},{10,9},{11,10},{4,15},{5,4},{... | collective-permute-start | bytes 688136 | tf_op jit(solution)/shard_map/ppermute | solution.py:32
  8.4 8.2 %collective-permute-start.2 = (bf16[128,896]{1,0:T(8,128)(2,1)S(1)}, bf16[128,896]{1,0:T(8,128)(2,1)S(1)}, u32[]{:S(2)}, u32[]{:S(2)}) collective-permute-start(bf16[128,896]{1,0:T(8,128)(2,1)S(1)} %get-tuple-element.51), channel_id=1, source_target_pairs={{0,2},{1,11},{2,8},{3,1},{8,10},{9,3},{10,0},{11,9},{4,6},{5,15},{... | collective-permute-start | bytes 688136 | tf_op jit(solution)/shard_map/ppermute | solution.py:32
  16.6 1.9 %collective-permute-start.3 = (bf16[128,896]{1,0:T(8,128)(2,1)S(1)}, bf16[128,896]{1,0:T(8,128)(2,1)S(1)}, u32[]{:S(2)}, u32[]{:S(2)}) collective-permute-start(bf16[128,896]{1,0:T(8,128)(2,1)S(1)} %get-tuple-element.55), channel_id=1, source_target_pairs={{0,4},{4,0},{1,5},{5,1},{2,6},{6,2},{3,7},{7,3},{8,12},{12,8},{9,1... | collective-permute-start | bytes 688136 | tf_op jit(solution)/shard_map/ppermute | solution.py:36
  19.6 2.4 %collective-permute-start.4 = (bf16[64,896]{1,0:T(8,128)(2,1)S(1)}, bf16[64,896]{1,0:T(8,128)(2,1)}, u32[]{:S(2)}, u32[]{:S(2)}) collective-permute-start(bf16[64,896]{1,0:T(8,128)(2,1)S(1)} %constant_dynamic-slice_fusion), channel_id=1, source_target_pairs={{0,4},{4,0},{1,5},{5,1},{2,6},{6,2},{3,7},{7,3},{8,12},{12,8},{9,1... | collective-permute-start | bytes 344072 | tf_op jit(solution)/shard_map/ppermute | solution.py:36
  23.1 2.3 %collective-permute-start.5 = (bf16[512,896]{1,0:T(8,128)(2,1)S(1)}, bf16[512,896]{1,0:T(8,128)(2,1)S(1)}, u32[]{:S(2)}, u32[]{:S(2)}) collective-permute-start(bf16[512,896]{1,0:T(8,128)(2,1)S(1)} %bitcast.41), channel_id=1, source_target_pairs={{0,4},{4,0},{1,5},{5,1},{2,6},{6,2},{3,7},{7,3},{8,12},{12,8},{9,1... | collective-permute-start | bytes 2752520 | tf_op jit(solution)/shard_map/ppermute | solution.py:36
  25.4 4.9 %collective-permute-start.6 = (bf16[256,896]{1,0:T(8,128)(2,1)S(1)}, bf16[256,896]{1,0:T(8,128)(2,1)}, u32[]{:S(2)}, u32[]{:S(2)}) collective-permute-start(bf16[256,896]{1,0:T(8,128)(2,1)S(1)} %pad_maximum_fusion.1), channel_id=1, source_target_pairs={{32,0},{48,16},{0,32},{16,48},{33,1},{49,17},{1,33},{17,49},{34,2}... | collective-permute-start | bytes 1376264 | tf_op jit(solution)/shard_map/ppermute | solution.py:115
  30.8 1.1 convolution_add_fusion
  32.0 5.7 %all-to-all-start = ((f32[4,32,512]{2,1,0:T(8,128)}), f32[4,32,512]{2,1,0:T(8,128)S(1)}, u32[]{:S(2)}, u32[]{:S(2)}) async-start(f32[4,32,512]{2,1,0:T(8,128)} %bitcast.5), calls=%async_computation | async-start | bytes 524288 | tf_op jit(solution)/shard_map/all_to_all | solution.py:40
  37.8 2.5 %collective-permute-start.9 = (bf16[256,896]{1,0:T(8,128)(2,1)S(1)}, bf16[256,896]{1,0:T(8,128)(2,1)}, u32[]{:S(2)}, u32[]{:S(2)}) collective-permute-start(bf16[256,896]{1,0:T(8,128)(2,1)S(1)} %pad_maximum_fusion.1), channel_id=1, source_target_pairs={{48,0},{0,16},{16,32},{32,48},{49,1},{1,17},{17,33},{33,49},{50,2}... | collective-permute-start | bytes 1376264 | tf_op jit(solution)/shard_map/ppermute | solution.py:115
  40.3 4.5 %collective-permute-start.8 = (bf16[256,896]{1,0:T(8,128)(2,1)S(1)}, bf16[256,896]{1,0:T(8,128)(2,1)}, u32[]{:S(2)}, u32[]{:S(2)}) collective-permute-start(bf16[256,896]{1,0:T(8,128)(2,1)S(1)} %pad_maximum_fusion.1), channel_id=1, source_target_pairs={{16,0},{32,16},{48,32},{0,48},{17,1},{33,17},{49,33},{1,49},{18,2}... | collective-permute-start | bytes 1376264 | tf_op jit(solution)/shard_map/ppermute | solution.py:115
  46.6 5.7 %all-to-all-start.1 = ((bf16[32,32,128]{2,1,0:T(8,128)(2,1)}), bf16[32,32,128]{2,1,0:T(8,128)(2,1)S(1)}, u32[]{:S(2)}, u32[]{:S(2)}) async-start(bf16[32,32,128]{2,1,0:T(8,128)(2,1)} %bitcast.10), calls=%async_computation.1 | async-start | bytes 524288 | tf_op jit(solution)/shard_map/all_to_all | solution.py:40
  52.3 1.6 %fusion.1 = bf16[8,8,896]{2,1,0:T(8,128)(2,1)} fusion(bf16[64,896]{1,0:T(8,128)(2,1)} %collective-permute-done.4, bf16[64,1792]{1,0:T(8,128)(2,1)} %copy-done.4, s32[]{:T(128)S(6)} %select_n.216), kind=kLoop, calls=%fused_computation.18 | loop fusion | flops 229376 | bytes 344068 | tf_op jit(solution)/shard_map/reshape | solution.py:163
  54.0 3.4 %collective-permute-start.7 = (bf16[32,640]{1,0:T(8,128)(2,1)S(1)}, bf16[32,640]{1,0:T(8,128)(2,1)S(1)}, u32[]{:S(2)}, u32[]{:S(2)}) collective-permute-start(bf16[32,640]{1,0:T(8,128)(2,1)S(1)} %concatenate.35), channel_id=1, source_target_pairs={{0,1},{1,0},{2,3},{3,2},{4,5},{5,4},{6,7},{7,6},{8,9},{9,8},{10,11... | collective-permute-start | bytes 122888 | tf_op jit(solution)/shard_map/ppermute | solution.py:149
  57.4 1.6 %pad_maximum_fusion = bf16[1024,896]{1,0:T(8,128)(2,1)S(1)} fusion(bf16[256,896]{1,0:T(8,128)(2,1)} %collective-permute-done.9, bf16[256,896]{1,0:T(8,128)(2,1)} %collective-permute-done.6, bf16[256,896]{1,0:T(8,128)(2,1)} %collective-permute-done.8, bf16[256,896]{1,0:T(8,128)(2,1)} %copy-done.3), kind=kLoop, calls=%fused_computation.1 | loop fusion | flops 7340032 | bytes 3670016 | tf_op jit(solution)/shard_map/concatenate | solution.py:154
  59.0 1.0 collective-permute-done.7
  60.0 1.5 %all-to-all-done.1 = bf16[32,32,128]{2,1,0:T(8,128)(2,1)S(1)} async-done(((bf16[32,32,128]{2,1,0:T(8,128)(2,1)}), bf16[32,32,128]{2,1,0:T(8,128)(2,1)S(1)}, u32[]{:S(2)}, u32[]{:S(2)}) %all-to-all-start.1) | async-done | bytes 262176 | tf_op jit(solution)/shard_map/all_to_all | solution.py:40
  62.5 0.8 pad_maximum_fusion.3
  63.3 7.1 %all-to-all-start.2 = ((bf16[8,24,896]{2,1,0:T(8,128)(2,1)}), bf16[8,24,896]{2,1,0:T(8,128)(2,1)S(1)}, u32[]{:S(2)}, u32[]{:S(2)}) async-start(bf16[8,24,896]{2,1,0:T(8,128)(2,1)} %pad_maximum_fusion.3), calls=%async_computation.2 | async-start | bytes 688128 | tf_op jit(solution)/shard_map/all_to_all | solution.py:40
  70.4 4.2 %collective-permute-start.10 = (bf16[64,640]{1,0:T(8,128)(2,1)S(1)}, bf16[64,640]{1,0:T(8,128)(2,1)S(1)}, u32[]{:S(2)}, u32[]{:S(2)}) collective-permute-start(bf16[64,640]{1,0:T(8,128)(2,1)S(1)} %pad_maximum_fusion.5), channel_id=1, source_target_pairs={{0,2},{1,3},{2,0},{3,1},{4,6},{5,7},{6,4},{7,5},{8,10},{9,11},{10,... | collective-permute-start | bytes 245768 | tf_op jit(solution)/shard_map/ppermute | solution.py:149
  74.6 3.1 %collective-permute-done.10 = bf16[64,640]{1,0:T(8,128)(2,1)S(1)} collective-permute-done((bf16[64,640]{1,0:T(8,128)(2,1)S(1)}, bf16[64,640]{1,0:T(8,128)(2,1)S(1)}, u32[]{:S(2)}, u32[]{:S(2)}) %collective-permute-start.10) | collective-permute-done | bytes 81952 | tf_op jit(solution)/shard_map/ppermute | solution.py:149
  77.7 6.8 %all-to-all-done.2 = bf16[8,24,896]{2,1,0:T(8,128)(2,1)S(1)} async-done(((bf16[8,24,896]{2,1,0:T(8,128)(2,1)}), bf16[8,24,896]{2,1,0:T(8,128)(2,1)S(1)}, u32[]{:S(2)}, u32[]{:S(2)}) %all-to-all-start.2) | async-done | bytes 344096 | tf_op jit(solution)/shard_map/all_to_all | solution.py:40
  84.6 4.9 %collective-permute-start.11 = (bf16[24,896]{1,0:T(8,128)(2,1)S(1)}, bf16[24,896]{1,0:T(8,128)(2,1)S(1)}, u32[]{:S(2)}, u32[]{:S(2)}) collective-permute-start(bf16[24,896]{1,0:T(8,128)(2,1)S(1)} %convert_element_type.54), channel_id=1, source_target_pairs={{0,8},{8,0},{1,9},{9,1},{2,10},{10,2},{3,11},{11,3},{4,12},{12,4},... | collective-permute-start | bytes 129032 | tf_op jit(solution)/shard_map/ppermute | solution.py:36
  90.2 4.2 %collective-permute-done.11 = bf16[24,896]{1,0:T(8,128)(2,1)S(1)} collective-permute-done((bf16[24,896]{1,0:T(8,128)(2,1)S(1)}, bf16[24,896]{1,0:T(8,128)(2,1)S(1)}, u32[]{:S(2)}, u32[]{:S(2)}) %collective-permute-start.11) | collective-permute-done | bytes 43040 | tf_op jit(solution)/shard_map/ppermute | solution.py:36
  94.5 4.0 %collective-permute-start.12 = (bf16[16,896]{1,0:T(8,128)(2,1)S(1)}, bf16[16,896]{1,0:T(8,128)(2,1)S(1)}, u32[]{:S(2)}, u32[]{:S(2)}) collective-permute-start(bf16[16,896]{1,0:T(8,128)(2,1)S(1)} %slice.118), channel_id=1, source_target_pairs={{0,0},{1,128},{2,256},{3,384},{4,64},{5,192},{6,320},{7,448},{8,8}... | collective-permute-start | bytes 86024 | tf_op jit(solution)/shard_map/ppermute | solution.py:174
  98.6 7.4 %collective-permute-done.12 = bf16[16,896]{1,0:T(8,128)(2,1)S(1)} collective-permute-done((bf16[16,896]{1,0:T(8,128)(2,1)S(1)}, bf16[16,896]{1,0:T(8,128)(2,1)S(1)}, u32[]{:S(2)}, u32[]{:S(2)}) %collective-permute-start.12) | collective-permute-done | bytes 28704 | tf_op jit(solution)/shard_map/ppermute | solution.py:174
  105.9 0.8 broadcast_in_dim.16
  106.7 3.4 %all-to-all-start.3 = ((bf16[8,24,896]{2,1,0:T(8,128)(2,1)}), bf16[8,24,896]{2,1,0:T(8,128)(2,1)S(1)}, u32[]{:S(2)}, u32[]{:S(2)}) async-start(bf16[8,24,896]{2,1,0:T(8,128)(2,1)} %broadcast_in_dim.16), calls=%async_computation.3 | async-start | bytes 688128 | tf_op jit(solution)/shard_map/all_to_all | solution.py:40
  110.7 0.8 pad_maximum_fusion.2
  111.5 7.0 %all-to-all-done.3 = bf16[8,24,896]{2,1,0:T(8,128)(2,1)S(1)} async-done(((bf16[8,24,896]{2,1,0:T(8,128)(2,1)}), bf16[8,24,896]{2,1,0:T(8,128)(2,1)S(1)}, u32[]{:S(2)}, u32[]{:S(2)}) %all-to-all-start.3) | async-done | bytes 344096 | tf_op jit(solution)/shard_map/all_to_all | solution.py:40
  119.2 0.8 slice.120
  (83 shorter events, 7.4 us)
Async XLA Ops:
  0.6 17.9 %copy-start = (bf16[128,1792]{1,0:T(8,128)(2,1)S(1)}, bf16[128,1792]{1,0:T(8,128)(2,1)}, u32[]{:S(2)}) copy-start(bf16[128,1792]{1,0:T(8,128)(2,1)} %param.8) | copy-start | bytes 1376260
  0.6 15.9 %copy-start.5 = (bf16[128,1792]{1,0:T(8,128)(2,1)S(1)}, bf16[128,1792]{1,0:T(8,128)(2,1)}, u32[]{:S(2)}) copy-start(bf16[128,1792]{1,0:T(8,128)(2,1)} %param.7) | copy-start | bytes 1376260
  0.7 17.9 %copy-start.10 = (s32[128]{0:T(128)S(1)}, s32[128]{0:T(128)}, u32[]{:S(2)}) copy-start(s32[128]{0:T(128)} %param.13) | copy-start | bytes 1540
  2.2 19.9 %collective-permute-start = (bf16[128,896]{1,0:T(8,128)(2,1)S(1)}, bf16[128,896]{1,0:T(8,128)(2,1)S(1)}, u32[]{:S(2)}, u32[]{:S(2)}) collective-permute-start(bf16[128,896]{1,0:T(8,128)(2,1)S(1)} %get-tuple-element.50), channel_id=1, source_target_pairs={{0,1},{1,2},{2,3},{3,8},{8,9},{9,10},{10,11},{11,0},{4,5},{5,6},{6... | collective-permute-start | bytes 688136 | tf_op jit(solution)/shard_map/ppermute | solution.py:32
  6.5 15.8 %collective-permute-start.1 = (bf16[128,896]{1,0:T(8,128)(2,1)S(1)}, bf16[128,896]{1,0:T(8,128)(2,1)S(1)}, u32[]{:S(2)}, u32[]{:S(2)}) collective-permute-start(bf16[128,896]{1,0:T(8,128)(2,1)S(1)} %get-tuple-element.49), channel_id=1, source_target_pairs={{0,11},{1,0},{2,1},{3,2},{8,3},{9,8},{10,9},{11,10},{4,15},{5,4},{... | collective-permute-start | bytes 688136 | tf_op jit(solution)/shard_map/ppermute | solution.py:32
  8.4 13.9 %collective-permute-start.2 = (bf16[128,896]{1,0:T(8,128)(2,1)S(1)}, bf16[128,896]{1,0:T(8,128)(2,1)S(1)}, u32[]{:S(2)}, u32[]{:S(2)}) collective-permute-start(bf16[128,896]{1,0:T(8,128)(2,1)S(1)} %get-tuple-element.51), channel_id=1, source_target_pairs={{0,2},{1,11},{2,8},{3,1},{8,10},{9,3},{10,0},{11,9},{4,6},{5,15},{... | collective-permute-start | bytes 688136 | tf_op jit(solution)/shard_map/ppermute | solution.py:32
  16.6 5.7 %collective-permute-start.3 = (bf16[128,896]{1,0:T(8,128)(2,1)S(1)}, bf16[128,896]{1,0:T(8,128)(2,1)S(1)}, u32[]{:S(2)}, u32[]{:S(2)}) collective-permute-start(bf16[128,896]{1,0:T(8,128)(2,1)S(1)} %get-tuple-element.55), channel_id=1, source_target_pairs={{0,4},{4,0},{1,5},{5,1},{2,6},{6,2},{3,7},{7,3},{8,12},{12,8},{9,1... | collective-permute-start | bytes 688136 | tf_op jit(solution)/shard_map/ppermute | solution.py:36
  18.9 0.7 copy-start.4
  19.6 3.5 %collective-permute-start.4 = (bf16[64,896]{1,0:T(8,128)(2,1)S(1)}, bf16[64,896]{1,0:T(8,128)(2,1)}, u32[]{:S(2)}, u32[]{:S(2)}) collective-permute-start(bf16[64,896]{1,0:T(8,128)(2,1)S(1)} %constant_dynamic-slice_fusion), channel_id=1, source_target_pairs={{0,4},{4,0},{1,5},{5,1},{2,6},{6,2},{3,7},{7,3},{8,12},{12,8},{9,1... | collective-permute-start | bytes 344072 | tf_op jit(solution)/shard_map/ppermute | solution.py:36
  22.4 17.9 %copy-start.3 = (bf16[256,896]{1,0:T(8,128)(2,1)}, bf16[256,896]{1,0:T(8,128)(2,1)S(1)}, u32[]{:S(2)}) copy-start(bf16[256,896]{1,0:T(8,128)(2,1)S(1)} %pad_maximum_fusion.1) | copy-start | bytes 1376260
  22.4 15.2 %copy-start.7 = (s32[128]{0:T(128)S(1)}, s32[128]{0:T(128)}, u32[]{:S(2)}) copy-start(s32[128]{0:T(128)} %param.12) | copy-start | bytes 1540
  22.4 15.3 %copy-start.8 = (f32[128]{0:T(128)S(1)}, f32[128]{0:T(128)}, u32[]{:S(2)}) copy-start(f32[128]{0:T(128)} %param.11) | copy-start | bytes 1540
  23.1 7.3 %collective-permute-start.5 = (bf16[512,896]{1,0:T(8,128)(2,1)S(1)}, bf16[512,896]{1,0:T(8,128)(2,1)S(1)}, u32[]{:S(2)}, u32[]{:S(2)}) collective-permute-start(bf16[512,896]{1,0:T(8,128)(2,1)S(1)} %bitcast.41), channel_id=1, source_target_pairs={{0,4},{4,0},{1,5},{5,1},{2,6},{6,2},{3,7},{7,3},{8,12},{12,8},{9,1... | collective-permute-start | bytes 2752520 | tf_op jit(solution)/shard_map/ppermute | solution.py:36
  25.4 19.6 %copy-start.9 = (f32[128]{0:T(128)S(1)}, f32[128]{0:T(128)}, u32[]{:S(2)}) copy-start(f32[128]{0:T(128)} %param.10) | copy-start | bytes 1540
  25.4 19.4 %collective-permute-start.6 = (bf16[256,896]{1,0:T(8,128)(2,1)S(1)}, bf16[256,896]{1,0:T(8,128)(2,1)}, u32[]{:S(2)}, u32[]{:S(2)}) collective-permute-start(bf16[256,896]{1,0:T(8,128)(2,1)S(1)} %pad_maximum_fusion.1), channel_id=1, source_target_pairs={{32,0},{48,16},{0,32},{16,48},{33,1},{49,17},{1,33},{17,49},{34,2}... | collective-permute-start | bytes 1376264 | tf_op jit(solution)/shard_map/ppermute | solution.py:115
  30.4 14.5 %copy-start.1 = (bf16[512,896]{1,0:T(8,128)(2,1)}, bf16[512,896]{1,0:T(8,128)(2,1)S(1)}, u32[]{:S(2)}) copy-start(bf16[512,896]{1,0:T(8,128)(2,1)S(1)} %collective-permute-done.5) | copy-start | bytes 2752516
  32.0 12.9 %all-to-all-start = ((f32[4,32,512]{2,1,0:T(8,128)}), f32[4,32,512]{2,1,0:T(8,128)S(1)}, u32[]{:S(2)}, u32[]{:S(2)}) async-start(f32[4,32,512]{2,1,0:T(8,128)} %bitcast.5), calls=%async_computation | async-start | bytes 524288 | tf_op jit(solution)/shard_map/all_to_all | solution.py:40
  37.8 19.6 %collective-permute-start.9 = (bf16[256,896]{1,0:T(8,128)(2,1)S(1)}, bf16[256,896]{1,0:T(8,128)(2,1)}, u32[]{:S(2)}, u32[]{:S(2)}) collective-permute-start(bf16[256,896]{1,0:T(8,128)(2,1)S(1)} %pad_maximum_fusion.1), channel_id=1, source_target_pairs={{48,0},{0,16},{16,32},{32,48},{49,1},{1,17},{17,33},{33,49},{50,2}... | collective-permute-start | bytes 1376264 | tf_op jit(solution)/shard_map/ppermute | solution.py:115
  40.3 17.1 %collective-permute-start.8 = (bf16[256,896]{1,0:T(8,128)(2,1)S(1)}, bf16[256,896]{1,0:T(8,128)(2,1)}, u32[]{:S(2)}, u32[]{:S(2)}) collective-permute-start(bf16[256,896]{1,0:T(8,128)(2,1)S(1)} %pad_maximum_fusion.1), channel_id=1, source_target_pairs={{16,0},{32,16},{48,32},{0,48},{17,1},{33,17},{49,33},{1,49},{18,2}... | collective-permute-start | bytes 1376264 | tf_op jit(solution)/shard_map/ppermute | solution.py:115
  46.6 14.9 %all-to-all-start.1 = ((bf16[32,32,128]{2,1,0:T(8,128)(2,1)}), bf16[32,32,128]{2,1,0:T(8,128)(2,1)S(1)}, u32[]{:S(2)}, u32[]{:S(2)}) async-start(bf16[32,32,128]{2,1,0:T(8,128)(2,1)} %bitcast.10), calls=%async_computation.1 | async-start | bytes 524288 | tf_op jit(solution)/shard_map/all_to_all | solution.py:40
  54.0 6.0 %collective-permute-start.7 = (bf16[32,640]{1,0:T(8,128)(2,1)S(1)}, bf16[32,640]{1,0:T(8,128)(2,1)S(1)}, u32[]{:S(2)}, u32[]{:S(2)}) collective-permute-start(bf16[32,640]{1,0:T(8,128)(2,1)S(1)} %concatenate.35), channel_id=1, source_target_pairs={{0,1},{1,0},{2,3},{3,2},{4,5},{5,4},{6,7},{7,6},{8,9},{9,8},{10,11... | collective-permute-start | bytes 122888 | tf_op jit(solution)/shard_map/ppermute | solution.py:149
  61.6 0.9 copy-start.6
  62.2 27.4 %copy-start.2 = (bf16[512,896]{1,0:T(8,128)(2,1)S(1)}, bf16[512,896]{1,0:T(8,128)(2,1)}, u32[]{:S(2)}) copy-start(bf16[512,896]{1,0:T(8,128)(2,1)} %copy-done.1) | copy-start | bytes 2752516
  63.3 21.3 %all-to-all-start.2 = ((bf16[8,24,896]{2,1,0:T(8,128)(2,1)}), bf16[8,24,896]{2,1,0:T(8,128)(2,1)S(1)}, u32[]{:S(2)}, u32[]{:S(2)}) async-start(bf16[8,24,896]{2,1,0:T(8,128)(2,1)} %pad_maximum_fusion.3), calls=%async_computation.2 | async-start | bytes 688128 | tf_op jit(solution)/shard_map/all_to_all | solution.py:40
  70.4 7.3 %collective-permute-start.10 = (bf16[64,640]{1,0:T(8,128)(2,1)S(1)}, bf16[64,640]{1,0:T(8,128)(2,1)S(1)}, u32[]{:S(2)}, u32[]{:S(2)}) collective-permute-start(bf16[64,640]{1,0:T(8,128)(2,1)S(1)} %pad_maximum_fusion.5), channel_id=1, source_target_pairs={{0,2},{1,3},{2,0},{3,1},{4,6},{5,7},{6,4},{7,5},{8,10},{9,11},{10,... | collective-permute-start | bytes 245768 | tf_op jit(solution)/shard_map/ppermute | solution.py:149
  84.6 9.8 %collective-permute-start.11 = (bf16[24,896]{1,0:T(8,128)(2,1)S(1)}, bf16[24,896]{1,0:T(8,128)(2,1)S(1)}, u32[]{:S(2)}, u32[]{:S(2)}) collective-permute-start(bf16[24,896]{1,0:T(8,128)(2,1)S(1)} %convert_element_type.54), channel_id=1, source_target_pairs={{0,8},{8,0},{1,9},{9,1},{2,10},{10,2},{3,11},{11,3},{4,12},{12,4},... | collective-permute-start | bytes 129032 | tf_op jit(solution)/shard_map/ppermute | solution.py:36
  94.5 11.5 %collective-permute-start.12 = (bf16[16,896]{1,0:T(8,128)(2,1)S(1)}, bf16[16,896]{1,0:T(8,128)(2,1)S(1)}, u32[]{:S(2)}, u32[]{:S(2)}) collective-permute-start(bf16[16,896]{1,0:T(8,128)(2,1)S(1)} %slice.118), channel_id=1, source_target_pairs={{0,0},{1,128},{2,256},{3,384},{4,64},{5,192},{6,320},{7,448},{8,8}... | collective-permute-start | bytes 86024 | tf_op jit(solution)/shard_map/ppermute | solution.py:174
  106.7 11.8 %all-to-all-start.3 = ((bf16[8,24,896]{2,1,0:T(8,128)(2,1)}), bf16[8,24,896]{2,1,0:T(8,128)(2,1)S(1)}, u32[]{:S(2)}, u32[]{:S(2)}) async-start(bf16[8,24,896]{2,1,0:T(8,128)(2,1)} %broadcast_in_dim.16), calls=%async_computation.3 | async-start | bytes 688128 | tf_op jit(solution)/shard_map/all_to_all | solution.py:40

commit v8 on v7

--- a/solution.py
+++ b/solution.py
@@ -53,7 +53,7 @@
 def window_half(head, core, rank):
     rows, width = head.shape
     half = width // 8
-    chunk = rows // 4
+    chunk = rows // 8
 
     def block(ahead):
         at = (rank + ahead) % 4 * (2 * half) + core * half
@@ -65,10 +65,10 @@
         (shift(block(2), across), 2),
         (block(0), 0),
     )
-    whole = jnp.zeros((4, 4, chunk, half), head.dtype)
+    whole = jnp.zeros((4, 2, 4, chunk, half), head.dtype)
     for piece, ahead in pieces:
-        piece = piece.reshape(4, 1, chunk, half)
-        whole = lax.dynamic_update_slice(whole, piece, (0, (rank + ahead) % 4, 0, 0))
+        piece = piece.reshape(4, 2, 1, chunk, half)
+        whole = lax.dynamic_update_slice(whole, piece, (0, 0, (rank + ahead) % 4, 0, 0))
     return whole.reshape(4 * rows, half)
 
 
@@ -84,7 +84,7 @@
         source, at_core = divmod(source, 2)
         source, at_zhi = divmod(source, 2)
         at_dp, at_x = divmod(source, 4)
-        return ((((2 * quarter + at_core) * 4 + at_x) * 2 + at_zhi) * 2 + at_dp % 2) * 4 + at_dp // 2
+        return ((((2 * quarter + at_core) * 4 + at_x) * 2 + at_zhi) * 2 + at_dp // 4) * 4 + at_dp % 4
 
     return [(i, place(i)) for i in range(lax.axis_size(EVERY))]
 
@@ -128,7 +128,7 @@
 
     lse_rest = own_part(rest_lse)
     column = lax.broadcasted_iota(jnp.int32, (1, vocab), 1)
-    column = (column // 32 % 4) * 128 + column // 128 * 32 + column % 32
+    column = column // 16 % 4 * 128 + column // 64 * 16 + column % 16
     hits = own_part(target_ids) == column
     top = jnp.maximum(jnp.max(logits, axis=1, keepdims=True), lse_rest)
     total = jnp.exp(lse_rest - top) + jnp.sum(jnp.exp(logits - top), axis=1, keepdims=True)

time: 121 us -> 120 us (level)
  the two profiles are of different devices: /device:TPU:128 before, /device:TPU:1 now
where the time goes in v8:
time: 120 us; the launch traced here: 119 us
  starting transfers between devices  69 us (58%)
  waiting for transfers between devices  33.2 us (28%)
  other arithmetic  6.99 us (6%)
  local copies, waits for them, and re-layouts  5.59 us (5%)
  matrix products  3 us (2%)
  between operations  1.34 us (1%)
    all_to_all x4, starting transfers between devices, exchange(): return lax.all_to_all(value, axes, 0, 0)  19.6 us
    all_to_all x4, waiting for transfers between devices, exchange(): return lax.all_to_all(value, axes, 0, 0)  16.7 us
    ppermute x3, starting transfers between devices, shift(): lax.ppermute(value, RING, [(i, step(i) % count) for i in range(count)])  15.3 us
    ppermute x4, starting transfers between devices, swap(): return lax.ppermute(value, axis, [(0, 1), (1, 0)])  13.4 us
    ppermute x3, starting transfers between devices, from_x(): return lax.ppermute(value, 'x', [((i + ahead) % 4, i) for i in range(4)])  11.1 us
    ppermute x2, waiting for transfers between devices, partner(): return lax.ppermute(value, 'tensor', [(i, i ^ step) for i in range(4)])  5.92 us
    ppermute x2, starting transfers between devices, partner(): return lax.ppermute(value, 'tensor', [(i, i ^ step) for i in range(4)])  5.72 us
    ppermute x1, waiting for transfers between devices, shards(): block = lax.ppermute(term[:16], EVERY, owner())  5.18 us
  transfers between devices with their start and end apart: 17, of which 9 were waited for; matrix products, arithmetic and copies ran while one was open for 8% of the time, Pallas kernels for 0%

profile of v8, /device:TPU:1, one launch (start us, length us, event | category | flops | bytes accessed | tf_op | source)
XLA Modules:
  0.0 119.2 jit_solution(15050225468522844486)
XLA Ops:
  0.7 1.4 %constant_dynamic-slice_fusion.2 = (bf16[128,896]{1,0:T(8,128)(2,1)S(1)}, bf16[128,896]{1,0:T(8,128)(2,1)S(1)}, bf16[128,896]{1,0:T(8,128)(2,1)S(1)}, bf16[128,896]{1,0:T(8,128)(2,1)S(1)}) fusion(bf16[128,7168]{1,0:T(8,128)(2,1)} %param.9, s32[]{:T(128)S(6)} %select_n.227, s32[]{:T(128)S(6)} %select_n.221, s32[]{:T(128)S(6)} %select_n.218, s32[]{:T(128)S(6)} %select_n.224), kind=kLoop, calls=%fused_computation.56 | loop fusion | bytes 1835024 | tf_op jit(solution)/shard_map/dynamic_slice | solution.py:60
  2.2 4.8 %collective-permute-start = (bf16[128,896]{1,0:T(8,128)(2,1)S(1)}, bf16[128,896]{1,0:T(8,128)(2,1)S(1)}, u32[]{:S(2)}, u32[]{:S(2)}) collective-permute-start(bf16[128,896]{1,0:T(8,128)(2,1)S(1)} %get-tuple-element.50), channel_id=1, source_target_pairs={{0,1},{1,2},{2,3},{3,8},{8,9},{9,10},{10,11},{11,0},{4,5},{5,6},{6... | collective-permute-start | bytes 688136 | tf_op jit(solution)/shard_map/ppermute | solution.py:32
  7.0 8.6 %collective-permute-start.1 = (bf16[128,896]{1,0:T(8,128)(2,1)S(1)}, bf16[128,896]{1,0:T(8,128)(2,1)S(1)}, u32[]{:S(2)}, u32[]{:S(2)}) collective-permute-start(bf16[128,896]{1,0:T(8,128)(2,1)S(1)} %get-tuple-element.49), channel_id=1, source_target_pairs={{0,11},{1,0},{2,1},{3,2},{8,3},{9,8},{10,9},{11,10},{4,15},{5,4},{... | collective-permute-start | bytes 688136 | tf_op jit(solution)/shard_map/ppermute | solution.py:32
  15.6 1.9 %collective-permute-start.2 = (bf16[128,896]{1,0:T(8,128)(2,1)S(1)}, bf16[128,896]{1,0:T(8,128)(2,1)S(1)}, u32[]{:S(2)}, u32[]{:S(2)}) collective-permute-start(bf16[128,896]{1,0:T(8,128)(2,1)S(1)} %get-tuple-element.51), channel_id=1, source_target_pairs={{0,2},{1,11},{2,8},{3,1},{8,10},{9,3},{10,0},{11,9},{4,6},{5,15},{... | collective-permute-start | bytes 688136 | tf_op jit(solution)/shard_map/ppermute | solution.py:32
  17.6 2.9 %collective-permute-start.3 = (bf16[128,896]{1,0:T(8,128)(2,1)S(1)}, bf16[128,896]{1,0:T(8,128)(2,1)S(1)}, u32[]{:S(2)}, u32[]{:S(2)}) collective-permute-start(bf16[128,896]{1,0:T(8,128)(2,1)S(1)} %get-tuple-element.55), channel_id=1, source_target_pairs={{0,4},{4,0},{1,5},{5,1},{2,6},{6,2},{3,7},{7,3},{8,12},{12,8},{9,1... | collective-permute-start | bytes 688136 | tf_op jit(solution)/shard_map/ppermute | solution.py:36
  21.6 1.9 %collective-permute-start.4 = (bf16[64,896]{1,0:T(8,128)(2,1)S(1)}, bf16[64,896]{1,0:T(8,128)(2,1)}, u32[]{:S(2)}, u32[]{:S(2)}) collective-permute-start(bf16[64,896]{1,0:T(8,128)(2,1)S(1)} %constant_dynamic-slice_fusion), channel_id=1, source_target_pairs={{0,4},{4,0},{1,5},{5,1},{2,6},{6,2},{3,7},{7,3},{8,12},{12,8},{9,1... | collective-permute-start | bytes 344072 | tf_op jit(solution)/shard_map/ppermute | solution.py:36
  23.7 2.1 %collective-permute-done.2 = bf16[128,896]{1,0:T(8,128)(2,1)S(1)} collective-permute-done((bf16[128,896]{1,0:T(8,128)(2,1)S(1)}, bf16[128,896]{1,0:T(8,128)(2,1)S(1)}, u32[]{:S(2)}, u32[]{:S(2)}) %collective-permute-start.2) | collective-permute-done | bytes 229408 | tf_op jit(solution)/shard_map/ppermute | solution.py:32
  26.0 3.9 %collective-permute-start.5 = (bf16[512,896]{1,0:T(8,128)(2,1)S(1)}, bf16[512,896]{1,0:T(8,128)(2,1)S(1)}, u32[]{:S(2)}, u32[]{:S(2)}) collective-permute-start(bf16[512,896]{1,0:T(8,128)(2,1)S(1)} %bitcast.41), channel_id=1, source_target_pairs={{0,4},{4,0},{1,5},{5,1},{2,6},{6,2},{3,7},{7,3},{8,12},{12,8},{9,1... | collective-permute-start | bytes 2752520 | tf_op jit(solution)/shard_map/ppermute | solution.py:36
  29.9 4.7 %collective-permute-start.6 = (bf16[256,896]{1,0:T(8,128)(2,1)S(1)}, bf16[256,896]{1,0:T(8,128)(2,1)}, u32[]{:S(2)}, u32[]{:S(2)}) collective-permute-start(bf16[256,896]{1,0:T(8,128)(2,1)S(1)} %pad_maximum_fusion.1), channel_id=1, source_target_pairs={{32,0},{48,16},{0,32},{16,48},{33,1},{49,17},{1,33},{17,49},{34,2}... | collective-permute-start | bytes 1376264 | tf_op jit(solution)/shard_map/ppermute | solution.py:115
  35.0 1.1 convolution_add_fusion
  36.2 3.7 %all-to-all-start = ((f32[4,32,512]{2,1,0:T(8,128)}), f32[4,32,512]{2,1,0:T(8,128)S(1)}, u32[]{:S(2)}, u32[]{:S(2)}) async-start(f32[4,32,512]{2,1,0:T(8,128)} %bitcast.5), calls=%async_computation | async-start | bytes 524288 | tf_op jit(solution)/shard_map/all_to_all | solution.py:40
  40.0 2.2 %collective-permute-start.9 = (bf16[256,896]{1,0:T(8,128)(2,1)S(1)}, bf16[256,896]{1,0:T(8,128)(2,1)}, u32[]{:S(2)}, u32[]{:S(2)}) collective-permute-start(bf16[256,896]{1,0:T(8,128)(2,1)S(1)} %pad_maximum_fusion.1), channel_id=1, source_target_pairs={{48,0},{0,16},{16,32},{32,48},{49,1},{1,17},{17,33},{33,49},{50,2}... | collective-permute-start | bytes 1376264 | tf_op jit(solution)/shard_map/ppermute | solution.py:115
  42.2 4.3 %collective-permute-start.8 = (bf16[256,896]{1,0:T(8,128)(2,1)S(1)}, bf16[256,896]{1,0:T(8,128)(2,1)}, u32[]{:S(2)}, u32[]{:S(2)}) collective-permute-start(bf16[256,896]{1,0:T(8,128)(2,1)S(1)} %pad_maximum_fusion.1), channel_id=1, source_target_pairs={{16,0},{32,16},{48,32},{0,48},{17,1},{33,17},{49,33},{1,49},{18,2}... | collective-permute-start | bytes 1376264 | tf_op jit(solution)/shard_map/ppermute | solution.py:115
  46.5 1.1 all-to-all-done
  49.3 5.8 %all-to-all-start.1 = ((bf16[32,32,128]{2,1,0:T(8,128)(2,1)}), bf16[32,32,128]{2,1,0:T(8,128)(2,1)S(1)}, u32[]{:S(2)}, u32[]{:S(2)}) async-start(bf16[32,32,128]{2,1,0:T(8,128)(2,1)} %bitcast.10), calls=%async_computation.1 | async-start | bytes 524288 | tf_op jit(solution)/shard_map/all_to_all | solution.py:40
  55.1 1.6 %fusion.1 = bf16[8,8,896]{2,1,0:T(8,128)(2,1)} fusion(bf16[64,896]{1,0:T(8,128)(2,1)} %collective-permute-done.4, bf16[64,1792]{1,0:T(8,128)(2,1)} %copy-done.4, s32[]{:T(128)S(6)} %select_n.216), kind=kLoop, calls=%fused_computation.18 | loop fusion | flops 229376 | bytes 344068 | tf_op jit(solution)/shard_map/reshape | solution.py:163
  56.8 3.3 %collective-permute-start.7 = (bf16[32,640]{1,0:T(8,128)(2,1)S(1)}, bf16[32,640]{1,0:T(8,128)(2,1)S(1)}, u32[]{:S(2)}, u32[]{:S(2)}) collective-permute-start(bf16[32,640]{1,0:T(8,128)(2,1)S(1)} %concatenate.35), channel_id=1, source_target_pairs={{0,1},{1,0},{2,3},{3,2},{4,5},{5,4},{6,7},{7,6},{8,9},{9,8},{10,11... | collective-permute-start | bytes 122888 | tf_op jit(solution)/shard_map/ppermute | solution.py:149
  60.1 1.6 %pad_maximum_fusion = bf16[1024,896]{1,0:T(8,128)(2,1)S(1)} fusion(bf16[256,896]{1,0:T(8,128)(2,1)} %collective-permute-done.9, bf16[256,896]{1,0:T(8,128)(2,1)} %collective-permute-done.6, bf16[256,896]{1,0:T(8,128)(2,1)} %collective-permute-done.8, bf16[256,896]{1,0:T(8,128)(2,1)} %copy-done.3), kind=kLoop, calls=%fused_computation.1 | loop fusion | flops 7340032 | bytes 3670016 | tf_op jit(solution)/shard_map/concatenate | solution.py:154
  62.4 3.8 %all-to-all-done.1 = bf16[32,32,128]{2,1,0:T(8,128)(2,1)S(1)} async-done(((bf16[32,32,128]{2,1,0:T(8,128)(2,1)}), bf16[32,32,128]{2,1,0:T(8,128)(2,1)S(1)}, u32[]{:S(2)}, u32[]{:S(2)}) %all-to-all-start.1) | async-done | bytes 262176 | tf_op jit(solution)/shard_map/all_to_all | solution.py:40
  67.2 0.8 pad_maximum_fusion.3
  68.0 6.8 %all-to-all-start.2 = ((bf16[8,24,896]{2,1,0:T(8,128)(2,1)}), bf16[8,24,896]{2,1,0:T(8,128)(2,1)S(1)}, u32[]{:S(2)}, u32[]{:S(2)}) async-start(bf16[8,24,896]{2,1,0:T(8,128)(2,1)} %pad_maximum_fusion.3), calls=%async_computation.2 | async-start | bytes 688128 | tf_op jit(solution)/shard_map/all_to_all | solution.py:40
  74.8 2.4 %collective-permute-start.10 = (bf16[64,640]{1,0:T(8,128)(2,1)S(1)}, bf16[64,640]{1,0:T(8,128)(2,1)S(1)}, u32[]{:S(2)}, u32[]{:S(2)}) collective-permute-start(bf16[64,640]{1,0:T(8,128)(2,1)S(1)} %pad_maximum_fusion.5), channel_id=1, source_target_pairs={{0,2},{1,3},{2,0},{3,1},{4,6},{5,7},{6,4},{7,5},{8,10},{9,11},{10,... | collective-permute-start | bytes 245768 | tf_op jit(solution)/shard_map/ppermute | solution.py:149
  77.3 5.2 %collective-permute-done.10 = bf16[64,640]{1,0:T(8,128)(2,1)S(1)} collective-permute-done((bf16[64,640]{1,0:T(8,128)(2,1)S(1)}, bf16[64,640]{1,0:T(8,128)(2,1)S(1)}, u32[]{:S(2)}, u32[]{:S(2)}) %collective-permute-start.10) | collective-permute-done | bytes 81952 | tf_op jit(solution)/shard_map/ppermute | solution.py:149
  82.5 6.3 %all-to-all-done.2 = bf16[8,24,896]{2,1,0:T(8,128)(2,1)S(1)} async-done(((bf16[8,24,896]{2,1,0:T(8,128)(2,1)}), bf16[8,24,896]{2,1,0:T(8,128)(2,1)S(1)}, u32[]{:S(2)}, u32[]{:S(2)}) %all-to-all-start.2) | async-done | bytes 344096 | tf_op jit(solution)/shard_map/all_to_all | solution.py:40
  88.9 4.6 %collective-permute-start.11 = (bf16[24,896]{1,0:T(8,128)(2,1)S(1)}, bf16[24,896]{1,0:T(8,128)(2,1)S(1)}, u32[]{:S(2)}, u32[]{:S(2)}) collective-permute-start(bf16[24,896]{1,0:T(8,128)(2,1)S(1)} %convert_element_type.54), channel_id=1, source_target_pairs={{0,8},{8,0},{1,9},{9,1},{2,10},{10,2},{3,11},{11,3},{4,12},{12,4},... | collective-permute-start | bytes 129032 | tf_op jit(solution)/shard_map/ppermute | solution.py:36
  94.2 3.3 %collective-permute-done.11 = bf16[24,896]{1,0:T(8,128)(2,1)S(1)} collective-permute-done((bf16[24,896]{1,0:T(8,128)(2,1)S(1)}, bf16[24,896]{1,0:T(8,128)(2,1)S(1)}, u32[]{:S(2)}, u32[]{:S(2)}) %collective-permute-start.11) | collective-permute-done | bytes 43040 | tf_op jit(solution)/shard_map/ppermute | solution.py:36
  97.6 3.8 %collective-permute-start.12 = (bf16[16,896]{1,0:T(8,128)(2,1)S(1)}, bf16[16,896]{1,0:T(8,128)(2,1)S(1)}, u32[]{:S(2)}, u32[]{:S(2)}) collective-permute-start(bf16[16,896]{1,0:T(8,128)(2,1)S(1)} %slice.118), channel_id=1, source_target_pairs={{0,0},{1,128},{2,256},{3,384},{4,64},{5,192},{6,320},{7,448},{8,8}... | collective-permute-start | bytes 86024 | tf_op jit(solution)/shard_map/ppermute | solution.py:174
  101.5 5.2 %collective-permute-done.12 = bf16[16,896]{1,0:T(8,128)(2,1)S(1)} collective-permute-done((bf16[16,896]{1,0:T(8,128)(2,1)S(1)}, bf16[16,896]{1,0:T(8,128)(2,1)S(1)}, u32[]{:S(2)}, u32[]{:S(2)}) %collective-permute-start.12) | collective-permute-done | bytes 28704 | tf_op jit(solution)/shard_map/ppermute | solution.py:174
  107.4 3.4 %all-to-all-start.3 = ((bf16[8,24,896]{2,1,0:T(8,128)(2,1)}), bf16[8,24,896]{2,1,0:T(8,128)(2,1)S(1)}, u32[]{:S(2)}, u32[]{:S(2)}) async-start(bf16[8,24,896]{2,1,0:T(8,128)(2,1)} %broadcast_in_dim.16), calls=%async_computation.3 | async-start | bytes 688128 | tf_op jit(solution)/shard_map/all_to_all | solution.py:40
  111.4 0.8 pad_maximum_fusion.2
  112.2 5.5 %all-to-all-done.3 = bf16[8,24,896]{2,1,0:T(8,128)(2,1)S(1)} async-done(((bf16[8,24,896]{2,1,0:T(8,128)(2,1)}), bf16[8,24,896]{2,1,0:T(8,128)(2,1)S(1)}, u32[]{:S(2)}, u32[]{:S(2)}) %all-to-all-start.3) | async-done | bytes 344096 | tf_op jit(solution)/shard_map/all_to_all | solution.py:40
  118.4 0.8 slice.120
  (83 shorter events, 8.2 us)
Async XLA Ops:
  0.6 19.9 %copy-start = (bf16[128,1792]{1,0:T(8,128)(2,1)S(1)}, bf16[128,1792]{1,0:T(8,128)(2,1)}, u32[]{:S(2)}) copy-start(bf16[128,1792]{1,0:T(8,128)(2,1)} %param.8) | copy-start | bytes 1376260
  0.6 16.9 %copy-start.5 = (bf16[128,1792]{1,0:T(8,128)(2,1)S(1)}, bf16[128,1792]{1,0:T(8,128)(2,1)}, u32[]{:S(2)}) copy-start(bf16[128,1792]{1,0:T(8,128)(2,1)} %param.7) | copy-start | bytes 1376260
  0.7 19.9 %copy-start.10 = (s32[128]{0:T(128)S(1)}, s32[128]{0:T(128)}, u32[]{:S(2)}) copy-start(s32[128]{0:T(128)} %param.13) | copy-start | bytes 1540
  2.2 21.4 %collective-permute-start = (bf16[128,896]{1,0:T(8,128)(2,1)S(1)}, bf16[128,896]{1,0:T(8,128)(2,1)S(1)}, u32[]{:S(2)}, u32[]{:S(2)}) collective-permute-start(bf16[128,896]{1,0:T(8,128)(2,1)S(1)} %get-tuple-element.50), channel_id=1, source_target_pairs={{0,1},{1,2},{2,3},{3,8},{8,9},{9,10},{10,11},{11,0},{4,5},{5,6},{6... | collective-permute-start | bytes 688136 | tf_op jit(solution)/shard_map/ppermute | solution.py:32
  7.0 16.6 %collective-permute-start.1 = (bf16[128,896]{1,0:T(8,128)(2,1)S(1)}, bf16[128,896]{1,0:T(8,128)(2,1)S(1)}, u32[]{:S(2)}, u32[]{:S(2)}) collective-permute-start(bf16[128,896]{1,0:T(8,128)(2,1)S(1)} %get-tuple-element.49), channel_id=1, source_target_pairs={{0,11},{1,0},{2,1},{3,2},{8,3},{9,8},{10,9},{11,10},{4,15},{5,4},{... | collective-permute-start | bytes 688136 | tf_op jit(solution)/shard_map/ppermute | solution.py:32
  15.6 10.2 %collective-permute-start.2 = (bf16[128,896]{1,0:T(8,128)(2,1)S(1)}, bf16[128,896]{1,0:T(8,128)(2,1)S(1)}, u32[]{:S(2)}, u32[]{:S(2)}) collective-permute-start(bf16[128,896]{1,0:T(8,128)(2,1)S(1)} %get-tuple-element.51), channel_id=1, source_target_pairs={{0,2},{1,11},{2,8},{3,1},{8,10},{9,3},{10,0},{11,9},{4,6},{5,15},{... | collective-permute-start | bytes 688136 | tf_op jit(solution)/shard_map/ppermute | solution.py:32
  17.6 8.2 %collective-permute-start.3 = (bf16[128,896]{1,0:T(8,128)(2,1)S(1)}, bf16[128,896]{1,0:T(8,128)(2,1)S(1)}, u32[]{:S(2)}, u32[]{:S(2)}) collective-permute-start(bf16[128,896]{1,0:T(8,128)(2,1)S(1)} %get-tuple-element.55), channel_id=1, source_target_pairs={{0,4},{4,0},{1,5},{5,1},{2,6},{6,2},{3,7},{7,3},{8,12},{12,8},{9,1... | collective-permute-start | bytes 688136 | tf_op jit(solution)/shard_map/ppermute | solution.py:36
  20.9 0.7 copy-start.4
  21.6 4.4 %collective-permute-start.4 = (bf16[64,896]{1,0:T(8,128)(2,1)S(1)}, bf16[64,896]{1,0:T(8,128)(2,1)}, u32[]{:S(2)}, u32[]{:S(2)}) collective-permute-start(bf16[64,896]{1,0:T(8,128)(2,1)S(1)} %constant_dynamic-slice_fusion), channel_id=1, source_target_pairs={{0,4},{4,0},{1,5},{5,1},{2,6},{6,2},{3,7},{7,3},{8,12},{12,8},{9,1... | collective-permute-start | bytes 344072 | tf_op jit(solution)/shard_map/ppermute | solution.py:36
  25.9 16.3 %copy-start.3 = (bf16[256,896]{1,0:T(8,128)(2,1)}, bf16[256,896]{1,0:T(8,128)(2,1)S(1)}, u32[]{:S(2)}) copy-start(bf16[256,896]{1,0:T(8,128)(2,1)S(1)} %pad_maximum_fusion.1) | copy-start | bytes 1376260
  25.9 13.9 %copy-start.7 = (s32[128]{0:T(128)S(1)}, s32[128]{0:T(128)}, u32[]{:S(2)}) copy-start(s32[128]{0:T(128)} %param.12) | copy-start | bytes 1540
  25.9 14.0 %copy-start.8 = (f32[128]{0:T(128)S(1)}, f32[128]{0:T(128)}, u32[]{:S(2)}) copy-start(f32[128]{0:T(128)} %param.11) | copy-start | bytes 1540
  26.0 8.6 %collective-permute-start.5 = (bf16[512,896]{1,0:T(8,128)(2,1)S(1)}, bf16[512,896]{1,0:T(8,128)(2,1)S(1)}, u32[]{:S(2)}, u32[]{:S(2)}) collective-permute-start(bf16[512,896]{1,0:T(8,128)(2,1)S(1)} %bitcast.41), channel_id=1, source_target_pairs={{0,4},{4,0},{1,5},{5,1},{2,6},{6,2},{3,7},{7,3},{8,12},{12,8},{9,1... | collective-permute-start | bytes 2752520 | tf_op jit(solution)/shard_map/ppermute | solution.py:36
  29.9 17.8 %copy-start.9 = (f32[128]{0:T(128)S(1)}, f32[128]{0:T(128)}, u32[]{:S(2)}) copy-start(f32[128]{0:T(128)} %param.10) | copy-start | bytes 1540
  29.9 16.6 %collective-permute-start.6 = (bf16[256,896]{1,0:T(8,128)(2,1)S(1)}, bf16[256,896]{1,0:T(8,128)(2,1)}, u32[]{:S(2)}, u32[]{:S(2)}) collective-permute-start(bf16[256,896]{1,0:T(8,128)(2,1)S(1)} %pad_maximum_fusion.1), channel_id=1, source_target_pairs={{32,0},{48,16},{0,32},{16,48},{33,1},{49,17},{1,33},{17,49},{34,2}... | collective-permute-start | bytes 1376264 | tf_op jit(solution)/shard_map/ppermute | solution.py:115
  34.6 13.0 %copy-start.1 = (bf16[512,896]{1,0:T(8,128)(2,1)}, bf16[512,896]{1,0:T(8,128)(2,1)S(1)}, u32[]{:S(2)}) copy-start(bf16[512,896]{1,0:T(8,128)(2,1)S(1)} %collective-permute-done.5) | copy-start | bytes 2752516
  36.2 11.4 %all-to-all-start = ((f32[4,32,512]{2,1,0:T(8,128)}), f32[4,32,512]{2,1,0:T(8,128)S(1)}, u32[]{:S(2)}, u32[]{:S(2)}) async-start(f32[4,32,512]{2,1,0:T(8,128)} %bitcast.5), calls=%async_computation | async-start | bytes 524288 | tf_op jit(solution)/shard_map/all_to_all | solution.py:40
  40.0 20.1 %collective-permute-start.9 = (bf16[256,896]{1,0:T(8,128)(2,1)S(1)}, bf16[256,896]{1,0:T(8,128)(2,1)}, u32[]{:S(2)}, u32[]{:S(2)}) collective-permute-start(bf16[256,896]{1,0:T(8,128)(2,1)S(1)} %pad_maximum_fusion.1), channel_id=1, source_target_pairs={{48,0},{0,16},{16,32},{32,48},{49,1},{1,17},{17,33},{33,49},{50,2}... | collective-permute-start | bytes 1376264 | tf_op jit(solution)/shard_map/ppermute | solution.py:115
  42.2 17.8 %collective-permute-start.8 = (bf16[256,896]{1,0:T(8,128)(2,1)S(1)}, bf16[256,896]{1,0:T(8,128)(2,1)}, u32[]{:S(2)}, u32[]{:S(2)}) collective-permute-start(bf16[256,896]{1,0:T(8,128)(2,1)S(1)} %pad_maximum_fusion.1), channel_id=1, source_target_pairs={{16,0},{32,16},{48,32},{0,48},{17,1},{33,17},{49,33},{1,49},{18,2}... | collective-permute-start | bytes 1376264 | tf_op jit(solution)/shard_map/ppermute | solution.py:115
  49.3 16.9 %all-to-all-start.1 = ((bf16[32,32,128]{2,1,0:T(8,128)(2,1)}), bf16[32,32,128]{2,1,0:T(8,128)(2,1)S(1)}, u32[]{:S(2)}, u32[]{:S(2)}) async-start(bf16[32,32,128]{2,1,0:T(8,128)(2,1)} %bitcast.10), calls=%async_computation.1 | async-start | bytes 524288 | tf_op jit(solution)/shard_map/all_to_all | solution.py:40
  56.8 5.6 %collective-permute-start.7 = (bf16[32,640]{1,0:T(8,128)(2,1)S(1)}, bf16[32,640]{1,0:T(8,128)(2,1)S(1)}, u32[]{:S(2)}, u32[]{:S(2)}) collective-permute-start(bf16[32,640]{1,0:T(8,128)(2,1)S(1)} %concatenate.35), channel_id=1, source_target_pairs={{0,1},{1,0},{2,3},{3,2},{4,5},{5,4},{6,7},{7,6},{8,9},{9,8},{10,11... | collective-permute-start | bytes 122888 | tf_op jit(solution)/shard_map/ppermute | solution.py:149
  66.3 0.9 copy-start.6
  66.9 26.6 %copy-start.2 = (bf16[512,896]{1,0:T(8,128)(2,1)S(1)}, bf16[512,896]{1,0:T(8,128)(2,1)}, u32[]{:S(2)}) copy-start(bf16[512,896]{1,0:T(8,128)(2,1)} %copy-done.1) | copy-start | bytes 2752516
  68.0 20.8 %all-to-all-start.2 = ((bf16[8,24,896]{2,1,0:T(8,128)(2,1)}), bf16[8,24,896]{2,1,0:T(8,128)(2,1)S(1)}, u32[]{:S(2)}, u32[]{:S(2)}) async-start(bf16[8,24,896]{2,1,0:T(8,128)(2,1)} %pad_maximum_fusion.3), calls=%async_computation.2 | async-start | bytes 688128 | tf_op jit(solution)/shard_map/all_to_all | solution.py:40
  74.8 7.7 %collective-permute-start.10 = (bf16[64,640]{1,0:T(8,128)(2,1)S(1)}, bf16[64,640]{1,0:T(8,128)(2,1)S(1)}, u32[]{:S(2)}, u32[]{:S(2)}) collective-permute-start(bf16[64,640]{1,0:T(8,128)(2,1)S(1)} %pad_maximum_fusion.5), channel_id=1, source_target_pairs={{0,2},{1,3},{2,0},{3,1},{4,6},{5,7},{6,4},{7,5},{8,10},{9,11},{10,... | collective-permute-start | bytes 245768 | tf_op jit(solution)/shard_map/ppermute | solution.py:149
  88.9 8.7 %collective-permute-start.11 = (bf16[24,896]{1,0:T(8,128)(2,1)S(1)}, bf16[24,896]{1,0:T(8,128)(2,1)S(1)}, u32[]{:S(2)}, u32[]{:S(2)}) collective-permute-start(bf16[24,896]{1,0:T(8,128)(2,1)S(1)} %convert_element_type.54), channel_id=1, source_target_pairs={{0,8},{8,0},{1,9},{9,1},{2,10},{10,2},{3,11},{11,3},{4,12},{12,4},... | collective-permute-start | bytes 129032 | tf_op jit(solution)/shard_map/ppermute | solution.py:36
  97.6 9.1 %collective-permute-start.12 = (bf16[16,896]{1,0:T(8,128)(2,1)S(1)}, bf16[16,896]{1,0:T(8,128)(2,1)S(1)}, u32[]{:S(2)}, u32[]{:S(2)}) collective-permute-start(bf16[16,896]{1,0:T(8,128)(2,1)S(1)} %slice.118), channel_id=1, source_target_pairs={{0,0},{1,128},{2,256},{3,384},{4,64},{5,192},{6,320},{7,448},{8,8}... | collective-permute-start | bytes 86024 | tf_op jit(solution)/shard_map/ppermute | solution.py:174
  107.4 10.2 %all-to-all-start.3 = ((bf16[8,24,896]{2,1,0:T(8,128)(2,1)}), bf16[8,24,896]{2,1,0:T(8,128)(2,1)S(1)}, u32[]{:S(2)}, u32[]{:S(2)}) async-start(bf16[8,24,896]{2,1,0:T(8,128)(2,1)} %broadcast_in_dim.16), calls=%async_computation.3 | async-start | bytes 688128 | tf_op jit(solution)/shard_map/all_to_all | solution.py:40

commit v9 on v8

--- a/solution.py
+++ b/solution.py
@@ -152,14 +152,14 @@
     quarter = exchange(quarters, GROUP + ("tensor",)).reshape(4, 2 * tokens, LANES)
     pair = partner(sent, 1)
     normed = jnp.concatenate((own, after, far, before), 0)
-    pair, normed = lax.optimization_barrier((pair, normed))
+    embed = (half_of(embed, core).astype(F32) + taken.astype(F32)).astype(BF16)
+    pair, normed, embed = lax.optimization_barrier((pair, normed, embed))
     sent = joined(sent, pair, 1)
     quarter, normed, sent = lax.optimization_barrier((quarter, normed, sent))
     quarter = lax.dynamic_slice_in_dim(jnp.concatenate((quarter, quarter[:3]), 0), lax.axis_index("x"), 4, 0)
     turned = jnp.concatenate((quarter[:, tokens:], quarter[:, :tokens]), 1)
     quarter = jnp.where(core == 0, quarter, turned)
     term = dot(quarter.reshape(8 * tokens, LANES), normed, ((0,), (0,))).astype(BF16)
-    embed = (half_of(embed, core).astype(F32) + taken.astype(F32)).astype(BF16)
     term = jnp.concatenate((term.reshape(replicas, 16, half), embed.reshape(replicas, 8, half)), 1)
     term, sent = lax.optimization_barrier((term, sent))
     term = exchange(term, "dp")

time: 120 us -> 126 us (1.050)
  waiting for transfers between devices: 33.2 us -> 40.1 us
    ppermute x3, waiting for transfers between devices: 2.06 us -> 8.89 us  [shift(): lax.ppermute(value, RING, [(i, step(i) % count) for i in range(count)])]
    ppermute x3, starting transfers between devices: 15.3 us -> 12 us  [shift(): lax.ppermute(value, RING, [(i, step(i) % count) for i in range(count)])]
    ppermute x4, starting transfers between devices: 13.4 us -> 16 us  [swap(): return lax.ppermute(value, axis, [(0, 1), (1, 0)])]
    convert_element_type x0 -> x1, other arithmetic: none -> 1.64 us  [shards(): embed = (half_of(embed, core).astype(F32) + taken.astype(F32)).astype(BF16)]
    reshape x1 -> x0, other arithmetic: 1.64 us -> none  [shards(): embed.reshape(replicas, 8, half)]
  transfers between devices with their start and end apart: 17 -> 17, of which waited for: 9 -> 10; matrix products, arithmetic and copies ran while one was open for 8% -> 8% of each run, Pallas kernels for 0% -> 0%
where the time goes in v9:
time: 126 us; the launch traced here: 125 us
  starting transfers between devices  67.8 us (54%)
  waiting for transfers between devices  40.1 us (32%)
  other arithmetic  6.99 us (6%)
  local copies, waits for them, and re-layouts  5.56 us (4%)
  matrix products  3 us (2%)
  between operations  1.34 us (1%)
    all_to_all x4, starting transfers between devices, exchange(): return lax.all_to_all(value, axes, 0, 0)  19.1 us
    all_to_all x4, waiting for transfers between devices, exchange(): return lax.all_to_all(value, axes, 0, 0)  17.2 us
    ppermute x4, starting transfers between devices, swap(): return lax.ppermute(value, axis, [(0, 1), (1, 0)])  16 us
    ppermute x3, starting transfers between devices, shift(): lax.ppermute(value, RING, [(i, step(i) % count) for i in range(count)])  12 us
    ppermute x3, starting transfers between devices, from_x(): return lax.ppermute(value, 'x', [((i + ahead) % 4, i) for i in range(4)])  11.1 us
    ppermute x3, waiting for transfers between devices, shift(): lax.ppermute(value, RING, [(i, step(i) % count) for i in range(count)])  8.89 us
    ppermute x2, starting transfers between devices, partner(): return lax.ppermute(value, 'tensor', [(i, i ^ step) for i in range(4)])  5.71 us
    ppermute x2, waiting for transfers between devices, partner(): return lax.ppermute(value, 'tensor', [(i, i ^ step) for i in range(4)])  5.66 us
  transfers between devices with their start and end apart: 17, of which 10 were waited for; matrix products, arithmetic and copies ran while one was open for 8% of the time, Pallas kernels for 0%

profile of v9, /device:TPU:1, one launch (start us, length us, event | category | flops | bytes accessed | tf_op | source)
XLA Modules:
  0.0 124.7 jit_solution(5775643056394988905)
XLA Ops:
  0.7 1.4 %constant_dynamic-slice_fusion.2 = (bf16[128,896]{1,0:T(8,128)(2,1)S(1)}, bf16[128,896]{1,0:T(8,128)(2,1)S(1)}, bf16[128,896]{1,0:T(8,128)(2,1)S(1)}, bf16[128,896]{1,0:T(8,128)(2,1)S(1)}) fusion(bf16[128,7168]{1,0:T(8,128)(2,1)} %param.9, s32[]{:T(128)S(6)} %select_n.227, s32[]{:T(128)S(6)} %select_n.221, s32[]{:T(128)S(6)} %select_n.218, s32[]{:T(128)S(6)} %select_n.224), kind=kLoop, calls=%fused_computation.55 | loop fusion | bytes 1835024 | tf_op jit(solution)/shard_map/dynamic_slice | solution.py:60
  2.2 4.8 %collective-permute-start = (bf16[128,896]{1,0:T(8,128)(2,1)S(1)}, bf16[128,896]{1,0:T(8,128)(2,1)S(1)}, u32[]{:S(2)}, u32[]{:S(2)}) collective-permute-start(bf16[128,896]{1,0:T(8,128)(2,1)S(1)} %get-tuple-element.52), channel_id=1, source_target_pairs={{0,1},{1,2},{2,3},{3,8},{8,9},{9,10},{10,11},{11,0},{4,5},{5,6},{6... | collective-permute-start | bytes 688136 | tf_op jit(solution)/shard_map/ppermute | solution.py:32
  8.1 5.9 %collective-permute-start.4 = (bf16[64,896]{1,0:T(8,128)(2,1)S(1)}, bf16[64,896]{1,0:T(8,128)(2,1)}, u32[]{:S(2)}, u32[]{:S(2)}) collective-permute-start(bf16[64,896]{1,0:T(8,128)(2,1)S(1)} %constant_dynamic-slice_fusion), channel_id=1, source_target_pairs={{0,4},{4,0},{1,5},{5,1},{2,6},{6,2},{3,7},{7,3},{8,12},{12,8},{9,1... | collective-permute-start | bytes 344072 | tf_op jit(solution)/shard_map/ppermute | solution.py:36
  14.0 5.3 %collective-permute-start.1 = (bf16[128,896]{1,0:T(8,128)(2,1)S(1)}, bf16[128,896]{1,0:T(8,128)(2,1)S(1)}, u32[]{:S(2)}, u32[]{:S(2)}) collective-permute-start(bf16[128,896]{1,0:T(8,128)(2,1)S(1)} %get-tuple-element.51), channel_id=1, source_target_pairs={{0,11},{1,0},{2,1},{3,2},{8,3},{9,8},{10,9},{11,10},{4,15},{5,4},{... | collective-permute-start | bytes 688136 | tf_op jit(solution)/shard_map/ppermute | solution.py:32
  19.3 2.2 %collective-permute-start.3 = (bf16[128,896]{1,0:T(8,128)(2,1)S(1)}, bf16[128,896]{1,0:T(8,128)(2,1)S(1)}, u32[]{:S(2)}, u32[]{:S(2)}) collective-permute-start(bf16[128,896]{1,0:T(8,128)(2,1)S(1)} %get-tuple-element.57), channel_id=1, source_target_pairs={{0,4},{4,0},{1,5},{5,1},{2,6},{6,2},{3,7},{7,3},{8,12},{12,8},{9,1... | collective-permute-start | bytes 688136 | tf_op jit(solution)/shard_map/ppermute | solution.py:36
  21.6 1.9 %collective-permute-start.2 = (bf16[128,896]{1,0:T(8,128)(2,1)S(1)}, bf16[128,896]{1,0:T(8,128)(2,1)S(1)}, u32[]{:S(2)}, u32[]{:S(2)}) collective-permute-start(bf16[128,896]{1,0:T(8,128)(2,1)S(1)} %get-tuple-element.53), channel_id=1, source_target_pairs={{0,2},{1,11},{2,8},{3,1},{8,10},{9,3},{10,0},{11,9},{4,6},{5,15},{... | collective-permute-start | bytes 688136 | tf_op jit(solution)/shard_map/ppermute | solution.py:32
  24.3 8.3 %collective-permute-done.2 = bf16[128,896]{1,0:T(8,128)(2,1)S(1)} collective-permute-done((bf16[128,896]{1,0:T(8,128)(2,1)S(1)}, bf16[128,896]{1,0:T(8,128)(2,1)S(1)}, u32[]{:S(2)}, u32[]{:S(2)}) %collective-permute-start.2) | collective-permute-done | bytes 229408 | tf_op jit(solution)/shard_map/ppermute | solution.py:32
  32.7 3.0 %collective-permute-start.5 = (bf16[512,896]{1,0:T(8,128)(2,1)S(1)}, bf16[512,896]{1,0:T(8,128)(2,1)S(1)}, u32[]{:S(2)}, u32[]{:S(2)}) collective-permute-start(bf16[512,896]{1,0:T(8,128)(2,1)S(1)} %bitcast.40), channel_id=1, source_target_pairs={{0,4},{4,0},{1,5},{5,1},{2,6},{6,2},{3,7},{7,3},{8,12},{12,8},{9,1... | collective-permute-start | bytes 2752520 | tf_op jit(solution)/shard_map/ppermute | solution.py:36
  35.9 4.7 %collective-permute-start.6 = (bf16[256,896]{1,0:T(8,128)(2,1)S(1)}, bf16[256,896]{1,0:T(8,128)(2,1)}, u32[]{:S(2)}, u32[]{:S(2)}) collective-permute-start(bf16[256,896]{1,0:T(8,128)(2,1)S(1)} %pad_maximum_fusion.1), channel_id=1, source_target_pairs={{32,0},{48,16},{0,32},{16,48},{33,1},{49,17},{1,33},{17,49},{34,2}... | collective-permute-start | bytes 1376264 | tf_op jit(solution)/shard_map/ppermute | solution.py:115
  41.0 1.1 convolution_add_fusion
  42.1 3.4 %all-to-all-start = ((f32[4,32,512]{2,1,0:T(8,128)}), f32[4,32,512]{2,1,0:T(8,128)S(1)}, u32[]{:S(2)}, u32[]{:S(2)}) async-start(f32[4,32,512]{2,1,0:T(8,128)} %bitcast.5), calls=%async_computation | async-start | bytes 524288 | tf_op jit(solution)/shard_map/all_to_all | solution.py:40
  45.7 2.2 %collective-permute-start.9 = (bf16[256,896]{1,0:T(8,128)(2,1)S(1)}, bf16[256,896]{1,0:T(8,128)(2,1)}, u32[]{:S(2)}, u32[]{:S(2)}) collective-permute-start(bf16[256,896]{1,0:T(8,128)(2,1)S(1)} %pad_maximum_fusion.1), channel_id=1, source_target_pairs={{48,0},{0,16},{16,32},{32,48},{49,1},{1,17},{17,33},{33,49},{50,2}... | collective-permute-start | bytes 1376264 | tf_op jit(solution)/shard_map/ppermute | solution.py:115
  47.9 4.3 %collective-permute-start.8 = (bf16[256,896]{1,0:T(8,128)(2,1)S(1)}, bf16[256,896]{1,0:T(8,128)(2,1)}, u32[]{:S(2)}, u32[]{:S(2)}) collective-permute-start(bf16[256,896]{1,0:T(8,128)(2,1)S(1)} %pad_maximum_fusion.1), channel_id=1, source_target_pairs={{16,0},{32,16},{48,32},{0,48},{17,1},{33,17},{49,33},{1,49},{18,2}... | collective-permute-start | bytes 1376264 | tf_op jit(solution)/shard_map/ppermute | solution.py:115
  52.2 1.2 all-to-all-done
  55.2 5.5 %all-to-all-start.1 = ((bf16[32,32,128]{2,1,0:T(8,128)(2,1)}), bf16[32,32,128]{2,1,0:T(8,128)(2,1)S(1)}, u32[]{:S(2)}, u32[]{:S(2)}) async-start(bf16[32,32,128]{2,1,0:T(8,128)(2,1)} %bitcast.10), calls=%async_computation.1 | async-start | bytes 524288 | tf_op jit(solution)/shard_map/all_to_all | solution.py:40
  60.6 1.6 %add_convert_fusion = bf16[64,896]{1,0:T(8,128)(2,1)} fusion(bf16[64,896]{1,0:T(8,128)(2,1)} %collective-permute-done.4, bf16[64,1792]{1,0:T(8,128)(2,1)} %copy-done.4, s32[]{:T(128)S(6)} %select_n.216), kind=kLoop, calls=%fused_computation.14 | loop fusion | flops 229376 | bytes 344068 | tf_op jit(solution)/shard_map/convert_element_type | solution.py:155
  62.3 3.3 %collective-permute-start.7 = (bf16[32,640]{1,0:T(8,128)(2,1)S(1)}, bf16[32,640]{1,0:T(8,128)(2,1)S(1)}, u32[]{:S(2)}, u32[]{:S(2)}) collective-permute-start(bf16[32,640]{1,0:T(8,128)(2,1)S(1)} %concatenate.35), channel_id=1, source_target_pairs={{0,1},{1,0},{2,3},{3,2},{4,5},{5,4},{6,7},{7,6},{8,9},{9,8},{10,11... | collective-permute-start | bytes 122888 | tf_op jit(solution)/shard_map/ppermute | solution.py:149
  65.6 1.6 %pad_maximum_fusion = bf16[1024,896]{1,0:T(8,128)(2,1)S(1)} fusion(bf16[256,896]{1,0:T(8,128)(2,1)} %collective-permute-done.9, bf16[256,896]{1,0:T(8,128)(2,1)} %collective-permute-done.6, bf16[256,896]{1,0:T(8,128)(2,1)} %collective-permute-done.8, bf16[256,896]{1,0:T(8,128)(2,1)} %copy-done.3), kind=kLoop, calls=%fused_computation.1 | loop fusion | flops 7340032 | bytes 3670016 | tf_op jit(solution)/shard_map/concatenate | solution.py:154
  67.6 4.2 %all-to-all-done.1 = bf16[32,32,128]{2,1,0:T(8,128)(2,1)S(1)} async-done(((bf16[32,32,128]{2,1,0:T(8,128)(2,1)}), bf16[32,32,128]{2,1,0:T(8,128)(2,1)S(1)}, u32[]{:S(2)}, u32[]{:S(2)}) %all-to-all-start.1) | async-done | bytes 262176 | tf_op jit(solution)/shard_map/all_to_all | solution.py:40
  72.8 0.8 pad_maximum_fusion.3
  73.6 6.8 %all-to-all-start.2 = ((bf16[8,24,896]{2,1,0:T(8,128)(2,1)}), bf16[8,24,896]{2,1,0:T(8,128)(2,1)S(1)}, u32[]{:S(2)}, u32[]{:S(2)}) async-start(bf16[8,24,896]{2,1,0:T(8,128)(2,1)} %pad_maximum_fusion.3), calls=%async_computation.2 | async-start | bytes 688128 | tf_op jit(solution)/shard_map/all_to_all | solution.py:40
  80.4 2.4 %collective-permute-start.10 = (bf16[64,640]{1,0:T(8,128)(2,1)S(1)}, bf16[64,640]{1,0:T(8,128)(2,1)S(1)}, u32[]{:S(2)}, u32[]{:S(2)}) collective-permute-start(bf16[64,640]{1,0:T(8,128)(2,1)S(1)} %pad_maximum_fusion.5), channel_id=1, source_target_pairs={{0,2},{1,3},{2,0},{3,1},{4,6},{5,7},{6,4},{7,5},{8,10},{9,11},{10,... | collective-permute-start | bytes 245768 | tf_op jit(solution)/shard_map/ppermute | solution.py:149
  82.9 5.2 %collective-permute-done.10 = bf16[64,640]{1,0:T(8,128)(2,1)S(1)} collective-permute-done((bf16[64,640]{1,0:T(8,128)(2,1)S(1)}, bf16[64,640]{1,0:T(8,128)(2,1)S(1)}, u32[]{:S(2)}, u32[]{:S(2)}) %collective-permute-start.10) | collective-permute-done | bytes 81952 | tf_op jit(solution)/shard_map/ppermute | solution.py:149
  88.1 6.3 %all-to-all-done.2 = bf16[8,24,896]{2,1,0:T(8,128)(2,1)S(1)} async-done(((bf16[8,24,896]{2,1,0:T(8,128)(2,1)}), bf16[8,24,896]{2,1,0:T(8,128)(2,1)S(1)}, u32[]{:S(2)}, u32[]{:S(2)}) %all-to-all-start.2) | async-done | bytes 344096 | tf_op jit(solution)/shard_map/all_to_all | solution.py:40
  94.5 4.8 %collective-permute-start.11 = (bf16[24,896]{1,0:T(8,128)(2,1)S(1)}, bf16[24,896]{1,0:T(8,128)(2,1)S(1)}, u32[]{:S(2)}, u32[]{:S(2)}) collective-permute-start(bf16[24,896]{1,0:T(8,128)(2,1)S(1)} %convert_element_type.54), channel_id=1, source_target_pairs={{0,8},{8,0},{1,9},{9,1},{2,10},{10,2},{3,11},{11,3},{4,12},{12,4},... | collective-permute-start | bytes 129032 | tf_op jit(solution)/shard_map/ppermute | solution.py:36
  100.0 3.1 %collective-permute-done.11 = bf16[24,896]{1,0:T(8,128)(2,1)S(1)} collective-permute-done((bf16[24,896]{1,0:T(8,128)(2,1)S(1)}, bf16[24,896]{1,0:T(8,128)(2,1)S(1)}, u32[]{:S(2)}, u32[]{:S(2)}) %collective-permute-start.11) | collective-permute-done | bytes 43040 | tf_op jit(solution)/shard_map/ppermute | solution.py:36
  103.2 3.8 %collective-permute-start.12 = (bf16[16,896]{1,0:T(8,128)(2,1)S(1)}, bf16[16,896]{1,0:T(8,128)(2,1)S(1)}, u32[]{:S(2)}, u32[]{:S(2)}) collective-permute-start(bf16[16,896]{1,0:T(8,128)(2,1)S(1)} %slice.118), channel_id=1, source_target_pairs={{0,0},{1,128},{2,256},{3,384},{4,64},{5,192},{6,320},{7,448},{8,8}... | collective-permute-start | bytes 86024 | tf_op jit(solution)/shard_map/ppermute | solution.py:174
  107.1 5.2 %collective-permute-done.12 = bf16[16,896]{1,0:T(8,128)(2,1)S(1)} collective-permute-done((bf16[16,896]{1,0:T(8,128)(2,1)S(1)}, bf16[16,896]{1,0:T(8,128)(2,1)S(1)}, u32[]{:S(2)}, u32[]{:S(2)}) %collective-permute-start.12) | collective-permute-done | bytes 28704 | tf_op jit(solution)/shard_map/ppermute | solution.py:174
  113.0 3.4 %all-to-all-start.3 = ((bf16[8,24,896]{2,1,0:T(8,128)(2,1)}), bf16[8,24,896]{2,1,0:T(8,128)(2,1)S(1)}, u32[]{:S(2)}, u32[]{:S(2)}) async-start(bf16[8,24,896]{2,1,0:T(8,128)(2,1)} %broadcast_in_dim.16), calls=%async_computation.3 | async-start | bytes 688128 | tf_op jit(solution)/shard_map/all_to_all | solution.py:40
  117.0 0.8 pad_maximum_fusion.2
  117.8 5.5 %all-to-all-done.3 = bf16[8,24,896]{2,1,0:T(8,128)(2,1)S(1)} async-done(((bf16[8,24,896]{2,1,0:T(8,128)(2,1)}), bf16[8,24,896]{2,1,0:T(8,128)(2,1)S(1)}, u32[]{:S(2)}, u32[]{:S(2)}) %all-to-all-start.3) | async-done | bytes 344096 | tf_op jit(solution)/shard_map/all_to_all | solution.py:40
  123.9 0.8 slice.120
  (83 shorter events, 8.5 us)
Async XLA Ops:
  0.6 6.4 %copy-start = (bf16[128,1792]{1,0:T(8,128)(2,1)S(1)}, bf16[128,1792]{1,0:T(8,128)(2,1)}, u32[]{:S(2)}) copy-start(bf16[128,1792]{1,0:T(8,128)(2,1)} %param.8) | copy-start | bytes 1376260
  0.6 6.4 %copy-start.10 = (s32[128]{0:T(128)S(1)}, s32[128]{0:T(128)}, u32[]{:S(2)}) copy-start(s32[128]{0:T(128)} %param.13) | copy-start | bytes 1540
  0.7 18.6 %copy-start.5 = (bf16[128,1792]{1,0:T(8,128)(2,1)S(1)}, bf16[128,1792]{1,0:T(8,128)(2,1)}, u32[]{:S(2)}) copy-start(bf16[128,1792]{1,0:T(8,128)(2,1)} %param.7) | copy-start | bytes 1376260
  2.2 21.3 %collective-permute-start = (bf16[128,896]{1,0:T(8,128)(2,1)S(1)}, bf16[128,896]{1,0:T(8,128)(2,1)S(1)}, u32[]{:S(2)}, u32[]{:S(2)}) collective-permute-start(bf16[128,896]{1,0:T(8,128)(2,1)S(1)} %get-tuple-element.52), channel_id=1, source_target_pairs={{0,1},{1,2},{2,3},{3,8},{8,9},{9,10},{10,11},{11,0},{4,5},{5,6},{6... | collective-permute-start | bytes 688136 | tf_op jit(solution)/shard_map/ppermute | solution.py:32
  7.4 0.7 copy-start.4
  8.1 24.7 %collective-permute-start.4 = (bf16[64,896]{1,0:T(8,128)(2,1)S(1)}, bf16[64,896]{1,0:T(8,128)(2,1)}, u32[]{:S(2)}, u32[]{:S(2)}) collective-permute-start(bf16[64,896]{1,0:T(8,128)(2,1)S(1)} %constant_dynamic-slice_fusion), channel_id=1, source_target_pairs={{0,4},{4,0},{1,5},{5,1},{2,6},{6,2},{3,7},{7,3},{8,12},{12,8},{9,1... | collective-permute-start | bytes 344072 | tf_op jit(solution)/shard_map/ppermute | solution.py:36
  14.0 10.3 %collective-permute-start.1 = (bf16[128,896]{1,0:T(8,128)(2,1)S(1)}, bf16[128,896]{1,0:T(8,128)(2,1)S(1)}, u32[]{:S(2)}, u32[]{:S(2)}) collective-permute-start(bf16[128,896]{1,0:T(8,128)(2,1)S(1)} %get-tuple-element.51), channel_id=1, source_target_pairs={{0,11},{1,0},{2,1},{3,2},{8,3},{9,8},{10,9},{11,10},{4,15},{5,4},{... | collective-permute-start | bytes 688136 | tf_op jit(solution)/shard_map/ppermute | solution.py:32
  19.3 13.3 %collective-permute-start.3 = (bf16[128,896]{1,0:T(8,128)(2,1)S(1)}, bf16[128,896]{1,0:T(8,128)(2,1)S(1)}, u32[]{:S(2)}, u32[]{:S(2)}) collective-permute-start(bf16[128,896]{1,0:T(8,128)(2,1)S(1)} %get-tuple-element.57), channel_id=1, source_target_pairs={{0,4},{4,0},{1,5},{5,1},{2,6},{6,2},{3,7},{7,3},{8,12},{12,8},{9,1... | collective-permute-start | bytes 688136 | tf_op jit(solution)/shard_map/ppermute | solution.py:36
  21.6 11.0 %collective-permute-start.2 = (bf16[128,896]{1,0:T(8,128)(2,1)S(1)}, bf16[128,896]{1,0:T(8,128)(2,1)S(1)}, u32[]{:S(2)}, u32[]{:S(2)}) collective-permute-start(bf16[128,896]{1,0:T(8,128)(2,1)S(1)} %get-tuple-element.53), channel_id=1, source_target_pairs={{0,2},{1,11},{2,8},{3,1},{8,10},{9,3},{10,0},{11,9},{4,6},{5,15},{... | collective-permute-start | bytes 688136 | tf_op jit(solution)/shard_map/ppermute | solution.py:32
  32.7 15.3 %copy-start.3 = (bf16[256,896]{1,0:T(8,128)(2,1)}, bf16[256,896]{1,0:T(8,128)(2,1)S(1)}, u32[]{:S(2)}) copy-start(bf16[256,896]{1,0:T(8,128)(2,1)S(1)} %pad_maximum_fusion.1) | copy-start | bytes 1376260
  32.7 12.8 %copy-start.7 = (s32[128]{0:T(128)S(1)}, s32[128]{0:T(128)}, u32[]{:S(2)}) copy-start(s32[128]{0:T(128)} %param.12) | copy-start | bytes 1540
  32.7 12.9 %copy-start.8 = (f32[128]{0:T(128)S(1)}, f32[128]{0:T(128)}, u32[]{:S(2)}) copy-start(f32[128]{0:T(128)} %param.11) | copy-start | bytes 1540
  32.7 7.8 %collective-permute-start.5 = (bf16[512,896]{1,0:T(8,128)(2,1)S(1)}, bf16[512,896]{1,0:T(8,128)(2,1)S(1)}, u32[]{:S(2)}, u32[]{:S(2)}) collective-permute-start(bf16[512,896]{1,0:T(8,128)(2,1)S(1)} %bitcast.40), channel_id=1, source_target_pairs={{0,4},{4,0},{1,5},{5,1},{2,6},{6,2},{3,7},{7,3},{8,12},{12,8},{9,1... | collective-permute-start | bytes 2752520 | tf_op jit(solution)/shard_map/ppermute | solution.py:36
  35.8 17.7 %copy-start.9 = (f32[128]{0:T(128)S(1)}, f32[128]{0:T(128)}, u32[]{:S(2)}) copy-start(f32[128]{0:T(128)} %param.10) | copy-start | bytes 1540
  35.9 16.4 %collective-permute-start.6 = (bf16[256,896]{1,0:T(8,128)(2,1)S(1)}, bf16[256,896]{1,0:T(8,128)(2,1)}, u32[]{:S(2)}, u32[]{:S(2)}) collective-permute-start(bf16[256,896]{1,0:T(8,128)(2,1)S(1)} %pad_maximum_fusion.1), channel_id=1, source_target_pairs={{32,0},{48,16},{0,32},{16,48},{33,1},{49,17},{1,33},{17,49},{34,2}... | collective-permute-start | bytes 1376264 | tf_op jit(solution)/shard_map/ppermute | solution.py:115
  40.5 12.9 %copy-start.1 = (bf16[512,896]{1,0:T(8,128)(2,1)}, bf16[512,896]{1,0:T(8,128)(2,1)S(1)}, u32[]{:S(2)}) copy-start(bf16[512,896]{1,0:T(8,128)(2,1)S(1)} %collective-permute-done.5) | copy-start | bytes 2752516
  42.1 11.3 %all-to-all-start = ((f32[4,32,512]{2,1,0:T(8,128)}), f32[4,32,512]{2,1,0:T(8,128)S(1)}, u32[]{:S(2)}, u32[]{:S(2)}) async-start(f32[4,32,512]{2,1,0:T(8,128)} %bitcast.5), calls=%async_computation | async-start | bytes 524288 | tf_op jit(solution)/shard_map/all_to_all | solution.py:40
  45.7 19.8 %collective-permute-start.9 = (bf16[256,896]{1,0:T(8,128)(2,1)S(1)}, bf16[256,896]{1,0:T(8,128)(2,1)}, u32[]{:S(2)}, u32[]{:S(2)}) collective-permute-start(bf16[256,896]{1,0:T(8,128)(2,1)S(1)} %pad_maximum_fusion.1), channel_id=1, source_target_pairs={{48,0},{0,16},{16,32},{32,48},{49,1},{1,17},{17,33},{33,49},{50,2}... | collective-permute-start | bytes 1376264 | tf_op jit(solution)/shard_map/ppermute | solution.py:115
  47.9 17.6 %collective-permute-start.8 = (bf16[256,896]{1,0:T(8,128)(2,1)S(1)}, bf16[256,896]{1,0:T(8,128)(2,1)}, u32[]{:S(2)}, u32[]{:S(2)}) collective-permute-start(bf16[256,896]{1,0:T(8,128)(2,1)S(1)} %pad_maximum_fusion.1), channel_id=1, source_target_pairs={{16,0},{32,16},{48,32},{0,48},{17,1},{33,17},{49,33},{1,49},{18,2}... | collective-permute-start | bytes 1376264 | tf_op jit(solution)/shard_map/ppermute | solution.py:115
  55.2 16.7 %all-to-all-start.1 = ((bf16[32,32,128]{2,1,0:T(8,128)(2,1)}), bf16[32,32,128]{2,1,0:T(8,128)(2,1)S(1)}, u32[]{:S(2)}, u32[]{:S(2)}) async-start(bf16[32,32,128]{2,1,0:T(8,128)(2,1)} %bitcast.10), calls=%async_computation.1 | async-start | bytes 524288 | tf_op jit(solution)/shard_map/all_to_all | solution.py:40
  62.3 5.3 %collective-permute-start.7 = (bf16[32,640]{1,0:T(8,128)(2,1)S(1)}, bf16[32,640]{1,0:T(8,128)(2,1)S(1)}, u32[]{:S(2)}, u32[]{:S(2)}) collective-permute-start(bf16[32,640]{1,0:T(8,128)(2,1)S(1)} %concatenate.35), channel_id=1, source_target_pairs={{0,1},{1,0},{2,3},{3,2},{4,5},{5,4},{6,7},{7,6},{8,9},{9,8},{10,11... | collective-permute-start | bytes 122888 | tf_op jit(solution)/shard_map/ppermute | solution.py:149
  71.9 0.9 copy-start.6
  72.5 26.8 %copy-start.2 = (bf16[512,896]{1,0:T(8,128)(2,1)S(1)}, bf16[512,896]{1,0:T(8,128)(2,1)}, u32[]{:S(2)}) copy-start(bf16[512,896]{1,0:T(8,128)(2,1)} %copy-done.1) | copy-start | bytes 2752516
  73.6 20.8 %all-to-all-start.2 = ((bf16[8,24,896]{2,1,0:T(8,128)(2,1)}), bf16[8,24,896]{2,1,0:T(8,128)(2,1)S(1)}, u32[]{:S(2)}, u32[]{:S(2)}) async-start(bf16[8,24,896]{2,1,0:T(8,128)(2,1)} %pad_maximum_fusion.3), calls=%async_computation.2 | async-start | bytes 688128 | tf_op jit(solution)/shard_map/all_to_all | solution.py:40
  80.4 7.7 %collective-permute-start.10 = (bf16[64,640]{1,0:T(8,128)(2,1)S(1)}, bf16[64,640]{1,0:T(8,128)(2,1)S(1)}, u32[]{:S(2)}, u32[]{:S(2)}) collective-permute-start(bf16[64,640]{1,0:T(8,128)(2,1)S(1)} %pad_maximum_fusion.5), channel_id=1, source_target_pairs={{0,2},{1,3},{2,0},{3,1},{4,6},{5,7},{6,4},{7,5},{8,10},{9,11},{10,... | collective-permute-start | bytes 245768 | tf_op jit(solution)/shard_map/ppermute | solution.py:149
  94.5 8.7 %collective-permute-start.11 = (bf16[24,896]{1,0:T(8,128)(2,1)S(1)}, bf16[24,896]{1,0:T(8,128)(2,1)S(1)}, u32[]{:S(2)}, u32[]{:S(2)}) collective-permute-start(bf16[24,896]{1,0:T(8,128)(2,1)S(1)} %convert_element_type.54), channel_id=1, source_target_pairs={{0,8},{8,0},{1,9},{9,1},{2,10},{10,2},{3,11},{11,3},{4,12},{12,4},... | collective-permute-start | bytes 129032 | tf_op jit(solution)/shard_map/ppermute | solution.py:36
  103.2 9.1 %collective-permute-start.12 = (bf16[16,896]{1,0:T(8,128)(2,1)S(1)}, bf16[16,896]{1,0:T(8,128)(2,1)S(1)}, u32[]{:S(2)}, u32[]{:S(2)}) collective-permute-start(bf16[16,896]{1,0:T(8,128)(2,1)S(1)} %slice.118), channel_id=1, source_target_pairs={{0,0},{1,128},{2,256},{3,384},{4,64},{5,192},{6,320},{7,448},{8,8}... | collective-permute-start | bytes 86024 | tf_op jit(solution)/shard_map/ppermute | solution.py:174
  113.0 10.2 %all-to-all-start.3 = ((bf16[8,24,896]{2,1,0:T(8,128)(2,1)}), bf16[8,24,896]{2,1,0:T(8,128)(2,1)S(1)}, u32[]{:S(2)}, u32[]{:S(2)}) async-start(bf16[8,24,896]{2,1,0:T(8,128)(2,1)} %broadcast_in_dim.16), calls=%async_computation.3 | async-start | bytes 688128 | tf_op jit(solution)/shard_map/all_to_all | solution.py:40
